TPU v7x, 128 devices: a whole 4x4x4 slice. The times are simulated.
128 devices in a mesh: seq: 32 (over z_hi, y, x), fsdp: 4 (over z_lo, core).
Axes of the slice: x: 4, y: 4, z: 4 (z_hi: 2, z_lo: 2; z = z_hi * 2 + z_lo), core: 2. Of those that a mesh axis runs over, the one named last changes fastest.
Arguments:
- tokens: float32 [4, 8192, 1024], P('fsdp', 'seq'), may hold values from -6 to 6
- token_pos: int32 [4, 8192], P('fsdp', 'seq'), may hold values from 0 to 8183, as said below
- w_in: bfloat16 [1024, 3072], P('seq', 'fsdp'), may hold values from -0.1875 to 0.1875
- w_mix: bfloat16 [1024, 1024], P('seq', 'fsdp'), may hold values from -0.1875 to 0.1875
- w_gate: bfloat16 [1024, 4608], P('seq', 'fsdp'), may hold values from -0.1875 to 0.1875
- w_up: bfloat16 [1024, 4608], P('seq', 'fsdp'), may hold values from -0.1875 to 0.1875
- w_down: bfloat16 [4608, 1024], P('seq', 'fsdp'), may hold values from -0.1875 to 0.1875
- conv_weight: bfloat16 [3, 1024], P(None, 'fsdp'), may hold values from -3 to 3
- norm_gains: bfloat16 [2, 1024], P(None, 'fsdp'), may hold values from 0.5 to 1.5
- cotangent: float32 [4, 8192, 1024], P('fsdp', 'seq'), may hold values from -6 to 6
Outputs:
- block_out: float32 [4, 8192, 1024], P('fsdp', 'seq')
- grad_tokens: float32 [4, 8192, 1024], P('fsdp', 'seq')
- grad_in: float32 [1024, 3072], P('seq', 'fsdp')
- grad_mix: float32 [1024, 1024], P('seq', 'fsdp')
- grad_gate: float32 [1024, 4608], P('seq', 'fsdp')
- grad_up: float32 [1024, 4608], P('seq', 'fsdp')
- grad_down: float32 [4608, 1024], P('seq', 'fsdp')
- grad_conv: float32 [3, 1024], P(None, 'fsdp')
- grad_gains: float32 [2, 1024], P(None, 'fsdp')
Inputs may be any that keep to these rules, and one draw needn't show every extreme that they name: `token_pos`: 0 at the first token of a sequence and one more at each following token of the same sequence within a stream; every stream starts a sequence at its first token.
All inputs are finite; a program needn't handle non-finite values.
Results may differ from a plain program's by a relative error of at most 0.025.
Values may be sent and summed in bfloat16 or wider, within the bound.
No kernel may reach another device: no remote copies, remote signals or barrier semaphores. Data moves between devices by JAX's collectives and lax.ppermute only.
A program may use at most 192 MiB of HBM per device.

v0:
```python
import functools

import jax
import jax.numpy as jnp
from jax import lax
from jax.experimental import pallas as pl
from jax.experimental.pallas import tpu as pltpu
from jax.sharding import Mesh
from jax.sharding import PartitionSpec as P

EPSILON = 1e-05
SEQ = ("zh", "y", "x")
YX = ("y", "x")
FSDP = ("zl", "c")
ALL = SEQ + FSDP
BF16 = jnp.bfloat16
F32 = jnp.float32


def swap(x, axis):
    return lax.ppermute(x, axis, [(0, 1), (1, 0)])


def gather_group(x):
    far = swap(x, "zl")
    near = swap(x, "c")
    far_near = swap(far, "c")
    return jnp.concatenate([x, near, far, far_near], axis=0)


def scatter_group(partial):
    return finish_scatter(partial[0::2], partial[1::2].astype(BF16))


def finish_scatter(keep, send):
    got = swap(send, "c").astype(F32)
    far = swap((keep[1] + got[1]).astype(BF16), "zl")
    return keep[0] + got[0] + far.astype(F32)


def norm_forward(values, norm_gain):
    inv_rms = lax.rsqrt(jnp.mean(values * values, axis=-1, keepdims=True) + EPSILON)
    normed = values * inv_rms
    return (normed, inv_rms, (normed * norm_gain).astype(BF16))


def norm_backward(grad_hidden, normed, inv_rms, norm_gain):
    grad_normed = grad_hidden * norm_gain
    inner_mean = jnp.mean(grad_normed * normed, axis=-1, keepdims=True)
    return (inv_rms * (grad_normed - normed * inner_mean), jnp.sum(grad_hidden * normed, axis=0))


def dot(a, b, dims):
    return lax.dot_general(a, b, (dims, ((), ())), preferred_element_type=F32)


ROW_ROUTE = [(s * 4 + f, (f * 8 + s % 8) * 4 + s // 8) for s in range(32) for f in range(4)]
ROW_BACK = [(b, a) for a, b in ROW_ROUTE]


def in_zh_order(mine, other):
    first = lax.axis_index("zh") == 0
    return jnp.where(first, jnp.stack([mine, other]), jnp.stack([other, mine]))


def in_member_order(x):
    x = jnp.where(lax.axis_index("c") == 1, jnp.stack([x[1], x[0], x[3], x[2]]), x)
    return jnp.where(lax.axis_index("zl") == 1, jnp.stack([x[2], x[3], x[0], x[1]]), x)


def ffn_kernel(rows_t, h_ref, gl_ref, wg_ref, wd_ref, out_keep, out_send, gh_keep, gh_send, packed,
               wj, wdj, act_s, gp_s, out_acc, gh_acc, g_s, d_s, sems):
    j = pl.program_id(0)
    for k in range(3):
        for zh in range(2):
            wj[512 * zh : 512 * (zh + 1), 256 * k : 256 * (k + 1)] = wg_ref[:, zh, 32 * k : 32 * (k + 1), :].reshape(512, 256)
    for i in range(8):
        at = 8 * j + i
        for f in range(4):
            wdj[48 * i : 48 * (i + 1), 256 * f : 256 * (f + 1)] = wd_ref[
                f % 2 * 8 + at // 3, f // 2, pl.ds(pl.multiple_of(at % 3 * 48, 16), 48), :
            ]

    @pl.when(j == 0)
    def _():
        out_acc[...] = jnp.zeros_like(out_acc)
        gh_acc[...] = jnp.zeros_like(gh_acc)

    def step(t, _):
        rows = pl.ds(pl.multiple_of(t * rows_t, rows_t), rows_t)
        gu = dot(h_ref[rows, :], wj[...], ((1,), (0,)))
        gate, up = gu[:, :384], gu[:, 384:]
        sig = jax.nn.sigmoid(gate)
        silu = gate * sig
        act = (silu * up).astype(BF16)
        grad_act = dot(gl_ref[rows, :], wdj[...], ((1,), (1,)))
        d_gate = grad_act * up * (sig * (1.0 + gate * (1.0 - sig)))
        d_up = grad_act * silu
        act_s[rows, :] = act
        gp_s[rows, :384] = d_gate.astype(BF16)
        gp_s[rows, 384:] = d_up.astype(BF16)
        out_acc[rows, :] += dot(act, wdj[...], ((1,), (0,)))
        gh_acc[rows, :] += dot(gp_s[rows, :], wj[...], ((1,), (1,)))
        return 0

    lax.fori_loop(0, 1024 // rows_t, step, 0)
    for k in range(3):
        acc = dot(h_ref[...], gp_s[:, 256 * k : 256 * (k + 1)], ((0,), (0,))).astype(BF16)
        for zh in range(2):
            g_s[j, :, zh, 32 * k : 32 * (k + 1), :] = acc[512 * zh : 512 * (zh + 1)].reshape(16, 32, 256)
    for f in range(4):
        acc = dot(act_s[...], gl_ref[:, 256 * f : 256 * (f + 1)], ((0,), (0,))).astype(BF16)
        for i in range(8):
            at = 8 * j + i
            d_s[f % 2 * 8 + at // 3, f // 2, pl.ds(pl.multiple_of(at % 3 * 48, 16), 48), :] = acc[48 * i : 48 * (i + 1)]

    def send(i):
        return pltpu.make_async_copy(g_s.at[i], packed.at[:, :, pl.ds(96 * i, 96), :], sems.at[i])

    for i in range(3):
        @pl.when(j == i)
        def _():
            send(i).start()

    @pl.when(j == 2)
    def _():
        last = pltpu.make_async_copy(d_s, packed.at[:, :, pl.ds(288, 144), :], sems.at[3])
        last.start()
        for i in range(2):
            out_keep[i] = out_acc[512 * i : 512 * i + 256]
            gh_keep[i] = gh_acc[512 * i : 512 * i + 256]
            out_send[i] = out_acc[512 * i + 256 : 512 * (i + 1)].astype(BF16)
            gh_send[i] = gh_acc[512 * i + 256 : 512 * (i + 1)].astype(BF16)
        for i in range(3):
            send(i).wait()
        last.wait()

def ffn(h, gl, pack, rows_t=512):
    whole = lambda shape: pl.BlockSpec(shape, lambda j: (0,) * len(shape))
    once = lambda shape: pl.BlockSpec(shape, lambda j: (0,) * len(shape), pipeline_mode=pl.Buffered(1))
    half = (2, 256, 1024)
    return pl.pallas_call(
        functools.partial(ffn_kernel, rows_t),
        grid=(3,),
        in_specs=[once((1024, 1024)), once((1024, 1024)), pl.BlockSpec((16, 2, 96, 256), lambda j: (0, 0, j, 0)),
                  pl.BlockSpec((16, 2, 144, 256), lambda j: (0, 0, 2, 0), pipeline_mode=pl.Buffered(1))],
        out_specs=[once(half)] * 4 + [pl.BlockSpec(memory_space=pl.ANY)],
        out_shape=[jax.ShapeDtypeStruct(half, F32), jax.ShapeDtypeStruct(half, BF16)] * 2 + [jax.ShapeDtypeStruct((16, 2, 432, 256), BF16)],
        scratch_shapes=[pltpu.VMEM((1024, 768), BF16), pltpu.VMEM((384, 1024), BF16), pltpu.VMEM((1024, 384), BF16), pltpu.VMEM((1024, 768), BF16),
            pltpu.VMEM((1024, 1024), F32), pltpu.VMEM((1024, 1024), F32), pltpu.VMEM((3, 16, 2, 96, 256), BF16), pltpu.VMEM((16, 2, 144, 256), BF16),
            pltpu.SemaphoreType.DMA((4,))],
        compiler_params=pltpu.CompilerParams(vmem_limit_bytes=56 * 1024 * 1024, dimension_semantics=("arbitrary",)),
        cost_estimate=pl.CostEstimate(flops=22 * 10**9, bytes_accessed=30 * 10**6, transcendentals=2 * 10**6),
    )(h, gl, pack, pack)


def local(tokens, token_pos, w_in, w_mix, w_gate, w_up, w_down, conv_weight, norm_gains, cotangent):
    inputs = tokens[0]
    grad_result = cotangent[0]
    rows, model = inputs.shape
    f_index = lax.axis_index(FSDP)

    line = jnp.concatenate([norm_gains[:1], norm_gains[1:], jnp.minimum(token_pos, 2).astype(BF16)], axis=1)
    start = gather_group(jnp.concatenate([w_in, line, jnp.zeros((15, 768), BF16)], axis=0)[None])
    in_blocks = []
    for part in range(3):
        column = 4 * part + f_index
        at = (column // 3 ^ f_index, 0, column % 3 * 256)
        in_blocks.append(lax.dynamic_slice(start, at, (1, 32, 256))[0])
    gain_rows = in_member_order(start[:, 32, :512].astype(F32)).reshape(4, 2, 256).transpose(1, 0, 2).reshape(2, 1024)
    positions = start[:, 32, 512:]
    mask_one = (positions >= 1).astype(F32)[:, :, None]
    mask_two = (positions >= 2).astype(F32)[:, :, None]
    conv_taps = conv_weight.astype(F32)

    row_blocks = lax.ppermute(jnp.concatenate([w_mix, w_down], axis=0), ALL, ROW_ROUTE)
    first_pack = jnp.concatenate([*in_blocks, row_blocks[:32]], axis=0)
    first_all = lax.all_to_all(jnp.broadcast_to(first_pack, (32, 128, 256)), SEQ, 0, 0, tiled=True).reshape(32, 128, 256)
    w_in_f = jnp.concatenate([first_all[:, 32 * i : 32 * (i + 1)].reshape(1024, 256) for i in range(3)], axis=1)
    w_mix_f = jnp.concatenate([first_all[8 * i : 8 * (i + 1), 96:].reshape(256, 256) for i in range(4)], axis=1)

    pieces = []
    for at in range(0, 1152, 384):
        pieces.append(w_gate[:, at : at + 256])
        pieces.append(jnp.concatenate([w_gate[:, at + 256 : at + 384], w_up[:, at : at + 128]], axis=1))
        pieces.append(w_up[:, at + 128 : at + 384])
    second_own = jnp.concatenate([*pieces, row_blocks[32:]], axis=0)
    second_pack = in_zh_order(second_own, swap(second_own, "zh"))
    second_all = lax.all_gather(second_pack.reshape(864, 256), YX, axis=0, tiled=True).reshape(16, 2, 432, 256)

    normed1, inv_one, hidden1 = norm_forward(inputs, gain_rows[0])
    hidden1_all = gather_group(hidden1)
    grad_low_all = gather_group(grad_result.astype(BF16))

    mixed = dot(hidden1_all, w_in_f, ((1,), (0,))).reshape(4, rows, 768)
    b_part, c_part, x_part = mixed[..., :256], mixed[..., 256:512], mixed[..., 512:]
    product_bx = (b_part * x_part).astype(BF16)
    arrived = lax.ppermute(product_bx[:, -2:], SEQ, [(i, i + 1) for i in range(31)])
    extended = jnp.concatenate([arrived, product_bx], axis=1).astype(F32)
    current, back_one, back_two = extended[:, 2:], extended[:, 1:-1], extended[:, :-2]
    conv_val = conv_taps[2] * current + conv_taps[1] * mask_one * back_one + conv_taps[0] * mask_two * back_two
    mixer = (c_part * conv_val).astype(BF16).reshape(4 * rows, 256)
    branch = scatter_group(dot(mixer, w_mix_f, ((1,), (0,))).reshape(4, rows, model))
    middle = inputs + branch
    normed2, inv_two, hidden2 = norm_forward(middle, gain_rows[1])
    hidden2_all = gather_group(hidden2)

    out_keep, out_send, grad_keep, grad_send, back_pack = ffn(hidden2_all, grad_low_all, second_all)
    ffn_sums = lax.psum_scatter(back_pack.reshape(16 * 864, 256), YX, scatter_dimension=0, tiled=True).reshape(2, 432, 256)
    ordered = in_zh_order(ffn_sums[0], ffn_sums[1])
    ffn_own = ordered[0].astype(F32) + swap(ordered[1], "zh").astype(F32)
    grad_down = lax.ppermute(ffn_own[288:].astype(BF16), ALL, ROW_BACK).astype(F32)

    grad_hidden2 = finish_scatter(grad_keep, grad_send)
    grad_norm_two, gain_two = norm_backward(grad_hidden2, normed2, inv_two, gain_rows[1])
    grad_middle = grad_result + grad_norm_two
    grad_branch_all = gather_group(grad_middle.astype(BF16))
    out_got = swap(out_send, "c").astype(F32)
    out_far, _ = lax.optimization_barrier(((out_keep[1] + out_got[1]).astype(BF16), grad_branch_all))
    out_far = swap(out_far, "zl")
    result = middle + out_keep[0] + out_got[0] + out_far.astype(F32)
    grad_mix = dot(mixer, grad_branch_all, ((0,), (0,))).astype(BF16)
    grad_mixer = dot(grad_branch_all, w_mix_f, ((1,), (1,))).reshape(4, rows, 256)
    grad_c = grad_mixer * conv_val
    grad_cv = grad_mixer * c_part
    lag_one = grad_cv * mask_one
    lag_two = grad_cv * mask_two
    later = lax.ppermute(
        jnp.concatenate([lag_one[:, :1], lag_two[:, :2]], axis=1), SEQ, [(i + 1, i) for i in range(31)]
    )
    ahead_one = jnp.concatenate([lag_one[:, 1:], later[:, :1]], axis=1)
    ahead_two = jnp.concatenate([lag_two[:, 2:], later[:, 1:]], axis=1)
    grad_bx = conv_taps[2] * grad_cv + conv_taps[1] * ahead_one + conv_taps[0] * ahead_two
    conv_grads = jnp.stack(
        [
            jnp.sum(lag_two * back_two, axis=(0, 1)),
            jnp.sum(lag_one * back_one, axis=(0, 1)),
            jnp.sum(grad_cv * current, axis=(0, 1)),
        ]
    )
    grad_bx_low = lax.optimization_barrier(grad_bx.astype(BF16)).astype(F32)
    grad_mixed = (
        jnp.concatenate([grad_bx_low * x_part, grad_c, grad_bx_low * b_part], axis=-1).astype(BF16).reshape(4 * rows, 768)
    )
    grad_in = dot(hidden1_all, grad_mixed, ((0,), (0,)))
    gain_one = jnp.sum(grad_in * w_in_f.astype(F32), axis=1) / gain_rows[0]
    small = jnp.concatenate(
        [gain_one.reshape(4, 256), gain_two.reshape(4, 256), conv_grads, jnp.zeros((5, 256), F32)], axis=0
    ).astype(BF16)
    grad_in = grad_in.astype(BF16)
    first_back = jnp.concatenate(
        [grad_in[:, 256 * i : 256 * (i + 1)].reshape(32, 32, 256) for i in range(3)]
        + [jnp.concatenate([grad_mix[:, 256 * i : 256 * (i + 1)].reshape(8, 32, 256) for i in range(4)], axis=0)]
        + [jnp.broadcast_to(small, (32, 16, 256))],
        axis=1,
    )
    first_back, _ = lax.optimization_barrier((first_back, out_far))
    first_got = lax.all_to_all(first_back, SEQ, 0, 0, tiled=True).reshape(32, 144, 256)
    first_got, _ = lax.optimization_barrier((first_got, grad_down))
    first_sums = jnp.sum(first_got.astype(F32), axis=0)
    conv_total = first_sums[136:139]
    group_sums = gather_group(first_sums[None].astype(BF16))
    in_own = []
    for i in range(3):
        column = 3 * f_index + i
        in_own.append(lax.dynamic_slice(group_sums, (column % 4 ^ f_index, column // 4 * 32, 0), (1, 32, 256))[0])
    grad_in_own = jnp.concatenate(in_own, axis=1).astype(F32)
    gain_terms = group_sums[:, 128:136].reshape(4, 2, 4, 256).astype(F32)
    gains_total = jnp.sum(lax.dynamic_index_in_dim(gain_terms, f_index, axis=2, keepdims=False), axis=0)
    grad_mix_own = lax.ppermute(first_sums[96:128].astype(BF16), ALL, ROW_BACK).astype(F32)

    grad_hidden1 = scatter_group(dot(grad_mixed, w_in_f, ((1,), (1,))).reshape(4, rows, model))
    grad_norm_one, _ = norm_backward(grad_hidden1, normed1, inv_one, gain_rows[0])
    grad_inputs = grad_middle + grad_norm_one

    grad_gu = ffn_own[:288].reshape(9, 32, 256)
    grad_gate = [c for i in (0, 3, 6) for c in (grad_gu[i], grad_gu[i + 1, :, :128])]
    grad_up = [c for i in (0, 3, 6) for c in (grad_gu[i + 1, :, 128:], grad_gu[i + 2])]
    return (
        result[None],
        grad_inputs[None],
        grad_in_own,
        grad_mix_own,
        jnp.concatenate(grad_gate, axis=1),
        jnp.concatenate(grad_up, axis=1),
        grad_down,
        conv_total,
        gains_total,
    )


def solution(mesh):
    fine = Mesh(mesh.devices.reshape(2, 4, 4, 2, 2), ALL)
    tokens, weight, small = P(FSDP, SEQ, None), P(SEQ, FSDP), P(None, FSDP)
    return jax.shard_map(
        local,
        mesh=fine,
        in_specs=(tokens, P(FSDP, SEQ), weight, weight, weight, weight, weight, small, small, tokens),
        out_specs=(tokens, tokens, weight, weight, weight, weight, weight, small, small),
        check_vma=False,
    )
```

profile of v0, /device:TPU:30, one launch (start us, length us, event | category | flops | bytes accessed | tf_op | source)
XLA Modules:
  0.0 324.7 jit_solution(6197635854366550251)
XLA Ops:
  8.2 2.6 collective-permute-start.6
  15.9 4.4 %collective-permute-start.16 = (bf16[432,256]{1,0:T(8,128)(2,1)S(1)}, bf16[432,256]{1,0:T(8,128)(2,1)S(1)}, u32[]{:S(2)}, u32[]{:S(2)}) collective-permute-start(bf16[432,256]{1,0:T(8,128)(2,1)S(1)} %slice_dynamic-update-slice_fusion), channel_id=1, source_target_pairs={{0,64},{64,0},{1,65},{65,1},{2,66},{66,2},{3,67},{67,3},{4,68},{68... | collective-permute-start | bytes 663560 | tf_op jit(solution)/shard_map/ppermute | solution.py:21
  20.3 4.3 %collective-permute-done.16 = bf16[432,256]{1,0:T(8,128)(2,1)S(1)} collective-permute-done((bf16[432,256]{1,0:T(8,128)(2,1)S(1)}, bf16[432,256]{1,0:T(8,128)(2,1)S(1)}, u32[]{:S(2)}, u32[]{:S(2)}) %collective-permute-start.16) | collective-permute-done | bytes 221216 | tf_op jit(solution)/shard_map/ppermute | solution.py:21
  27.1 3.0 collective-permute-start.1
  30.2 2.2 collective-permute-done.1
  32.4 1.2 collective-permute-done.2
  33.8 1.6 broadcast_in_dim.30
  35.4 9.2 %all-to-all-start = ((bf16[32,128,256]{2,1,0:T(8,128)(2,1)}), bf16[32,128,256]{2,1,0:T(8,128)(2,1)S(1)}, u32[]{:S(2)}, u32[]{:S(2)}) async-start(bf16[32,128,256]{2,1,0:T(8,128)(2,1)} %broadcast_in_dim.30), calls=%async_computation | async-start | bytes 4194304 | tf_op jit(solution)/shard_map/all_to_all | solution.py:178
  46.2 33.1 %collective-permute-done.4 = bf16[256,1024]{1,0:T(8,128)(2,1)} collective-permute-done((bf16[256,1024]{1,0:T(8,128)(2,1)}, bf16[256,1024]{1,0:T(8,128)(2,1)}, u32[]{:S(2)}, u32[]{:S(2)}) %collective-permute-start.4) | collective-permute-done | bytes 524320 | tf_op jit(solution)/shard_map/ppermute | solution.py:21
  79.5 2.0 collective-permute-done.5
  81.6 3.3 %fusion.40 = f32[1024,768]{1,0:T(8,128)S(1)} fusion(bf16[256,1024]{1,0:T(8,128)(2,1)} %collective-permute-done.5, bf16[256,1024]{1,0:T(8,128)(2,1)} %collective-permute-done.4, bf16[256,1024]{1,0:T(8,128)(2,1)} %collective-permute-done.3, bf16[256,1024]{1,0:T(8,128)(2,1)} %multiply_convert_fusion.4, bf16[1024,256]{1,0:T(8,128)(2,1)S(1)} %bitcast.208, ...), kind=kOutput, calls=%fused_computation.88 | convolution fusion | flops 1623719936 | bytes 6815744 | tf_op jit(solution)/shard_map/dot_general | solution.py:54
  85.0 5.8 %collective-permute-start.7 = (bf16[4,2,256]{2,1,0:T(2,128)(2,1)S(1)}, bf16[4,2,256]{2,1,0:T(2,128)(2,1)S(1)}, u32[]{:S(2)}, u32[]{:S(2)}) collective-permute-start(bf16[4,2,256]{2,1,0:T(2,128)(2,1)S(1)} %slice.456), channel_id=1, source_target_pairs={{0,4},{4,8},{8,12},{12,16},{16,20},{20,24},{24,28},{28,32},{32,36}... | collective-permute-start | bytes 12296 | tf_op jit(solution)/shard_map/ppermute | solution.py:198
  91.0 1.2 collective-permute-done.7
  92.3 1.5 multiply_convert_fusion.2
  95.0 2.4 collective-permute-done.8
  100.1 12.6 %collective-permute-done.9 = bf16[256,1024]{1,0:T(8,128)(2,1)S(1)} collective-permute-done((bf16[256,1024]{1,0:T(8,128)(2,1)S(1)}, bf16[256,1024]{1,0:T(8,128)(2,1)S(1)}, u32[]{:S(2)}, u32[]{:S(2)}) %collective-permute-start.9) | collective-permute-done | bytes 524320 | tf_op jit(solution)/shard_map/ppermute | solution.py:21
  113.9 10.1 %collective-permute-done.14 = bf16[256,1024]{1,0:T(8,128)(2,1)S(1)} collective-permute-done((bf16[256,1024]{1,0:T(8,128)(2,1)S(1)}, bf16[256,1024]{1,0:T(8,128)(2,1)S(1)}, u32[]{:S(2)}, u32[]{:S(2)}) %collective-permute-start.14) | collective-permute-done | bytes 524320 | tf_op jit(solution)/shard_map/ppermute | solution.py:21
  124.5 9.9 %collective-permute-done.11 = bf16[256,1024]{1,0:T(8,128)(2,1)S(1)} collective-permute-done((bf16[256,1024]{1,0:T(8,128)(2,1)S(1)}, bf16[256,1024]{1,0:T(8,128)(2,1)S(1)}, u32[]{:S(2)}, u32[]{:S(2)}) %collective-permute-start.11) | collective-permute-done | bytes 524320 | tf_op jit(solution)/shard_map/ppermute | solution.py:21
  134.4 1.6 pad_maximum_fusion.2.gl_ref
  136.3 1.5 pad_maximum_fusion.1.h_ref
  137.8 34.8 %shard_map.169 = (f32[2,256,1024]{2,1,0:T(8,128)}, bf16[2,256,1024]{2,1,0:T(8,128)(2,1)}, f32[2,256,1024]{2,1,0:T(8,128)}, bf16[2,256,1024]{2,1,0:T(8,128)(2,1)}, bf16[16,2,432,256]{3,2,1,0:T(8,128)(2,1)}) custom-call(bf16[1024,1024]{1,0:T(8,128)(2,1)} %pad_maximum_fusion.1.h_ref, bf16[1024,1024]{1,0:T(8,128)(2,1)} %pad_maximum_fusion.2.gl_ref, ...), custom_call_target="tpu_custom_call" | custom-call | flops 22000001024 | bytes 30000000 | tf_op jit(solution)/shard_map/pallas_call | solution.py:142
  172.9 2.7 collective-permute-done.18
  176.7 13.5 %collective-permute-done.19 = bf16[256,1024]{1,0:T(8,128)(2,1)S(1)} collective-permute-done((bf16[256,1024]{1,0:T(8,128)(2,1)S(1)}, bf16[256,1024]{1,0:T(8,128)(2,1)S(1)}, u32[]{:S(2)}, u32[]{:S(2)}) %collective-permute-start.19) | collective-permute-done | bytes 524320 | tf_op jit(solution)/shard_map/ppermute | solution.py:21
  190.6 1.6 fusion.50
  192.8 13.1 %collective-permute-done.21 = bf16[256,1024]{1,0:T(8,128)(2,1)} collective-permute-done((bf16[256,1024]{1,0:T(8,128)(2,1)}, bf16[256,1024]{1,0:T(8,128)(2,1)}, u32[]{:S(2)}, u32[]{:S(2)}) %collective-permute-start.21) | collective-permute-done | bytes 524320 | tf_op jit(solution)/shard_map/ppermute | solution.py:21
  205.8 1.6 convert_element_type.191
  207.5 1.4 copy-done.9
  210.4 1.8 pad_maximum_fusion.3
  215.0 1.9 collective-permute-start.24
  221.1 5.8 %collective-permute-done.24 = f32[4,3,256]{2,1,0:T(4,128)S(1)} collective-permute-done((f32[4,3,256]{2,1,0:T(4,128)S(1)}, f32[4,3,256]{2,1,0:T(4,128)S(1)}, u32[]{:S(2)}, u32[]{:S(2)}) %collective-permute-start.24) | collective-permute-done | bytes 12320 | tf_op jit(solution)/shard_map/ppermute | solution.py:228
  228.6 3.8 %fusion.64 = (bf16[4,256,1024]{2,1,0:T(8,128)(2,1)S(1)}, f32[4,256,1024]{2,1,0:T(8,128)}) fusion(bf16[1024,256]{1,0:T(8,128)(2,1)S(1)} %bitcast.209, bf16[1024,256]{1,0:T(8,128)(2,1)S(1)} %bitcast.212, bf16[1024,256]{1,0:T(8,128)(2,1)S(1)} %bitcast.206, bf16[4,256,256]{2,1,0:T(8,128)(2,1)S(1)} %get-tuple-element.45, ...), kind=kOutput, calls=%fused_computation.184 | convolution fusion | flops 1621098496 | bytes 9437184 | tf_op jit(solution)/shard_map/dot_general | solution.py:54
  233.5 4.7 %multiply_reduce_fusion = (f32[1024]{0:T(1024)S(1)}, bf16[1024,768]{1,0:T(8,128)(2,1)}) fusion(bf16[1024,256]{1,0:T(8,128)(2,1)S(1)} %bitcast.210, bf16[1024,256]{1,0:T(8,128)(2,1)S(1)} %bitcast.213, bf16[1024,256]{1,0:T(8,128)(2,1)S(1)} %bitcast.207, bf16[1024,256]{1,0:T(8,128)(2,1)S(1)} %bitcast.200, bf16[1024,256]{1,0:T(8,128)(2,1)S(1)} %bitcast.198, ...), kind=kOutput, calls=%fused_computation.1 | convolution fusion | flops 1630796800 | bytes 6819840 | tf_op jit(solution)/shard_map/dot_general | solution.py:54
  238.2 1.5 fusion.55
  243.2 1.5 slice.404
  245.0 1.4 copy-done.1
  249.2 6.8 %all-to-all-start.1 = ((bf16[32,144,256]{2,1,0:T(8,128)(2,1)}), bf16[32,144,256]{2,1,0:T(8,128)(2,1)}, u32[]{:S(2)}, u32[]{:S(2)}) async-start(bf16[32,144,256]{2,1,0:T(8,128)(2,1)} %broadcast_dynamic-update-slice_fusion), calls=%async_computation.1 | async-start | bytes 4718592 | tf_op jit(solution)/shard_map/all_to_all | solution.py:258
  256.1 3.2 fusion.25
  259.3 27.4 %collective-permute-done.26 = bf16[256,1024]{1,0:T(8,128)(2,1)} collective-permute-done((bf16[256,1024]{1,0:T(8,128)(2,1)}, bf16[256,1024]{1,0:T(8,128)(2,1)}, u32[]{:S(2)}, u32[]{:S(2)}) %collective-permute-start.26) | collective-permute-done | bytes 524320 | tf_op jit(solution)/shard_map/ppermute | solution.py:21
  286.6 1.4 multiply_reduce_fusion.5
  288.1 1.2 slice_bitcast_fusion.4
  289.9 2.7 add_bitcast_fusion
  292.6 5.1 %collective-permute-done.27 = bf16[432,256]{1,0:T(8,128)(2,1)S(1)} collective-permute-done((bf16[432,256]{1,0:T(8,128)(2,1)S(1)}, bf16[432,256]{1,0:T(8,128)(2,1)S(1)}, u32[]{:S(2)}, u32[]{:S(2)}) %collective-permute-start.27) | collective-permute-done | bytes 221216 | tf_op jit(solution)/shard_map/ppermute | solution.py:21
  297.8 1.9 collective-permute-start.28
  299.8 5.2 %collective-permute-done.28 = bf16[144,256]{1,0:T(8,128)(2,1)S(1)} collective-permute-done((bf16[144,256]{1,0:T(8,128)(2,1)S(1)}, bf16[144,256]{1,0:T(8,128)(2,1)S(1)}, u32[]{:S(2)}, u32[]{:S(2)}) %collective-permute-start.28) | collective-permute-done | bytes 73760 | tf_op jit(solution)/shard_map/ppermute | solution.py:212
  305.7 2.0 convert_reduce_fusion
  307.7 1.6 collective-permute-start.30
  309.4 1.9 collective-permute-start.32
  312.8 3.2 collective-permute-done.32
  (239 shorter events, 41.8 us)
Async XLA Ops:
  7.2 19.9 %copy-start.29 = (bf16[32,768]{1,0:T(8,128)(2,1)S(1)}, bf16[32,768]{1,0:T(8,128)(2,1)}, u32[]{:S(2)}) copy-start(bf16[32,768]{1,0:T(8,128)(2,1)} %param.12) | copy-start | bytes 147460
  7.2 22.9 %copy-start = (f32[1,256,1024]{2,1,0:T(8,128)S(1)}, f32[1,256,1024]{2,1,0:T(8,128)}, u32[]{:S(2)}) copy-start(f32[1,256,1024]{2,1,0:T(8,128)} %param.10) | copy-start | bytes 3145732
  7.2 130.6 %all-gather.2.cloned.1.call-start = ((), (), s32[]{:S(2)}) async-start(), calls=%async_computation.3 | async-start | bytes 7520256 | tf_op jit(solution)/shard_map/all_gather | solution.py:189
  8.2 7.7 %collective-permute-start.6 = (bf16[176,256]{1,0:T(8,128)(2,1)S(1)}, bf16[176,256]{1,0:T(8,128)(2,1)S(1)}, u32[]{:S(2)}, u32[]{:S(2)}) collective-permute-start(bf16[176,256]{1,0:T(8,128)(2,1)S(1)} %pad_maximum_fusion.10), channel_id=1, source_target_pairs={{0,0},{1,32},{2,64},{3,96},{4,4},{5,36},{6,68},{7,100},{8,8},{9,40... | collective-permute-start | bytes 270344 | tf_op jit(solution)/shard_map/ppermute | solution.py:176
  15.9 8.7 %collective-permute-start.16 = (bf16[432,256]{1,0:T(8,128)(2,1)S(1)}, bf16[432,256]{1,0:T(8,128)(2,1)S(1)}, u32[]{:S(2)}, u32[]{:S(2)}) collective-permute-start(bf16[432,256]{1,0:T(8,128)(2,1)S(1)} %slice_dynamic-update-slice_fusion), channel_id=1, source_target_pairs={{0,64},{64,0},{1,65},{65,1},{2,66},{66,2},{3,67},{67,3},{4,68},{68... | collective-permute-start | bytes 663560 | tf_op jit(solution)/shard_map/ppermute | solution.py:21
  27.1 5.3 %collective-permute-start.1 = (bf16[1,48,768]{2,1,0:T(8,128)(2,1)S(1)}, bf16[1,48,768]{2,1,0:T(8,128)(2,1)S(1)}, u32[]{:S(2)}, u32[]{:S(2)}) collective-permute-start(bf16[1,48,768]{2,1,0:T(8,128)(2,1)S(1)} %maximum_bitcast_fusion), channel_id=1, source_target_pairs={{0,2},{2,0},{1,3},{3,1},{4,6},{6,4},{5,7},{7,5},{8,10},{10,8},{9,1... | collective-permute-start | bytes 221192 | tf_op jit(solution)/shard_map/ppermute | solution.py:21
  30.1 2.4 collective-permute-start
  32.4 1.3 collective-permute-start.2
  35.4 10.7 %copy-start.34 = (bf16[3,256]{1,0:T(4,128)(2,1)S(1)}, bf16[3,256]{1,0:T(4,128)(2,1)}, u32[]{:S(2)}) copy-start(bf16[3,256]{1,0:T(4,128)(2,1)} %param.17) | copy-start | bytes 4612
  35.4 44.0 %all-to-all-start = ((bf16[32,128,256]{2,1,0:T(8,128)(2,1)}), bf16[32,128,256]{2,1,0:T(8,128)(2,1)S(1)}, u32[]{:S(2)}, u32[]{:S(2)}) async-start(bf16[32,128,256]{2,1,0:T(8,128)(2,1)} %broadcast_in_dim.30), calls=%async_computation | async-start | bytes 4194304 | tf_op jit(solution)/shard_map/all_to_all | solution.py:178
  44.5 243.6 %reduce-scatter.2.cloned.1.call-start = ((), (), s32[]{:S(2)}) async-start(), calls=%async_computation.4 | async-start | bytes 7520256 | tf_op jit(solution)/shard_map/reduce_scatter | solution.py:209
  45.8 33.5 %collective-permute-start.4 = (bf16[256,1024]{1,0:T(8,128)(2,1)}, bf16[256,1024]{1,0:T(8,128)(2,1)}, u32[]{:S(2)}, u32[]{:S(2)}) collective-permute-start(bf16[256,1024]{1,0:T(8,128)(2,1)} %multiply_convert_fusion.4), channel_id=1, source_target_pairs={{0,2},{2,0},{1,3},{3,1},{4,6},{6,4},{5,7},{7,5},{8,10},{10,8},{9,1... | collective-permute-start | bytes 1572872 | tf_op jit(solution)/shard_map/ppermute | solution.py:21
  46.1 46.2 %copy-start.30 = (f32[1,256]{1,0:T(1,128)}, f32[1,256]{1,0:T(1,128)S(1)}, u32[]{:S(2)}) copy-start(f32[1,256]{1,0:T(1,128)S(1)} %get-tuple-element.99) | copy-start | bytes 3076
  46.1 33.4 %collective-permute-start.3 = (bf16[256,1024]{1,0:T(8,128)(2,1)}, bf16[256,1024]{1,0:T(8,128)(2,1)}, u32[]{:S(2)}, u32[]{:S(2)}) collective-permute-start(bf16[256,1024]{1,0:T(8,128)(2,1)} %multiply_convert_fusion.4), channel_id=1, source_target_pairs={{0,1},{1,0},{2,3},{3,2},{4,5},{5,4},{6,7},{7,6},{8,9},{9,8},{10,11... | collective-permute-start | bytes 1572872 | tf_op jit(solution)/shard_map/ppermute | solution.py:21
  79.3 2.3 collective-permute-start.5
  84.9 7.4 %copy-start.7 = (f32[1024,768]{1,0:T(8,128)}, f32[1024,768]{1,0:T(8,128)S(1)}, u32[]{:S(2)}) copy-start(f32[1024,768]{1,0:T(8,128)S(1)} %fusion.40) | copy-start | bytes 9437188
  85.0 7.2 %collective-permute-start.7 = (bf16[4,2,256]{2,1,0:T(2,128)(2,1)S(1)}, bf16[4,2,256]{2,1,0:T(2,128)(2,1)S(1)}, u32[]{:S(2)}, u32[]{:S(2)}) collective-permute-start(bf16[4,2,256]{2,1,0:T(2,128)(2,1)S(1)} %slice.456), channel_id=1, source_target_pairs={{0,4},{4,8},{8,12},{12,16},{16,20},{20,24},{24,28},{28,32},{32,36}... | collective-permute-start | bytes 12296 | tf_op jit(solution)/shard_map/ppermute | solution.py:198
  94.7 2.7 collective-permute-start.8
  97.9 14.8 %collective-permute-start.9 = (bf16[256,1024]{1,0:T(8,128)(2,1)S(1)}, bf16[256,1024]{1,0:T(8,128)(2,1)S(1)}, u32[]{:S(2)}, u32[]{:S(2)}) collective-permute-start(bf16[256,1024]{1,0:T(8,128)(2,1)S(1)} %fusion.34), channel_id=1, source_target_pairs={{0,2},{2,0},{1,3},{3,1},{4,6},{6,4},{5,7},{7,5},{8,10},{10,8},{9,1... | collective-permute-start | bytes 1572872 | tf_op jit(solution)/shard_map/ppermute | solution.py:21
  99.0 24.9 %collective-permute-start.14 = (bf16[256,1024]{1,0:T(8,128)(2,1)S(1)}, bf16[256,1024]{1,0:T(8,128)(2,1)S(1)}, u32[]{:S(2)}, u32[]{:S(2)}) collective-permute-start(bf16[256,1024]{1,0:T(8,128)(2,1)S(1)} %bitcast_convert_fusion), channel_id=1, source_target_pairs={{0,2},{2,0},{1,3},{3,1},{4,6},{6,4},{5,7},{7,5},{8,10},{10,8},{9,1... | collective-permute-start | bytes 1572872 | tf_op jit(solution)/shard_map/ppermute | solution.py:21
  113.3 21.1 %collective-permute-start.11 = (bf16[256,1024]{1,0:T(8,128)(2,1)S(1)}, bf16[256,1024]{1,0:T(8,128)(2,1)S(1)}, u32[]{:S(2)}, u32[]{:S(2)}) collective-permute-start(bf16[256,1024]{1,0:T(8,128)(2,1)S(1)} %multiply_convert_fusion.1), channel_id=1, source_target_pairs={{0,2},{2,0},{1,3},{3,1},{4,6},{6,4},{5,7},{7,5},{8,10},{10,8},{9,1... | collective-permute-start | bytes 1572872 | tf_op jit(solution)/shard_map/ppermute | solution.py:21
  113.9 20.5 %collective-permute-start.13 = (bf16[256,1024]{1,0:T(8,128)(2,1)S(1)}, bf16[256,1024]{1,0:T(8,128)(2,1)S(1)}, u32[]{:S(2)}, u32[]{:S(2)}) collective-permute-start(bf16[256,1024]{1,0:T(8,128)(2,1)S(1)} %bitcast_convert_fusion), channel_id=1, source_target_pairs={{0,1},{1,0},{2,3},{3,2},{4,5},{5,4},{6,7},{7,6},{8,9},{9,8},{10,11... | collective-permute-start | bytes 1572872 | tf_op jit(solution)/shard_map/ppermute | solution.py:21
  124.0 10.4 %collective-permute-start.15 = (bf16[256,1024]{1,0:T(8,128)(2,1)S(1)}, bf16[256,1024]{1,0:T(8,128)(2,1)S(1)}, u32[]{:S(2)}, u32[]{:S(2)}) collective-permute-start(bf16[256,1024]{1,0:T(8,128)(2,1)S(1)} %collective-permute-done.14), channel_id=1, source_target_pairs={{0,1},{1,0},{2,3},{3,2},{4,5},{5,4},{6,7},{7,6},{8,9},{9,8},{10,11... | collective-permute-start | bytes 1572872 | tf_op jit(solution)/shard_map/ppermute | solution.py:21
  124.0 12.0 %collective-permute-start.10 = (bf16[256,1024]{1,0:T(8,128)(2,1)S(1)}, bf16[256,1024]{1,0:T(8,128)(2,1)S(1)}, u32[]{:S(2)}, u32[]{:S(2)}) collective-permute-start(bf16[256,1024]{1,0:T(8,128)(2,1)S(1)} %multiply_convert_fusion.1), channel_id=1, source_target_pairs={{0,1},{1,0},{2,3},{3,2},{4,5},{5,4},{6,7},{7,6},{8,9},{9,8},{10,11... | collective-permute-start | bytes 1572872 | tf_op jit(solution)/shard_map/ppermute | solution.py:21
  134.4 1.9 collective-permute-start.12
  172.7 3.0 collective-permute-start.18
  176.0 14.1 %collective-permute-start.19 = (bf16[256,1024]{1,0:T(8,128)(2,1)S(1)}, bf16[256,1024]{1,0:T(8,128)(2,1)S(1)}, u32[]{:S(2)}, u32[]{:S(2)}) collective-permute-start(bf16[256,1024]{1,0:T(8,128)(2,1)S(1)} %fusion.36), channel_id=1, source_target_pairs={{0,2},{2,0},{1,3},{3,1},{4,6},{6,4},{5,7},{7,5},{8,10},{10,8},{9,1... | collective-permute-start | bytes 1572872 | tf_op jit(solution)/shard_map/ppermute | solution.py:21
  176.7 14.0 %copy-start.13 = (f32[1,256,1024]{2,1,0:T(8,128)S(1)}, f32[1,256,1024]{2,1,0:T(8,128)}, u32[]{:S(2)}) copy-start(f32[1,256,1024]{2,1,0:T(8,128)} %param.19) | copy-start | bytes 3145732
  176.7 29.2 %collective-permute-start.17 = (bf16[2,256,1024]{2,1,0:T(8,128)(2,1)}, bf16[2,256,1024]{2,1,0:T(8,128)(2,1)}, u32[]{:S(2)}, u32[]{:S(2)}) collective-permute-start(bf16[2,256,1024]{2,1,0:T(8,128)(2,1)} %get-tuple-element.18), channel_id=1, source_target_pairs={{0,1},{1,0},{2,3},{3,2},{4,5},{5,4},{6,7},{7,6},{8,9},{9,8},{10,11... | collective-permute-start | bytes 3145736 | tf_op jit(solution)/shard_map/ppermute | solution.py:21
  192.2 13.6 %collective-permute-start.21 = (bf16[256,1024]{1,0:T(8,128)(2,1)}, bf16[256,1024]{1,0:T(8,128)(2,1)}, u32[]{:S(2)}, u32[]{:S(2)}) collective-permute-start(bf16[256,1024]{1,0:T(8,128)(2,1)} %get-tuple-element.37), channel_id=1, source_target_pairs={{0,2},{2,0},{1,3},{3,1},{4,6},{6,4},{5,7},{7,5},{8,10},{10,8},{9,1... | collective-permute-start | bytes 1572872 | tf_op jit(solution)/shard_map/ppermute | solution.py:21
  192.8 17.6 %collective-permute-start.20 = (bf16[256,1024]{1,0:T(8,128)(2,1)}, bf16[256,1024]{1,0:T(8,128)(2,1)}, u32[]{:S(2)}, u32[]{:S(2)}) collective-permute-start(bf16[256,1024]{1,0:T(8,128)(2,1)} %get-tuple-element.37), channel_id=1, source_target_pairs={{0,1},{1,0},{2,3},{3,2},{4,5},{5,4},{6,7},{7,6},{8,9},{9,8},{10,11... | collective-permute-start | bytes 1572872 | tf_op jit(solution)/shard_map/ppermute | solution.py:21
  205.8 4.5 %collective-permute-start.22 = (bf16[256,1024]{1,0:T(8,128)(2,1)}, bf16[256,1024]{1,0:T(8,128)(2,1)}, u32[]{:S(2)}, u32[]{:S(2)}) collective-permute-start(bf16[256,1024]{1,0:T(8,128)(2,1)} %collective-permute-done.21), channel_id=1, source_target_pairs={{0,1},{1,0},{2,3},{3,2},{4,5},{5,4},{6,7},{7,6},{8,9},{9,8},{10,11... | collective-permute-start | bytes 1572872 | tf_op jit(solution)/shard_map/ppermute | solution.py:21
  215.0 11.9 %collective-permute-start.24 = (f32[4,3,256]{2,1,0:T(4,128)S(1)}, f32[4,3,256]{2,1,0:T(4,128)S(1)}, u32[]{:S(2)}, u32[]{:S(2)}) collective-permute-start(f32[4,3,256]{2,1,0:T(4,128)S(1)} %pad_maximum_fusion.14), channel_id=1, source_target_pairs={{4,0},{8,4},{12,8},{16,12},{20,16},{24,20},{28,24},{32,28},{36,32}... | collective-permute-start | bytes 36872 | tf_op jit(solution)/shard_map/ppermute | solution.py:228
  218.4 8.6 %copy-start.31 = (f32[1,256]{1,0:T(1,128)S(1)}, f32[1,256]{1,0:T(1,128)}, u32[]{:S(2)}) copy-start(f32[1,256]{1,0:T(1,128)} %copy-done.30) | copy-start | bytes 3076
  220.3 28.9 %collective-permute-start.23 = (bf16[256,1024]{1,0:T(8,128)(2,1)}, bf16[256,1024]{1,0:T(8,128)(2,1)}, u32[]{:S(2)}, u32[]{:S(2)}) collective-permute-start(bf16[256,1024]{1,0:T(8,128)(2,1)} %fusion.35), channel_id=1, source_target_pairs={{0,2},{2,0},{1,3},{3,1},{4,6},{6,4},{5,7},{7,5},{8,10},{10,8},{9,1... | collective-permute-start | bytes 1572872 | tf_op jit(solution)/shard_map/ppermute | solution.py:21
  233.4 11.3 %collective-permute-start.25 = (bf16[2,256,1024]{2,1,0:T(8,128)(2,1)}, bf16[2,256,1024]{2,1,0:T(8,128)(2,1)S(1)}, u32[]{:S(2)}, u32[]{:S(2)}) collective-permute-start(bf16[2,256,1024]{2,1,0:T(8,128)(2,1)} %slice.406), channel_id=1, source_target_pairs={{0,1},{1,0},{2,3},{3,2},{4,5},{5,4},{6,7},{7,6},{8,9},{9,8},{10,11... | collective-permute-start | bytes 3145736 | tf_op jit(solution)/shard_map/ppermute | solution.py:21
  247.9 38.7 %collective-permute-start.26 = (bf16[256,1024]{1,0:T(8,128)(2,1)}, bf16[256,1024]{1,0:T(8,128)(2,1)}, u32[]{:S(2)}, u32[]{:S(2)}) collective-permute-start(bf16[256,1024]{1,0:T(8,128)(2,1)} %fusion.37), channel_id=1, source_target_pairs={{0,2},{2,0},{1,3},{3,1},{4,6},{6,4},{5,7},{7,5},{8,10},{10,8},{9,1... | collective-permute-start | bytes 1572872 | tf_op jit(solution)/shard_map/ppermute | solution.py:21
  249.2 56.4 %all-to-all-start.1 = ((bf16[32,144,256]{2,1,0:T(8,128)(2,1)}), bf16[32,144,256]{2,1,0:T(8,128)(2,1)}, u32[]{:S(2)}, u32[]{:S(2)}) async-start(bf16[32,144,256]{2,1,0:T(8,128)(2,1)} %broadcast_dynamic-update-slice_fusion), calls=%async_computation.1 | async-start | bytes 4718592 | tf_op jit(solution)/shard_map/all_to_all | solution.py:258
  256.1 30.6 %copy-start.2 = (f32[2,256,1024]{2,1,0:T(8,128)S(1)}, f32[2,256,1024]{2,1,0:T(8,128)}, u32[]{:S(2)}) copy-start(f32[2,256,1024]{2,1,0:T(8,128)} %slice.404) | copy-start | bytes 6291460
  256.1 30.6 %copy-start.5 = (f32[2,256,1024]{2,1,0:T(8,128)S(1)}, f32[2,256,1024]{2,1,0:T(8,128)}, u32[]{:S(2)}) copy-start(f32[2,256,1024]{2,1,0:T(8,128)} %copy-done.4) | copy-start | bytes 6291460
  259.3 30.3 %copy-start.3 = (f32[2,256,1024]{2,1,0:T(8,128)S(1)}, f32[2,256,1024]{2,1,0:T(8,128)}, u32[]{:S(2)}) copy-start(f32[2,256,1024]{2,1,0:T(8,128)} %slice.404) | copy-start | bytes 6291460
  289.4 8.3 %collective-permute-start.27 = (bf16[432,256]{1,0:T(8,128)(2,1)S(1)}, bf16[432,256]{1,0:T(8,128)(2,1)S(1)}, u32[]{:S(2)}, u32[]{:S(2)}) collective-permute-start(bf16[432,256]{1,0:T(8,128)(2,1)S(1)} %slice_bitcast_fusion.1), channel_id=1, source_target_pairs={{0,64},{64,0},{1,65},{65,1},{2,66},{66,2},{3,67},{67,3},{4,68},{68... | collective-permute-start | bytes 663560 | tf_op jit(solution)/shard_map/ppermute | solution.py:21
  297.8 7.2 %collective-permute-start.28 = (bf16[144,256]{1,0:T(8,128)(2,1)S(1)}, bf16[144,256]{1,0:T(8,128)(2,1)S(1)}, u32[]{:S(2)}, u32[]{:S(2)}) collective-permute-start(bf16[144,256]{1,0:T(8,128)(2,1)S(1)} %slice.649), channel_id=1, source_target_pairs={{0,0},{32,1},{64,2},{96,3},{4,4},{36,5},{68,6},{100,7},{8,8},{40,9... | collective-permute-start | bytes 221192 | tf_op jit(solution)/shard_map/ppermute | solution.py:212
  307.7 4.4 %collective-permute-start.30 = (bf16[1,144,256]{2,1,0:T(8,128)(2,1)S(1)}, bf16[1,144,256]{2,1,0:T(8,128)(2,1)S(1)}, u32[]{:S(2)}, u32[]{:S(2)}) collective-permute-start(bf16[1,144,256]{2,1,0:T(8,128)(2,1)S(1)} %convert_bitcast_fusion), channel_id=1, source_target_pairs={{0,2},{2,0},{1,3},{3,1},{4,6},{6,4},{5,7},{7,5},{8,10},{10,8},{9,1... | collective-permute-start | bytes 221192 | tf_op jit(solution)/shard_map/ppermute | solution.py:21
  309.2 8.7 %copy-start.35 = (f32[32,1152]{1,0:T(8,128)}, f32[32,1152]{1,0:T(8,128)S(1)}, u32[]{:S(2)}) copy-start(f32[32,1152]{1,0:T(8,128)S(1)} %get-tuple-element.63) | copy-start | bytes 442372
  309.2 7.3 %collective-permute-start.29 = (bf16[1,144,256]{2,1,0:T(8,128)(2,1)S(1)}, bf16[1,144,256]{2,1,0:T(8,128)(2,1)S(1)}, u32[]{:S(2)}, u32[]{:S(2)}) collective-permute-start(bf16[1,144,256]{2,1,0:T(8,128)(2,1)S(1)} %convert_bitcast_fusion), channel_id=1, source_target_pairs={{0,1},{1,0},{2,3},{3,2},{4,5},{5,4},{6,7},{7,6},{8,9},{9,8},{10,11... | collective-permute-start | bytes 221192 | tf_op jit(solution)/shard_map/ppermute | solution.py:21
  309.4 6.6 %collective-permute-start.32 = (bf16[32,256]{1,0:T(8,128)(2,1)S(1)}, bf16[32,256]{1,0:T(8,128)(2,1)S(1)}, u32[]{:S(2)}, u32[]{:S(2)}) collective-permute-start(bf16[32,256]{1,0:T(8,128)(2,1)S(1)} %slice.499), channel_id=1, source_target_pairs={{0,0},{32,1},{64,2},{96,3},{4,4},{36,5},{68,6},{100,7},{8,8},{40,9... | collective-permute-start | bytes 49160 | tf_op jit(solution)/shard_map/ppermute | solution.py:270
  312.1 4.4 %collective-permute-start.31 = (bf16[1,144,256]{2,1,0:T(8,128)(2,1)S(1)}, bf16[1,144,256]{2,1,0:T(8,128)(2,1)S(1)}, u32[]{:S(2)}, u32[]{:S(2)}) collective-permute-start(bf16[1,144,256]{2,1,0:T(8,128)(2,1)S(1)} %collective-permute-done.30), channel_id=1, source_target_pairs={{0,1},{1,0},{2,3},{3,2},{4,5},{5,4},{6,7},{7,6},{8,9},{9,8},{10,11... | collective-permute-start | bytes 221192 | tf_op jit(solution)/shard_map/ppermute | solution.py:21
  (28 other events, 69.9 us)
Sparse Core Ops, SparseCore 0:
  25.6 85.4 all-gather.1
  172.8 81.8 reduce-scatter.1
where the time goes:
time: 326 us; the launch traced here: 325 us
  waiting for transfers between devices  156 us (48%)
  starting transfers between devices  45.6 us (14%)
  Pallas kernels  34.8 us (11%)
  other arithmetic  31.7 us (10%)
  local copies, waits for them, and re-layouts  27.5 us (8%)
  between operations  15 us (5%)
  matrix products  14 us (4%)
    ppermute x28, waiting for transfers between devices, swap(): return lax.ppermute(x, axis, [(0, 1), (1, 0)])  141 us
    pallas_call x1, Pallas kernels, ffn(): pl.pallas_call(functools.partial(ffn_kernel, rows_t), grid=(3,), in_specs...  34.8 us
    ppermute x28, starting transfers between devices, swap(): return lax.ppermute(x, axis, [(0, 1), (1, 0)])  15.4 us
    dot_general x6, matrix products, dot(): return lax.dot_general(a, b, (dims, ((), ())), preferred_element_type=F32)  14 us
    unnamed x93, local copies, waits for them, and re-layouts  13.7 us
    all_to_all x1, starting transfers between devices, local(): lax.all_to_all(jnp.broadcast_to(first_pack, (32, 128, 256)), SEQ, 0, 0, t...  9.15 us
    all_to_all x1, starting transfers between devices, local(): lax.all_to_all(first_back, SEQ, 0, 0, tiled=True).reshape(32, 144, 256)  6.83 us
  transfers between devices with their start and end apart: 37, of which 20 were waited for; matrix products, arithmetic and copies ran while one was open for 19% of the time, Pallas kernels for 0%

commit v1 on v0

--- a/solution.py
+++ b/solution.py
@@ -21,11 +21,19 @@
     return lax.ppermute(x, axis, [(0, 1), (1, 0)])
 
 
-def gather_group(x):
+def group_blocks(x):
     far = swap(x, "zl")
     near = swap(x, "c")
-    far_near = swap(far, "c")
-    return jnp.concatenate([x, near, far, far_near], axis=0)
+    return (x, near, far, swap(far, "c"))
+
+
+def gather_group(x):
+    across = lax.ppermute(x, FSDP, [(f, 3 - f) for f in range(4)])
+    return jnp.concatenate((x, swap(x, "c"), swap(x, "zl"), across), axis=0)
+
+
+def after(x, *others):
+    return lax.optimization_barrier((x, *others))[0]
 
 
 def scatter_group(partial):
@@ -56,6 +64,7 @@
 
 ROW_ROUTE = [(s * 4 + f, (f * 8 + s % 8) * 4 + s // 8) for s in range(32) for f in range(4)]
 ROW_BACK = [(b, a) for a, b in ROW_ROUTE]
+ROW_OTHER = [(a, (b + 64) % 128) for a, b in ROW_ROUTE]
 
 
 def in_zh_order(mine, other):
@@ -68,8 +77,10 @@
     return jnp.where(lax.axis_index("zl") == 1, jnp.stack([x[2], x[3], x[0], x[1]]), x)
 
 
-def ffn_kernel(rows_t, h_ref, gl_ref, wg_ref, wd_ref, out_keep, out_send, gh_keep, gh_send, packed,
-               wj, wdj, act_s, gp_s, out_acc, gh_acc, g_s, d_s, sems):
+def ffn_kernel(rows_t, *refs):
+    h_blocks, gl_blocks = refs[:4], refs[4:8]
+    wg_ref, wd_ref, out_keep, out_send, gh_keep, gh_send, packed = refs[8:15]
+    h_ref, gl_ref, wj, wdj, act_s, gp_s, out_acc, gh_acc, g_s, d_s, sems = refs[15:]
     j = pl.program_id(0)
     for k in range(3):
         for zh in range(2):
@@ -83,6 +94,9 @@
 
     @pl.when(j == 0)
     def _():
+        for i in range(4):
+            h_ref[256 * i : 256 * (i + 1), :] = h_blocks[i][...]
+            gl_ref[256 * i : 256 * (i + 1), :] = gl_blocks[i][...]
         out_acc[...] = jnp.zeros_like(out_acc)
         gh_acc[...] = jnp.zeros_like(gh_acc)
 
@@ -142,16 +156,97 @@
     return pl.pallas_call(
         functools.partial(ffn_kernel, rows_t),
         grid=(3,),
-        in_specs=[once((1024, 1024)), once((1024, 1024)), pl.BlockSpec((16, 2, 96, 256), lambda j: (0, 0, j, 0)),
+        in_specs=[once((256, 1024))] * 8 + [pl.BlockSpec((16, 2, 96, 256), lambda j: (0, 0, j, 0)),
                   pl.BlockSpec((16, 2, 144, 256), lambda j: (0, 0, 2, 0), pipeline_mode=pl.Buffered(1))],
         out_specs=[once(half)] * 4 + [pl.BlockSpec(memory_space=pl.ANY)],
         out_shape=[jax.ShapeDtypeStruct(half, F32), jax.ShapeDtypeStruct(half, BF16)] * 2 + [jax.ShapeDtypeStruct((16, 2, 432, 256), BF16)],
-        scratch_shapes=[pltpu.VMEM((1024, 768), BF16), pltpu.VMEM((384, 1024), BF16), pltpu.VMEM((1024, 384), BF16), pltpu.VMEM((1024, 768), BF16),
+        scratch_shapes=[pltpu.VMEM((1024, 1024), BF16)] * 2 + [pltpu.VMEM((1024, 768), BF16), pltpu.VMEM((384, 1024), BF16), pltpu.VMEM((1024, 384), BF16), pltpu.VMEM((1024, 768), BF16),
             pltpu.VMEM((1024, 1024), F32), pltpu.VMEM((1024, 1024), F32), pltpu.VMEM((3, 16, 2, 96, 256), BF16), pltpu.VMEM((16, 2, 144, 256), BF16),
             pltpu.SemaphoreType.DMA((4,))],
         compiler_params=pltpu.CompilerParams(vmem_limit_bytes=56 * 1024 * 1024, dimension_semantics=("arbitrary",)),
         cost_estimate=pl.CostEstimate(flops=22 * 10**9, bytes_accessed=30 * 10**6, transcendentals=2 * 10**6),
-    )(h, gl, pack, pack)
+    )(*h, *gl, pack, pack)
+
+
+def mix_back_kernel(gm_ref, gmix_ref, mixed_ref, cv_ref, bx_ref, arrived_ref, later_ref, one_ref, two_ref, taps_ref,
+                    h_ref, w_ref, gains_ref, gain_two_ref, back_ref, keep_ref, send_ref, grads, small):
+    rows = lax.broadcasted_iota(jnp.int32, (256, 256), 0)
+    taps = taps_ref[...]
+    tap_grads = [jnp.zeros((1, 256), F32) for _ in range(3)]
+    gain_one = jnp.zeros((1, 1024), F32)
+    for s in range(4):
+        grad_mixer = gm_ref[s]
+        b_part, c_part, x_part = (mixed_ref[s, :, 256 * i : 256 * (i + 1)] for i in range(3))
+        grad_cv = grad_mixer * c_part
+        lag_one, lag_two = grad_cv * one_ref[s], grad_cv * two_ref[s]
+        later = later_ref[s]
+        ahead_one = jnp.where(rows == 255, later[0:1], pltpu.roll(lag_one, 255, 0))
+        ahead_two = jnp.where(rows == 255, later[2:3], jnp.where(rows == 254, later[1:2], pltpu.roll(lag_two, 254, 0)))
+        current = bx_ref[s].astype(F32)
+        before = arrived_ref[s].astype(F32)
+        back_one = jnp.where(rows == 0, before[1:2], pltpu.roll(current, 1, 0))
+        back_two = jnp.where(rows == 0, before[0:1], jnp.where(rows == 1, before[1:2], pltpu.roll(current, 2, 0)))
+        for i, term in enumerate((lag_two * back_two, lag_one * back_one, grad_cv * current)):
+            tap_grads[i] += jnp.sum(term, axis=0, keepdims=True)
+        grad_bx = taps[2:3] * grad_cv + taps[1:2] * ahead_one + taps[0:1] * ahead_two
+        grad_bx = grad_bx.astype(BF16).astype(F32)
+        at = slice(256 * s, 256 * (s + 1))
+        grads[at, 0:256] = (grad_bx * x_part).astype(BF16)
+        grads[at, 256:512] = (grad_mixer * cv_ref[s]).astype(BF16)
+        grads[at, 512:768] = (grad_bx * b_part).astype(BF16)
+        grad_h = dot(grads[at, :], w_ref[...], ((1,), (1,)))
+        gain_one += jnp.sum(grad_h * h_ref[at, :].astype(F32), axis=0, keepdims=True)
+        if s % 2 == 0:
+            keep_ref[s // 2] = grad_h
+        else:
+            send_ref[s // 2] = grad_h.astype(BF16)
+    gain_one = gain_one / gains_ref[0:1, :]
+    small[...] = jnp.zeros_like(small)
+    for i in range(4):
+        small[i : i + 1] = gain_one[:, 256 * i : 256 * (i + 1)]
+        small[4 + i : 5 + i] = gain_two_ref[:, 256 * i : 256 * (i + 1)]
+    for i in range(3):
+        small[8 + i : 9 + i] = tap_grads[i]
+    back_ref[:, 128:144, :] = jnp.broadcast_to(small[...].astype(BF16)[None], (32, 16, 256))
+    for i in range(3):
+        grad_in = dot(h_ref[...], grads[:, 256 * i : 256 * (i + 1)], ((0,), (0,)))
+        back_ref[:, 32 * i : 32 * (i + 1), :] = grad_in.astype(BF16).reshape(32, 32, 256)
+    for i in range(4):
+        back_ref[8 * i : 8 * (i + 1), 96:128, :] = gmix_ref[:, 256 * i : 256 * (i + 1)].reshape(8, 32, 256)
+
+
+def mix_back(*args):
+    vmem = pl.BlockSpec(memory_space=pltpu.VMEM)
+    half = (2, 256, 1024)
+    return pl.pallas_call(
+        mix_back_kernel,
+        in_specs=[vmem] * len(args),
+        out_specs=[vmem] * 3,
+        out_shape=[jax.ShapeDtypeStruct((32, 144, 256), BF16), jax.ShapeDtypeStruct(half, F32), jax.ShapeDtypeStruct(half, BF16)],
+        scratch_shapes=[pltpu.VMEM((1024, 768), BF16), pltpu.VMEM((16, 256), F32)],
+        compiler_params=pltpu.CompilerParams(vmem_limit_bytes=40 * 1024 * 1024),
+        cost_estimate=pl.CostEstimate(flops=4 * 10**9, bytes_accessed=10**7, transcendentals=0),
+    )(*args)
+
+
+def pack_columns_kernel(gate_ref, up_ref, out_ref):
+    for j in range(3):
+        at = 384 * j
+        out_ref[96 * j : 96 * j + 32, :] = gate_ref[:, at : at + 256]
+        out_ref[96 * j + 32 : 96 * j + 64, 0:128] = gate_ref[:, at + 256 : at + 384]
+        out_ref[96 * j + 32 : 96 * j + 64, 128:256] = up_ref[:, at : at + 128]
+        out_ref[96 * j + 64 : 96 * j + 96, :] = up_ref[:, at + 128 : at + 384]
+
+
+def pack_columns(w_gate, w_up):
+    vmem = pl.BlockSpec(memory_space=pltpu.VMEM)
+    return pl.pallas_call(
+        pack_columns_kernel,
+        in_specs=[vmem] * 2,
+        out_specs=vmem,
+        out_shape=jax.ShapeDtypeStruct((288, 256), BF16),
+        compiler_params=pltpu.CompilerParams(vmem_limit_bytes=4 * 1024 * 1024),
+    )(w_gate, w_up)
 
 
 def local(tokens, token_pos, w_in, w_mix, w_gate, w_up, w_down, conv_weight, norm_gains, cotangent):
@@ -159,6 +254,7 @@
     grad_result = cotangent[0]
     rows, model = inputs.shape
     f_index = lax.axis_index(FSDP)
+    grad_low_all = group_blocks(grad_result.astype(BF16))
 
     line = jnp.concatenate([norm_gains[:1], norm_gains[1:], jnp.minimum(token_pos, 2).astype(BF16)], axis=1)
     start = gather_group(jnp.concatenate([w_in, line, jnp.zeros((15, 768), BF16)], axis=0)[None])
@@ -173,24 +269,23 @@
     mask_two = (positions >= 2).astype(F32)[:, :, None]
     conv_taps = conv_weight.astype(F32)
 
+    gu_own = pack_columns(w_gate, w_up)
+    gu_far = swap(gu_own, "zh")
     row_blocks = lax.ppermute(jnp.concatenate([w_mix, w_down], axis=0), ALL, ROW_ROUTE)
+    down_far = lax.ppermute(w_down, ALL, ROW_OTHER)
+    second_pack = jnp.concatenate([in_zh_order(gu_own, gu_far), in_zh_order(row_blocks[32:], down_far)], axis=1)
+    second_all = lax.all_gather(second_pack.reshape(864, 256), YX, axis=0, tiled=True).reshape(16, 2, 432, 256)
+
     first_pack = jnp.concatenate([*in_blocks, row_blocks[:32]], axis=0)
     first_all = lax.all_to_all(jnp.broadcast_to(first_pack, (32, 128, 256)), SEQ, 0, 0, tiled=True).reshape(32, 128, 256)
+    grad_low_all = group_blocks(grad_result.astype(BF16))
+    first_all = after(first_all, *grad_low_all)
     w_in_f = jnp.concatenate([first_all[:, 32 * i : 32 * (i + 1)].reshape(1024, 256) for i in range(3)], axis=1)
     w_mix_f = jnp.concatenate([first_all[8 * i : 8 * (i + 1), 96:].reshape(256, 256) for i in range(4)], axis=1)
 
-    pieces = []
-    for at in range(0, 1152, 384):
-        pieces.append(w_gate[:, at : at + 256])
-        pieces.append(jnp.concatenate([w_gate[:, at + 256 : at + 384], w_up[:, at : at + 128]], axis=1))
-        pieces.append(w_up[:, at + 128 : at + 384])
-    second_own = jnp.concatenate([*pieces, row_blocks[32:]], axis=0)
-    second_pack = in_zh_order(second_own, swap(second_own, "zh"))
-    second_all = lax.all_gather(second_pack.reshape(864, 256), YX, axis=0, tiled=True).reshape(16, 2, 432, 256)
-
     normed1, inv_one, hidden1 = norm_forward(inputs, gain_rows[0])
-    hidden1_all = gather_group(hidden1)
-    grad_low_all = gather_group(grad_result.astype(BF16))
+    hidden1_blocks = group_blocks(hidden1)
+    hidden1_all = jnp.concatenate(hidden1_blocks, axis=0)
 
     mixed = dot(hidden1_all, w_in_f, ((1,), (0,))).reshape(4, rows, 768)
     b_part, c_part, x_part = mixed[..., :256], mixed[..., 256:512], mixed[..., 512:]
@@ -203,7 +298,7 @@
     branch = scatter_group(dot(mixer, w_mix_f, ((1,), (0,))).reshape(4, rows, model))
     middle = inputs + branch
     normed2, inv_two, hidden2 = norm_forward(middle, gain_rows[1])
-    hidden2_all = gather_group(hidden2)
+    hidden2_all = group_blocks(hidden2)
 
     out_keep, out_send, grad_keep, grad_send, back_pack = ffn(hidden2_all, grad_low_all, second_all)
     ffn_sums = lax.psum_scatter(back_pack.reshape(16 * 864, 256), YX, scatter_dimension=0, tiled=True).reshape(2, 432, 256)
@@ -214,47 +309,32 @@
     grad_hidden2 = finish_scatter(grad_keep, grad_send)
     grad_norm_two, gain_two = norm_backward(grad_hidden2, normed2, inv_two, gain_rows[1])
     grad_middle = grad_result + grad_norm_two
-    grad_branch_all = gather_group(grad_middle.astype(BF16))
+    grad_branch_all = jnp.concatenate(group_blocks(grad_middle.astype(BF16)), axis=0)
     out_got = swap(out_send, "c").astype(F32)
     out_far, _ = lax.optimization_barrier(((out_keep[1] + out_got[1]).astype(BF16), grad_branch_all))
     out_far = swap(out_far, "zl")
     result = middle + out_keep[0] + out_got[0] + out_far.astype(F32)
     grad_mix = dot(mixer, grad_branch_all, ((0,), (0,))).astype(BF16)
     grad_mixer = dot(grad_branch_all, w_mix_f, ((1,), (1,))).reshape(4, rows, 256)
-    grad_c = grad_mixer * conv_val
-    grad_cv = grad_mixer * c_part
-    lag_one = grad_cv * mask_one
-    lag_two = grad_cv * mask_two
-    later = lax.ppermute(
-        jnp.concatenate([lag_one[:, :1], lag_two[:, :2]], axis=1), SEQ, [(i + 1, i) for i in range(31)]
+    edge = grad_mixer[:, :2] * c_part[:, :2]
+    later = jnp.concatenate([edge[:, :1] * mask_one[:, :1], edge * mask_two[:, :2]], axis=1)
+    later = lax.ppermute(later, SEQ, [(i + 1, i) for i in range(31)])
+    first_back, keep, send = mix_back(
+        grad_mixer,
+        grad_mix,
+        mixed,
+        conv_val,
+        product_bx,
+        arrived,
+        later,
+        mask_one,
+        mask_two,
+        conv_taps,
+        hidden1_all,
+        w_in_f,
+        gain_rows,
+        gain_two[None],
     )
-    ahead_one = jnp.concatenate([lag_one[:, 1:], later[:, :1]], axis=1)
-    ahead_two = jnp.concatenate([lag_two[:, 2:], later[:, 1:]], axis=1)
-    grad_bx = conv_taps[2] * grad_cv + conv_taps[1] * ahead_one + conv_taps[0] * ahead_two
-    conv_grads = jnp.stack(
-        [
-            jnp.sum(lag_two * back_two, axis=(0, 1)),
-            jnp.sum(lag_one * back_one, axis=(0, 1)),
-            jnp.sum(grad_cv * current, axis=(0, 1)),
-        ]
-    )
-    grad_bx_low = lax.optimization_barrier(grad_bx.astype(BF16)).astype(F32)
-    grad_mixed = (
-        jnp.concatenate([grad_bx_low * x_part, grad_c, grad_bx_low * b_part], axis=-1).astype(BF16).reshape(4 * rows, 768)
-    )
-    grad_in = dot(hidden1_all, grad_mixed, ((0,), (0,)))
-    gain_one = jnp.sum(grad_in * w_in_f.astype(F32), axis=1) / gain_rows[0]
-    small = jnp.concatenate(
-        [gain_one.reshape(4, 256), gain_two.reshape(4, 256), conv_grads, jnp.zeros((5, 256), F32)], axis=0
-    ).astype(BF16)
-    grad_in = grad_in.astype(BF16)
-    first_back = jnp.concatenate(
-        [grad_in[:, 256 * i : 256 * (i + 1)].reshape(32, 32, 256) for i in range(3)]
-        + [jnp.concatenate([grad_mix[:, 256 * i : 256 * (i + 1)].reshape(8, 32, 256) for i in range(4)], axis=0)]
-        + [jnp.broadcast_to(small, (32, 16, 256))],
-        axis=1,
-    )
-    first_back, _ = lax.optimization_barrier((first_back, out_far))
     first_got = lax.all_to_all(first_back, SEQ, 0, 0, tiled=True).reshape(32, 144, 256)
     first_got, _ = lax.optimization_barrier((first_got, grad_down))
     first_sums = jnp.sum(first_got.astype(F32), axis=0)
@@ -269,7 +349,7 @@
     gains_total = jnp.sum(lax.dynamic_index_in_dim(gain_terms, f_index, axis=2, keepdims=False), axis=0)
     grad_mix_own = lax.ppermute(first_sums[96:128].astype(BF16), ALL, ROW_BACK).astype(F32)
 
-    grad_hidden1 = scatter_group(dot(grad_mixed, w_in_f, ((1,), (1,))).reshape(4, rows, model))
+    grad_hidden1 = finish_scatter(keep, send)
     grad_norm_one, _ = norm_backward(grad_hidden1, normed1, inv_one, gain_rows[0])
     grad_inputs = grad_middle + grad_norm_one
 

time: 326 us -> 312 us (0.957)
  local copies, waits for them, and re-layouts: 27.5 us -> 18.4 us
  matrix products: 14 us -> 5.46 us
  other arithmetic: 31.7 us -> 24.4 us
  Pallas kernels: 34.8 us -> 41.4 us
  starting transfers between devices: 45.6 us -> 48.9 us
    dot_general x6 -> x4, matrix products: 14 us -> 5.46 us  [dot(): return lax.dot_general(a, b, (dims, ((), ())), preferred_element_type=F32)]
    ppermute x1 -> x4, starting transfers between devices: 1.92 us -> 10 us  [the longest x1 5.5 us: local(): down_far = lax.ppermute(w_down, ALL, ROW_OTHER)]
    pallas_call x0 -> x2, Pallas kernels: none -> 6.25 us  [the longest x1 6.23 us: mix_back(): pl.pallas_call(mix_back_kernel, in_specs=[vmem] * len(args), out_specs=[v...]
    ppermute x28 -> x26, starting transfers between devices: 15.4 us -> 10.3 us  [swap(): return lax.ppermute(x, axis, [(0, 1), (1, 0)])]
    ppermute x1 -> x4, waiting for transfers between devices: 5.79 us -> 9.37 us  [the longest x1 8.73 us: local(): later = lax.ppermute(later, SEQ, [(i + 1, i) for i in range(31)])]
    unnamed x93 -> x106, local copies, waits for them, and re-layouts: 13.7 us -> 10.4 us
    ppermute x28 -> x26, waiting for transfers between devices: 141 us -> 139 us  [swap(): return lax.ppermute(x, axis, [(0, 1), (1, 0)])]
  transfers between devices with their start and end apart: 37 -> 38, of which waited for: 20 -> 18; matrix products, arithmetic and copies ran while one was open for 19% -> 11% of each run, Pallas kernels for 0% -> 2%
where the time goes in v1:
time: 312 us; the launch traced here: 311 us
  waiting for transfers between devices  157 us (50%)
  starting transfers between devices  48.9 us (16%)
  Pallas kernels  41.4 us (13%)
  other arithmetic  24.4 us (8%)
  local copies, waits for them, and re-layouts  18.4 us (6%)
  between operations  15.2 us (5%)
  matrix products  5.46 us (2%)
    ppermute x26, waiting for transfers between devices, swap(): return lax.ppermute(x, axis, [(0, 1), (1, 0)])  139 us
    pallas_call x1, Pallas kernels, ffn(): pl.pallas_call(functools.partial(ffn_kernel, rows_t), grid=(3,), in_specs...  35.2 us
    unnamed x106, local copies, waits for them, and re-layouts  10.4 us
    ppermute x26, starting transfers between devices, swap(): return lax.ppermute(x, axis, [(0, 1), (1, 0)])  10.3 us
    all_to_all x1, starting transfers between devices, local(): lax.all_to_all(jnp.broadcast_to(first_pack, (32, 128, 256)), SEQ, 0, 0, t...  9.36 us
    ppermute x1, waiting for transfers between devices, local(): later = lax.ppermute(later, SEQ, [(i + 1, i) for i in range(31)])  8.73 us
    all_to_all x1, starting transfers between devices, local(): lax.all_to_all(first_back, SEQ, 0, 0, tiled=True).reshape(32, 144, 256)  6.96 us
  transfers between devices with their start and end apart: 38, of which 18 were waited for; matrix products, arithmetic and copies ran while one was open for 11% of the time, Pallas kernels for 2%

profile of v1, /device:TPU:30, one launch (start us, length us, event | category | flops | bytes accessed | tf_op | source)
XLA Modules:
  0.0 311.1 jit_solution(6460448881142673318)
XLA Ops:
  8.1 2.6 collective-permute-start.6
  10.7 5.5 %collective-permute-start.17 = (bf16[144,256]{1,0:T(8,128)(2,1)}, bf16[144,256]{1,0:T(8,128)(2,1)S(1)}, u32[]{:S(2)}, u32[]{:S(2)}) collective-permute-start(bf16[144,256]{1,0:T(8,128)(2,1)} %param.16), channel_id=1, source_target_pairs={{0,64},{1,96},{2,0},{3,32},{4,68},{5,100},{6,4},{7,36},{8,72},{9,1... | collective-permute-start | bytes 221192 | tf_op jit(solution)/shard_map/ppermute | solution.py:275
  18.0 2.2 collective-permute-start.16
  20.2 4.5 %collective-permute-done.16 = bf16[288,256]{1,0:T(8,128)(2,1)S(1)} collective-permute-done((bf16[288,256]{1,0:T(8,128)(2,1)S(1)}, bf16[288,256]{1,0:T(8,128)(2,1)S(1)}, u32[]{:S(2)}, u32[]{:S(2)}) %collective-permute-start.16) | collective-permute-done | bytes 147488 | tf_op jit(solution)/shard_map/ppermute | solution.py:21
  26.0 1.8 collective-permute-start.2
  28.5 2.6 collective-permute-done.1
  31.8 1.6 broadcast_in_dim.27
  33.4 9.4 %all-to-all-start = ((bf16[32,128,256]{2,1,0:T(8,128)(2,1)}), bf16[32,128,256]{2,1,0:T(8,128)(2,1)}, u32[]{:S(2)}, u32[]{:S(2)}) async-start(bf16[32,128,256]{2,1,0:T(8,128)(2,1)} %broadcast_in_dim.27), calls=%async_computation | async-start | bytes 4194304 | tf_op jit(solution)/shard_map/all_to_all | solution.py:280
  44.7 33.9 %collective-permute-done.4 = bf16[256,1024]{1,0:T(8,128)(2,1)S(1)} collective-permute-done((bf16[256,1024]{1,0:T(8,128)(2,1)S(1)}, bf16[256,1024]{1,0:T(8,128)(2,1)S(1)}, u32[]{:S(2)}, u32[]{:S(2)}) %collective-permute-start.4) | collective-permute-done | bytes 524320 | tf_op jit(solution)/shard_map/ppermute | solution.py:21
  79.5 1.5 fusion.36
  81.1 3.3 %fusion.30 = f32[1024,768]{1,0:T(8,128)S(1)} fusion(bf16[1024,256]{1,0:T(8,128)(2,1)S(1)} %bitcast.195, bf16[1024,256]{1,0:T(8,128)(2,1)S(1)} %bitcast.197, bf16[1024,256]{1,0:T(8,128)(2,1)S(1)} %bitcast.193, bf16[256,1024]{1,0:T(8,128)(2,1)} %collective-permute-done.5, bf16[256,1024]{1,0:T(8,128)(2,1)S(1)} %collective-permute-done.4, ...), kind=kOutput, calls=%fused_computation.132 | convolution fusion | flops 1623719936 | bytes 6815744 | tf_op jit(solution)/shard_map/dot_general | solution.py:62
  84.6 5.4 %collective-permute-start.10 = (bf16[4,2,256]{2,1,0:T(2,128)(2,1)S(1)}, bf16[4,2,256]{2,1,0:T(2,128)(2,1)S(1)}, u32[]{:S(2)}, u32[]{:S(2)}) collective-permute-start(bf16[4,2,256]{2,1,0:T(2,128)(2,1)S(1)} %slice.361), channel_id=1, source_target_pairs={{0,4},{4,8},{8,12},{12,16},{16,20},{20,24},{24,28},{28,32},{32,36}... | collective-permute-start | bytes 12296 | tf_op jit(solution)/shard_map/ppermute | solution.py:293
  90.0 1.1 fusion.35
  91.5 1.5 fusion.18
  94.2 2.3 collective-permute-done.11
  97.1 13.9 %collective-permute-done.12 = bf16[256,1024]{1,0:T(8,128)(2,1)S(1)} collective-permute-done((bf16[256,1024]{1,0:T(8,128)(2,1)S(1)}, bf16[256,1024]{1,0:T(8,128)(2,1)S(1)}, u32[]{:S(2)}, u32[]{:S(2)}) %collective-permute-start.12) | collective-permute-done | bytes 524320 | tf_op jit(solution)/shard_map/ppermute | solution.py:21
  111.9 13.0 %collective-permute-done.14.refs_2_ = bf16[256,1024]{1,0:T(8,128)(2,1)S(1)} collective-permute-done((bf16[256,1024]{1,0:T(8,128)(2,1)S(1)}, bf16[256,1024]{1,0:T(8,128)(2,1)S(1)}, u32[]{:S(2)}, u32[]{:S(2)}) %collective-permute-start.14) | collective-permute-done | bytes 524320 | tf_op jit(solution)/shard_map/ppermute | solution.py:21
  124.9 2.0 collective-permute-done.15.refs_3_
  126.9 35.2 %shard_map.170 = (f32[2,256,1024]{2,1,0:T(8,128)}, bf16[2,256,1024]{2,1,0:T(8,128)(2,1)}, f32[2,256,1024]{2,1,0:T(8,128)}, bf16[2,256,1024]{2,1,0:T(8,128)(2,1)}, bf16[16,2,432,256]{3,2,1,0:T(8,128)(2,1)}) custom-call(bf16[256,1024]{1,0:T(8,128)(2,1)} %copy-done.34, bf16[256,1024]{1,0:T(8,128)(2,1)} %copy-done.47, bf16[256,1024]{1,0:T(8,128)(2,1)} %copy-done.46, ...), custom_call_target="tpu_custom_call" | custom-call | flops 22000001024 | bytes 30000000 | tf_op jit(solution)/shard_map/pallas_call | solution.py:156
  162.2 1.2 copy-done.44
  163.5 2.5 collective-permute-done.19
  167.1 13.4 %collective-permute-done.20 = bf16[256,1024]{1,0:T(8,128)(2,1)S(1)} collective-permute-done((bf16[256,1024]{1,0:T(8,128)(2,1)S(1)}, bf16[256,1024]{1,0:T(8,128)(2,1)S(1)}, u32[]{:S(2)}, u32[]{:S(2)}) %collective-permute-start.20) | collective-permute-done | bytes 524320 | tf_op jit(solution)/shard_map/ppermute | solution.py:21
  181.0 1.3 fusion.31
  183.2 1.0 copy.53.two_ref
  184.4 11.2 %collective-permute-done.22 = bf16[256,1024]{1,0:T(8,128)(2,1)S(1)} collective-permute-done((bf16[256,1024]{1,0:T(8,128)(2,1)S(1)}, bf16[256,1024]{1,0:T(8,128)(2,1)S(1)}, u32[]{:S(2)}, u32[]{:S(2)}) %collective-permute-start.22) | collective-permute-done | bytes 524320 | tf_op jit(solution)/shard_map/ppermute | solution.py:21
  195.6 1.7 pad_maximum_fusion.h_ref
  197.6 1.2 copy-done.43
  200.6 0.9 broadcast_multiply_fusion
  201.6 2.1 collective-permute-start.25
  204.5 8.7 %collective-permute-done.25.later_ref = f32[4,3,256]{2,1,0:T(4,128)S(1)} collective-permute-done((f32[4,3,256]{2,1,0:T(4,128)S(1)}, f32[4,3,256]{2,1,0:T(4,128)S(1)}, u32[]{:S(2)}, u32[]{:S(2)}) %collective-permute-start.25) | collective-permute-done | bytes 12320 | tf_op jit(solution)/shard_map/ppermute | solution.py:321
  213.3 6.2 %shard_map.171 = (bf16[32,144,256]{2,1,0:T(8,128)(2,1)S(1)}, f32[2,256,1024]{2,1,0:T(8,128)S(1)}, bf16[2,256,1024]{2,1,0:T(8,128)(2,1)S(1)}) custom-call(f32[4,256,256]{2,1,0:T(8,128)S(1)} %bitcast.186, bf16[256,1024]{1,0:T(8,128)(2,1)S(1)} %convolution_convert_fusion.gmix_ref, f32[4,256,768]{2,1,0:T(8,128)} %bitcast.192, f32[4,256,256]{2,1,0:T(8,128)S(1)} %copy-done.1, ...), custom_call_target="tpu_custom_call" | custom-call | flops 4000000000 | bytes 10000000 | tf_op jit(solution)/shard_map/pallas_call | solution.py:221
  219.9 2.8 copy-done.19
  224.4 1.3 copy-done.10
  226.6 1.5 collective-permute-start.27
  228.1 7.0 %all-to-all-start.1 = ((bf16[32,144,256]{2,1,0:T(8,128)(2,1)}), bf16[32,144,256]{2,1,0:T(8,128)(2,1)}, u32[]{:S(2)}, u32[]{:S(2)}) async-start(bf16[32,144,256]{2,1,0:T(8,128)(2,1)} %copy-done), calls=%async_computation.1 | async-start | bytes 4718592 | tf_op jit(solution)/shard_map/all_to_all | solution.py:338
  235.1 8.7 %collective-permute-done.24 = bf16[256,1024]{1,0:T(8,128)(2,1)} collective-permute-done((bf16[256,1024]{1,0:T(8,128)(2,1)}, bf16[256,1024]{1,0:T(8,128)(2,1)}, u32[]{:S(2)}, u32[]{:S(2)}) %collective-permute-start.24) | collective-permute-done | bytes 524320 | tf_op jit(solution)/shard_map/ppermute | solution.py:21
  243.9 3.1 fusion.10
  246.9 26.5 %collective-permute-done.27 = bf16[256,1024]{1,0:T(8,128)(2,1)} collective-permute-done((bf16[256,1024]{1,0:T(8,128)(2,1)}, bf16[256,1024]{1,0:T(8,128)(2,1)}, u32[]{:S(2)}, u32[]{:S(2)}) %collective-permute-start.27) | collective-permute-done | bytes 524320 | tf_op jit(solution)/shard_map/ppermute | solution.py:21
  273.4 1.4 multiply_reduce_fusion
  274.9 1.2 slice_bitcast_fusion.4
  276.7 2.7 add_bitcast_fusion
  279.4 4.3 %collective-permute-done.28 = bf16[432,256]{1,0:T(8,128)(2,1)S(1)} collective-permute-done((bf16[432,256]{1,0:T(8,128)(2,1)S(1)}, bf16[432,256]{1,0:T(8,128)(2,1)S(1)}, u32[]{:S(2)}, u32[]{:S(2)}) %collective-permute-start.28) | collective-permute-done | bytes 221216 | tf_op jit(solution)/shard_map/ppermute | solution.py:21
  283.8 1.9 collective-permute-start.29
  285.8 5.2 %collective-permute-done.29 = bf16[144,256]{1,0:T(8,128)(2,1)S(1)} collective-permute-done((bf16[144,256]{1,0:T(8,128)(2,1)S(1)}, bf16[144,256]{1,0:T(8,128)(2,1)S(1)}, u32[]{:S(2)}, u32[]{:S(2)}) %collective-permute-start.29) | collective-permute-done | bytes 73760 | tf_op jit(solution)/shard_map/ppermute | solution.py:307
  291.7 2.0 convert_reduce_fusion
  293.8 1.3 collective-permute-start.31
  295.7 2.2 collective-permute-start.33
  298.5 3.7 %collective-permute-done.33 = bf16[32,256]{1,0:T(8,128)(2,1)S(1)} collective-permute-done((bf16[32,256]{1,0:T(8,128)(2,1)S(1)}, bf16[32,256]{1,0:T(8,128)(2,1)S(1)}, u32[]{:S(2)}, u32[]{:S(2)}) %collective-permute-start.33) | collective-permute-done | bytes 16416 | tf_op jit(solution)/shard_map/ppermute | solution.py:350
  (228 shorter events, 24.4 us)
Async XLA Ops:
  7.2 18.5 %copy-start.42 = (s32[1,256]{1,0:T(1,128)S(1)}, s32[1,256]{1,0:T(1,128)}, u32[]{:S(2)}) copy-start(s32[1,256]{1,0:T(1,128)} %param.11) | copy-start | bytes 3076
  7.2 18.5 %copy-start.40 = (bf16[2,256]{1,0:T(2,128)(2,1)S(1)}, bf16[2,256]{1,0:T(2,128)(2,1)}, u32[]{:S(2)}) copy-start(bf16[2,256]{1,0:T(2,128)(2,1)} %param.18) | copy-start | bytes 3076
  7.2 18.5 %copy-start.37 = (bf16[32,768]{1,0:T(8,128)(2,1)S(1)}, bf16[32,768]{1,0:T(8,128)(2,1)}, u32[]{:S(2)}) copy-start(bf16[32,768]{1,0:T(8,128)(2,1)} %param.12) | copy-start | bytes 147460
  7.2 119.7 %all-gather.2.cloned.1.call-start = ((), (), s32[]{:S(2)}) async-start(), calls=%async_computation.3 | async-start | bytes 7520256 | tf_op jit(solution)/shard_map/all_gather | solution.py:277
  8.1 12.0 %collective-permute-start.6 = (bf16[176,256]{1,0:T(8,128)(2,1)S(1)}, bf16[176,256]{1,0:T(8,128)(2,1)S(1)}, u32[]{:S(2)}, u32[]{:S(2)}) collective-permute-start(bf16[176,256]{1,0:T(8,128)(2,1)S(1)} %pad_maximum_fusion.7), channel_id=1, source_target_pairs={{0,0},{1,32},{2,64},{3,96},{4,4},{5,36},{6,68},{7,100},{8,8},{9,40... | collective-permute-start | bytes 270344 | tf_op jit(solution)/shard_map/ppermute | solution.py:274
  10.7 9.5 %collective-permute-start.17 = (bf16[144,256]{1,0:T(8,128)(2,1)}, bf16[144,256]{1,0:T(8,128)(2,1)S(1)}, u32[]{:S(2)}, u32[]{:S(2)}) collective-permute-start(bf16[144,256]{1,0:T(8,128)(2,1)} %param.16), channel_id=1, source_target_pairs={{0,64},{1,96},{2,0},{3,32},{4,68},{5,100},{6,4},{7,36},{8,72},{9,1... | collective-permute-start | bytes 221192 | tf_op jit(solution)/shard_map/ppermute | solution.py:275
  18.0 6.7 %collective-permute-start.16 = (bf16[288,256]{1,0:T(8,128)(2,1)S(1)}, bf16[288,256]{1,0:T(8,128)(2,1)S(1)}, u32[]{:S(2)}, u32[]{:S(2)}) collective-permute-start(bf16[288,256]{1,0:T(8,128)(2,1)S(1)} %shard_map.169), channel_id=1, source_target_pairs={{0,64},{64,0},{1,65},{65,1},{2,66},{66,2},{3,67},{67,3},{4,68},{68... | collective-permute-start | bytes 442376 | tf_op jit(solution)/shard_map/ppermute | solution.py:21
  25.8 2.7 collective-permute-start
  25.9 5.2 %collective-permute-start.1 = (bf16[1,48,768]{2,1,0:T(8,128)(2,1)S(1)}, bf16[1,48,768]{2,1,0:T(8,128)(2,1)S(1)}, u32[]{:S(2)}, u32[]{:S(2)}) collective-permute-start(bf16[1,48,768]{2,1,0:T(8,128)(2,1)S(1)} %maximum_bitcast_fusion), channel_id=1, source_target_pairs={{0,2},{2,0},{1,3},{3,1},{4,6},{6,4},{5,7},{7,5},{8,10},{10,8},{9,1... | collective-permute-start | bytes 221192 | tf_op jit(solution)/shard_map/ppermute | solution.py:21
  26.0 5.7 %collective-permute-start.2 = (bf16[1,48,768]{2,1,0:T(8,128)(2,1)S(1)}, bf16[1,48,768]{2,1,0:T(8,128)(2,1)S(1)}, u32[]{:S(2)}, u32[]{:S(2)}) collective-permute-start(bf16[1,48,768]{2,1,0:T(8,128)(2,1)S(1)} %maximum_bitcast_fusion), channel_id=1, source_target_pairs={{0,3},{1,2},{2,1},{3,0},{4,7},{5,6},{6,5},{7,4},{8,11},{9,10},{10,... | collective-permute-start | bytes 221192 | tf_op jit(solution)/shard_map/ppermute | solution.py:31
  27.8 16.2 %copy-start.33 = (bf16[256,1024]{1,0:T(8,128)(2,1)}, bf16[256,1024]{1,0:T(8,128)(2,1)S(1)}, u32[]{:S(2)}) copy-start(bf16[256,1024]{1,0:T(8,128)(2,1)S(1)} %bitcast_convert_fusion.refs_4_) | copy-start | bytes 1572868
  27.8 16.2 %collective-permute-start.8 = (bf16[256,1024]{1,0:T(8,128)(2,1)S(1)}, bf16[256,1024]{1,0:T(8,128)(2,1)}, u32[]{:S(2)}, u32[]{:S(2)}) collective-permute-start(bf16[256,1024]{1,0:T(8,128)(2,1)S(1)} %bitcast_convert_fusion.refs_4_), channel_id=1, source_target_pairs={{0,2},{2,0},{1,3},{3,1},{4,6},{6,4},{5,7},{7,5},{8,10},{10,8},{9,1... | collective-permute-start | bytes 1572872 | tf_op jit(solution)/shard_map/ppermute | solution.py:21
  33.4 46.1 %all-to-all-start = ((bf16[32,128,256]{2,1,0:T(8,128)(2,1)}), bf16[32,128,256]{2,1,0:T(8,128)(2,1)}, u32[]{:S(2)}, u32[]{:S(2)}) async-start(bf16[32,128,256]{2,1,0:T(8,128)(2,1)} %broadcast_in_dim.27), calls=%async_computation | async-start | bytes 4194304 | tf_op jit(solution)/shard_map/all_to_all | solution.py:280
  42.8 232.1 %reduce-scatter.2.cloned.1.call-start = ((), (), s32[]{:S(2)}) async-start(), calls=%async_computation.4 | async-start | bytes 7520256 | tf_op jit(solution)/shard_map/reduce_scatter | solution.py:304
  43.1 41.3 %copy-start.27 = (bf16[256,1024]{1,0:T(8,128)(2,1)}, bf16[256,1024]{1,0:T(8,128)(2,1)S(1)}, u32[]{:S(2)}) copy-start(bf16[256,1024]{1,0:T(8,128)(2,1)S(1)} %multiply_convert_fusion.1) | copy-start | bytes 1572868
  43.1 35.5 %collective-permute-start.4 = (bf16[256,1024]{1,0:T(8,128)(2,1)S(1)}, bf16[256,1024]{1,0:T(8,128)(2,1)S(1)}, u32[]{:S(2)}, u32[]{:S(2)}) collective-permute-start(bf16[256,1024]{1,0:T(8,128)(2,1)S(1)} %multiply_convert_fusion.1), channel_id=1, source_target_pairs={{0,2},{2,0},{1,3},{3,1},{4,6},{6,4},{5,7},{7,5},{8,10},{10,8},{9,1... | collective-permute-start | bytes 1572872 | tf_op jit(solution)/shard_map/ppermute | solution.py:21
  44.1 34.6 %collective-permute-start.7 = (bf16[256,1024]{1,0:T(8,128)(2,1)S(1)}, bf16[256,1024]{1,0:T(8,128)(2,1)S(1)}, u32[]{:S(2)}, u32[]{:S(2)}) collective-permute-start(bf16[256,1024]{1,0:T(8,128)(2,1)S(1)} %bitcast_convert_fusion.refs_4_), channel_id=1, source_target_pairs={{0,1},{1,0},{2,3},{3,2},{4,5},{5,4},{6,7},{7,6},{8,9},{9,8},{10,11... | collective-permute-start | bytes 1572872 | tf_op jit(solution)/shard_map/ppermute | solution.py:21
  44.1 35.4 %collective-permute-start.9 = (bf16[256,1024]{1,0:T(8,128)(2,1)}, bf16[256,1024]{1,0:T(8,128)(2,1)}, u32[]{:S(2)}, u32[]{:S(2)}) collective-permute-start(bf16[256,1024]{1,0:T(8,128)(2,1)} %collective-permute-done.8.refs_6_), channel_id=1, source_target_pairs={{0,1},{1,0},{2,3},{3,2},{4,5},{5,4},{6,7},{7,6},{8,9},{9,8},{10,11... | collective-permute-start | bytes 1572872 | tf_op jit(solution)/shard_map/ppermute | solution.py:21
  44.6 36.5 %collective-permute-start.3 = (bf16[256,1024]{1,0:T(8,128)(2,1)S(1)}, bf16[256,1024]{1,0:T(8,128)(2,1)S(1)}, u32[]{:S(2)}, u32[]{:S(2)}) collective-permute-start(bf16[256,1024]{1,0:T(8,128)(2,1)S(1)} %multiply_convert_fusion.1), channel_id=1, source_target_pairs={{0,1},{1,0},{2,3},{3,2},{4,5},{5,4},{6,7},{7,6},{8,9},{9,8},{10,11... | collective-permute-start | bytes 1572872 | tf_op jit(solution)/shard_map/ppermute | solution.py:21
  78.6 2.5 collective-permute-start.5
  84.6 6.8 %collective-permute-start.10 = (bf16[4,2,256]{2,1,0:T(2,128)(2,1)S(1)}, bf16[4,2,256]{2,1,0:T(2,128)(2,1)S(1)}, u32[]{:S(2)}, u32[]{:S(2)}) collective-permute-start(bf16[4,2,256]{2,1,0:T(2,128)(2,1)S(1)} %slice.361), channel_id=1, source_target_pairs={{0,4},{4,8},{8,12},{12,16},{16,20},{20,24},{24,28},{28,32},{32,36}... | collective-permute-start | bytes 12296 | tf_op jit(solution)/shard_map/ppermute | solution.py:293
  93.8 2.7 collective-permute-start.11
  97.0 14.0 %collective-permute-start.12 = (bf16[256,1024]{1,0:T(8,128)(2,1)S(1)}, bf16[256,1024]{1,0:T(8,128)(2,1)S(1)}, u32[]{:S(2)}, u32[]{:S(2)}) collective-permute-start(bf16[256,1024]{1,0:T(8,128)(2,1)S(1)} %fusion.20), channel_id=1, source_target_pairs={{0,2},{2,0},{1,3},{3,1},{4,6},{6,4},{5,7},{7,5},{8,10},{10,8},{9,1... | collective-permute-start | bytes 1572872 | tf_op jit(solution)/shard_map/ppermute | solution.py:21
  111.4 69.6 %copy-start.5 = (f32[256,1024]{1,0:T(8,128)}, f32[256,1024]{1,0:T(8,128)S(1)}, u32[]{:S(2)}) copy-start(f32[256,1024]{1,0:T(8,128)S(1)} %get-tuple-element.39) | copy-start | bytes 3145732
  111.6 13.3 %collective-permute-start.14 = (bf16[256,1024]{1,0:T(8,128)(2,1)S(1)}, bf16[256,1024]{1,0:T(8,128)(2,1)S(1)}, u32[]{:S(2)}, u32[]{:S(2)}) collective-permute-start(bf16[256,1024]{1,0:T(8,128)(2,1)S(1)} %multiply_convert_fusion.refs_0_), channel_id=1, source_target_pairs={{0,2},{2,0},{1,3},{3,1},{4,6},{6,4},{5,7},{7,5},{8,10},{10,8},{9,1... | collective-permute-start | bytes 1572872 | tf_op jit(solution)/shard_map/ppermute | solution.py:21
  111.9 13.0 %collective-permute-start.13 = (bf16[256,1024]{1,0:T(8,128)(2,1)S(1)}, bf16[256,1024]{1,0:T(8,128)(2,1)S(1)}, u32[]{:S(2)}, u32[]{:S(2)}) collective-permute-start(bf16[256,1024]{1,0:T(8,128)(2,1)S(1)} %multiply_convert_fusion.refs_0_), channel_id=1, source_target_pairs={{0,1},{1,0},{2,3},{3,2},{4,5},{5,4},{6,7},{7,6},{8,9},{9,8},{10,11... | collective-permute-start | bytes 1572872 | tf_op jit(solution)/shard_map/ppermute | solution.py:21
  124.9 2.0 collective-permute-start.15
  163.3 2.7 collective-permute-start.19
  166.4 14.0 %collective-permute-start.20 = (bf16[256,1024]{1,0:T(8,128)(2,1)S(1)}, bf16[256,1024]{1,0:T(8,128)(2,1)S(1)}, u32[]{:S(2)}, u32[]{:S(2)}) collective-permute-start(bf16[256,1024]{1,0:T(8,128)(2,1)S(1)} %fusion.22), channel_id=1, source_target_pairs={{0,2},{2,0},{1,3},{3,1},{4,6},{6,4},{5,7},{7,5},{8,10},{10,8},{9,1... | collective-permute-start | bytes 1572872 | tf_op jit(solution)/shard_map/ppermute | solution.py:21
  182.3 13.2 %collective-permute-start.22 = (bf16[256,1024]{1,0:T(8,128)(2,1)S(1)}, bf16[256,1024]{1,0:T(8,128)(2,1)S(1)}, u32[]{:S(2)}, u32[]{:S(2)}) collective-permute-start(bf16[256,1024]{1,0:T(8,128)(2,1)S(1)} %get-tuple-element.35), channel_id=1, source_target_pairs={{0,2},{2,0},{1,3},{3,1},{4,6},{6,4},{5,7},{7,5},{8,10},{10,8},{9,1... | collective-permute-start | bytes 1572872 | tf_op jit(solution)/shard_map/ppermute | solution.py:21
  184.3 14.9 %collective-permute-start.21 = (bf16[256,1024]{1,0:T(8,128)(2,1)S(1)}, bf16[256,1024]{1,0:T(8,128)(2,1)S(1)}, u32[]{:S(2)}, u32[]{:S(2)}) collective-permute-start(bf16[256,1024]{1,0:T(8,128)(2,1)S(1)} %get-tuple-element.35), channel_id=1, source_target_pairs={{0,1},{1,0},{2,3},{3,2},{4,5},{5,4},{6,7},{7,6},{8,9},{9,8},{10,11... | collective-permute-start | bytes 1572872 | tf_op jit(solution)/shard_map/ppermute | solution.py:21
  195.6 3.6 %collective-permute-start.23 = (bf16[256,1024]{1,0:T(8,128)(2,1)S(1)}, bf16[256,1024]{1,0:T(8,128)(2,1)S(1)}, u32[]{:S(2)}, u32[]{:S(2)}) collective-permute-start(bf16[256,1024]{1,0:T(8,128)(2,1)S(1)} %collective-permute-done.22), channel_id=1, source_target_pairs={{0,1},{1,0},{2,3},{3,2},{4,5},{5,4},{6,7},{7,6},{8,9},{9,8},{10,11... | collective-permute-start | bytes 1572872 | tf_op jit(solution)/shard_map/ppermute | solution.py:21
  198.8 20.8 %collective-permute-start.18 = (bf16[2,256,1024]{2,1,0:T(8,128)(2,1)S(1)}, bf16[2,256,1024]{2,1,0:T(8,128)(2,1)S(1)}, u32[]{:S(2)}, u32[]{:S(2)}) collective-permute-start(bf16[2,256,1024]{2,1,0:T(8,128)(2,1)S(1)} %copy-done.43), channel_id=1, source_target_pairs={{0,1},{1,0},{2,3},{3,2},{4,5},{5,4},{6,7},{7,6},{8,9},{9,8},{10,11... | collective-permute-start | bytes 3145736 | tf_op jit(solution)/shard_map/ppermute | solution.py:21
  201.6 11.6 %collective-permute-start.25 = (f32[4,3,256]{2,1,0:T(4,128)S(1)}, f32[4,3,256]{2,1,0:T(4,128)S(1)}, u32[]{:S(2)}, u32[]{:S(2)}) collective-permute-start(f32[4,3,256]{2,1,0:T(4,128)S(1)} %pad_maximum_fusion.11), channel_id=1, source_target_pairs={{4,0},{8,4},{12,8},{16,12},{20,16},{24,20},{28,24},{32,28},{36,32}... | collective-permute-start | bytes 36872 | tf_op jit(solution)/shard_map/ppermute | solution.py:321
  219.5 4.6 %collective-permute-start.26 = (bf16[2,256,1024]{2,1,0:T(8,128)(2,1)S(1)}, bf16[2,256,1024]{2,1,0:T(8,128)(2,1)S(1)}, u32[]{:S(2)}, u32[]{:S(2)}) collective-permute-start(bf16[2,256,1024]{2,1,0:T(8,128)(2,1)S(1)} %get-tuple-element.27), channel_id=1, source_target_pairs={{0,1},{1,0},{2,3},{3,2},{4,5},{5,4},{6,7},{7,6},{8,9},{9,8},{10,11... | collective-permute-start | bytes 3145736 | tf_op jit(solution)/shard_map/ppermute | solution.py:21
  223.6 20.2 %collective-permute-start.24 = (bf16[256,1024]{1,0:T(8,128)(2,1)}, bf16[256,1024]{1,0:T(8,128)(2,1)}, u32[]{:S(2)}, u32[]{:S(2)}) collective-permute-start(bf16[256,1024]{1,0:T(8,128)(2,1)} %fusion.21), channel_id=1, source_target_pairs={{0,2},{2,0},{1,3},{3,1},{4,6},{6,4},{5,7},{7,5},{8,10},{10,8},{9,1... | collective-permute-start | bytes 1572872 | tf_op jit(solution)/shard_map/ppermute | solution.py:21
  226.6 46.8 %collective-permute-start.27 = (bf16[256,1024]{1,0:T(8,128)(2,1)}, bf16[256,1024]{1,0:T(8,128)(2,1)}, u32[]{:S(2)}, u32[]{:S(2)}) collective-permute-start(bf16[256,1024]{1,0:T(8,128)(2,1)} %fusion.23), channel_id=1, source_target_pairs={{0,2},{2,0},{1,3},{3,1},{4,6},{6,4},{5,7},{7,5},{8,10},{10,8},{9,1... | collective-permute-start | bytes 1572872 | tf_op jit(solution)/shard_map/ppermute | solution.py:21
  228.1 63.5 %all-to-all-start.1 = ((bf16[32,144,256]{2,1,0:T(8,128)(2,1)}), bf16[32,144,256]{2,1,0:T(8,128)(2,1)}, u32[]{:S(2)}, u32[]{:S(2)}) async-start(bf16[32,144,256]{2,1,0:T(8,128)(2,1)} %copy-done), calls=%async_computation.1 | async-start | bytes 4718592 | tf_op jit(solution)/shard_map/all_to_all | solution.py:338
  235.1 38.3 %copy-start.8 = (f32[1,256,1024]{2,1,0:T(8,128)S(1)}, f32[1,256,1024]{2,1,0:T(8,128)}, u32[]{:S(2)}) copy-start(f32[1,256,1024]{2,1,0:T(8,128)} %param.10) | copy-start | bytes 3145732
  235.1 38.3 %copy-start.11 = (f32[2,256,1024]{2,1,0:T(8,128)S(1)}, f32[2,256,1024]{2,1,0:T(8,128)}, u32[]{:S(2)}) copy-start(f32[2,256,1024]{2,1,0:T(8,128)} %copy-done.10) | copy-start | bytes 6291460
  246.9 29.4 %copy-start.9 = (f32[1,256,1024]{2,1,0:T(8,128)S(1)}, f32[1,256,1024]{2,1,0:T(8,128)}, u32[]{:S(2)}) copy-start(f32[1,256,1024]{2,1,0:T(8,128)} %param.10) | copy-start | bytes 3145732
  276.2 7.5 %collective-permute-start.28 = (bf16[432,256]{1,0:T(8,128)(2,1)S(1)}, bf16[432,256]{1,0:T(8,128)(2,1)S(1)}, u32[]{:S(2)}, u32[]{:S(2)}) collective-permute-start(bf16[432,256]{1,0:T(8,128)(2,1)S(1)} %slice_bitcast_fusion.1), channel_id=1, source_target_pairs={{0,64},{64,0},{1,65},{65,1},{2,66},{66,2},{3,67},{67,3},{4,68},{68... | collective-permute-start | bytes 663560 | tf_op jit(solution)/shard_map/ppermute | solution.py:21
  283.8 7.2 %collective-permute-start.29 = (bf16[144,256]{1,0:T(8,128)(2,1)S(1)}, bf16[144,256]{1,0:T(8,128)(2,1)S(1)}, u32[]{:S(2)}, u32[]{:S(2)}) collective-permute-start(bf16[144,256]{1,0:T(8,128)(2,1)S(1)} %slice.543), channel_id=1, source_target_pairs={{0,0},{32,1},{64,2},{96,3},{4,4},{36,5},{68,6},{100,7},{8,8},{40,9... | collective-permute-start | bytes 221192 | tf_op jit(solution)/shard_map/ppermute | solution.py:307
  285.8 18.4 %copy-start.41 = (f32[32,1152]{1,0:T(8,128)}, f32[32,1152]{1,0:T(8,128)S(1)}, u32[]{:S(2)}) copy-start(f32[32,1152]{1,0:T(8,128)S(1)} %get-tuple-element.49) | copy-start | bytes 442372
  293.7 9.2 %collective-permute-start.30 = (bf16[1,144,256]{2,1,0:T(8,128)(2,1)S(1)}, bf16[1,144,256]{2,1,0:T(8,128)(2,1)S(1)}, u32[]{:S(2)}, u32[]{:S(2)}) collective-permute-start(bf16[1,144,256]{2,1,0:T(8,128)(2,1)S(1)} %convert_bitcast_fusion), channel_id=1, source_target_pairs={{0,1},{1,0},{2,3},{3,2},{4,5},{5,4},{6,7},{7,6},{8,9},{9,8},{10,11... | collective-permute-start | bytes 221192 | tf_op jit(solution)/shard_map/ppermute | solution.py:21
  293.8 9.1 %collective-permute-start.31 = (bf16[1,144,256]{2,1,0:T(8,128)(2,1)S(1)}, bf16[1,144,256]{2,1,0:T(8,128)(2,1)S(1)}, u32[]{:S(2)}, u32[]{:S(2)}) collective-permute-start(bf16[1,144,256]{2,1,0:T(8,128)(2,1)S(1)} %convert_bitcast_fusion), channel_id=1, source_target_pairs={{0,2},{2,0},{1,3},{3,1},{4,6},{6,4},{5,7},{7,5},{8,10},{10,8},{9,1... | collective-permute-start | bytes 221192 | tf_op jit(solution)/shard_map/ppermute | solution.py:21
  295.0 7.8 %collective-permute-start.32 = (bf16[1,144,256]{2,1,0:T(8,128)(2,1)S(1)}, bf16[1,144,256]{2,1,0:T(8,128)(2,1)S(1)}, u32[]{:S(2)}, u32[]{:S(2)}) collective-permute-start(bf16[1,144,256]{2,1,0:T(8,128)(2,1)S(1)} %convert_bitcast_fusion), channel_id=1, source_target_pairs={{0,3},{1,2},{2,1},{3,0},{4,7},{5,6},{6,5},{7,4},{8,11},{9,10},{10,... | collective-permute-start | bytes 221192 | tf_op jit(solution)/shard_map/ppermute | solution.py:31
  295.7 6.6 %collective-permute-start.33 = (bf16[32,256]{1,0:T(8,128)(2,1)S(1)}, bf16[32,256]{1,0:T(8,128)(2,1)S(1)}, u32[]{:S(2)}, u32[]{:S(2)}) collective-permute-start(bf16[32,256]{1,0:T(8,128)(2,1)S(1)} %slice.390), channel_id=1, source_target_pairs={{0,0},{32,1},{64,2},{96,3},{4,4},{36,5},{68,6},{100,7},{8,8},{40,9... | collective-permute-start | bytes 49160 | tf_op jit(solution)/shard_map/ppermute | solution.py:350
  (38 other events, 193.2 us)
Sparse Core Ops, SparseCore 0:
  25.7 85.8 all-gather.1
  162.3 105.2 reduce-scatter.1

commit v2 on v1

--- a/solution.py
+++ b/solution.py
@@ -64,7 +64,6 @@
 
 ROW_ROUTE = [(s * 4 + f, (f * 8 + s % 8) * 4 + s // 8) for s in range(32) for f in range(4)]
 ROW_BACK = [(b, a) for a, b in ROW_ROUTE]
-ROW_OTHER = [(a, (b + 64) % 128) for a, b in ROW_ROUTE]
 
 
 def in_zh_order(mine, other):
@@ -254,7 +253,6 @@
     grad_result = cotangent[0]
     rows, model = inputs.shape
     f_index = lax.axis_index(FSDP)
-    grad_low_all = group_blocks(grad_result.astype(BF16))
 
     line = jnp.concatenate([norm_gains[:1], norm_gains[1:], jnp.minimum(token_pos, 2).astype(BF16)], axis=1)
     start = gather_group(jnp.concatenate([w_in, line, jnp.zeros((15, 768), BF16)], axis=0)[None])
@@ -269,19 +267,19 @@
     mask_two = (positions >= 2).astype(F32)[:, :, None]
     conv_taps = conv_weight.astype(F32)
 
-    gu_own = pack_columns(w_gate, w_up)
-    gu_far = swap(gu_own, "zh")
     row_blocks = lax.ppermute(jnp.concatenate([w_mix, w_down], axis=0), ALL, ROW_ROUTE)
-    down_far = lax.ppermute(w_down, ALL, ROW_OTHER)
-    second_pack = jnp.concatenate([in_zh_order(gu_own, gu_far), in_zh_order(row_blocks[32:], down_far)], axis=1)
-    second_all = lax.all_gather(second_pack.reshape(864, 256), YX, axis=0, tiled=True).reshape(16, 2, 432, 256)
-
-    first_pack = jnp.concatenate([*in_blocks, row_blocks[:32]], axis=0)
-    first_all = lax.all_to_all(jnp.broadcast_to(first_pack, (32, 128, 256)), SEQ, 0, 0, tiled=True).reshape(32, 128, 256)
+    own = jnp.concatenate([pack_columns(w_gate, w_up), row_blocks[32:], *in_blocks, row_blocks[:32]], axis=0)
+    both = in_zh_order(own, swap(own, "zh"))
+    first_copies = jnp.broadcast_to(both[:, 432:], (16, 2, 128, 256))
+    first_all = lax.all_to_all(first_copies, YX, 0, 0, tiled=True)
+    second_all = lax.all_gather(both[:, :432].reshape(864, 256), YX, axis=0, tiled=True).reshape(16, 2, 432, 256)
     grad_low_all = group_blocks(grad_result.astype(BF16))
     first_all = after(first_all, *grad_low_all)
-    w_in_f = jnp.concatenate([first_all[:, 32 * i : 32 * (i + 1)].reshape(1024, 256) for i in range(3)], axis=1)
-    w_mix_f = jnp.concatenate([first_all[8 * i : 8 * (i + 1), 96:].reshape(256, 256) for i in range(4)], axis=1)
+    in_rows = first_all.transpose(1, 0, 2, 3)
+    w_in_f = jnp.concatenate([in_rows[:, :, 32 * i : 32 * (i + 1)].reshape(1024, 256) for i in range(3)], axis=1)
+    w_mix_f = jnp.concatenate(
+        [in_rows[i // 2, i % 2 * 8 : i % 2 * 8 + 8, 96:].reshape(256, 256) for i in range(4)], axis=1
+    )
 
     normed1, inv_one, hidden1 = norm_forward(inputs, gain_rows[0])
     hidden1_blocks = group_blocks(hidden1)
@@ -320,7 +318,7 @@
     later = jnp.concatenate([edge[:, :1] * mask_one[:, :1], edge * mask_two[:, :2]], axis=1)
     later = lax.ppermute(later, SEQ, [(i + 1, i) for i in range(31)])
     first_back, keep, send = mix_back(
-        grad_mixer,
+        after(grad_mixer, out_far),
         grad_mix,
         mixed,
         conv_val,

time: 312 us -> 307 us (0.984)
  waiting for transfers between devices: 157 us -> 131 us
  starting transfers between devices: 48.9 us -> 68.5 us
  other arithmetic: 24.4 us -> 29.3 us
    ppermute x26, waiting for transfers between devices: 139 us -> 85.8 us  [swap(): return lax.ppermute(x, axis, [(0, 1), (1, 0)])]
    ppermute x26, starting transfers between devices: 10.3 us -> 33.1 us  [swap(): return lax.ppermute(x, axis, [(0, 1), (1, 0)])]
    all_to_all x1, waiting for transfers between devices: 0.01 us -> 18.2 us  [local(): first_all = lax.all_to_all(first_copies, YX, 0, 0, tiled=True)]
    reduce_scatter x1, waiting for transfers between devices: 0.02 us -> 13.6 us  [local(): lax.psum_scatter(back_pack.reshape(16 * 864, 256), YX, scatter_dimension=...]
    ppermute x1, waiting for transfers between devices: 8.73 us -> 1.42 us  [local(): later = lax.ppermute(later, SEQ, [(i + 1, i) for i in range(31)])]
    ppermute x1 -> x0, starting transfers between devices: 5.5 us -> none  [local(): down_far = lax.ppermute(w_down, ALL, ROW_OTHER)]
    unnamed x106 -> x103, local copies, waits for them, and re-layouts: 10.4 us -> 5.76 us
    all_to_all x1, starting transfers between devices: 6.96 us -> 11 us  [local(): lax.all_to_all(first_back, SEQ, 0, 0, tiled=True).reshape(32, 144, 256)]
  transfers between devices with their start and end apart: 38 -> 37, of which waited for: 18 -> 20; matrix products, arithmetic and copies ran while one was open for 11% -> 12% of each run, Pallas kernels for 2% -> 2%
where the time goes in v2:
time: 307 us; the launch traced here: 304 us
  waiting for transfers between devices  131 us (43%)
  starting transfers between devices  68.5 us (22%)
  Pallas kernels  41.3 us (13%)
  other arithmetic  29.3 us (10%)
  local copies, waits for them, and re-layouts  15.4 us (5%)
  between operations  15.3 us (5%)
  matrix products  3.99 us (1%)
    ppermute x26, waiting for transfers between devices, swap(): return lax.ppermute(x, axis, [(0, 1), (1, 0)])  85.8 us
    pallas_call x1, Pallas kernels, ffn(): pl.pallas_call(functools.partial(ffn_kernel, rows_t), grid=(3,), in_specs...  35.1 us
    ppermute x26, starting transfers between devices, swap(): return lax.ppermute(x, axis, [(0, 1), (1, 0)])  33.1 us
    all_to_all x1, waiting for transfers between devices, local(): first_all = lax.all_to_all(first_copies, YX, 0, 0, tiled=True)  18.2 us
    reduce_scatter x1, waiting for transfers between devices, local(): lax.psum_scatter(back_pack.reshape(16 * 864, 256), YX, scatter_dimension=...  13.6 us
    all_to_all x1, starting transfers between devices, local(): lax.all_to_all(first_back, SEQ, 0, 0, tiled=True).reshape(32, 144, 256)  11 us
    ppermute x1, starting transfers between devices, local(): lax.ppermute(product_bx[:, -2:], SEQ, [(i, i + 1) for i in range(31)])  8.01 us
    all_to_all x1, starting transfers between devices, local(): first_all = lax.all_to_all(first_copies, YX, 0, 0, tiled=True)  7.22 us
  transfers between devices with their start and end apart: 37, of which 20 were waited for; matrix products, arithmetic and copies ran while one was open for 12% of the time, Pallas kernels for 2%

profile of v2, /device:TPU:30, one launch (start us, length us, event | category | flops | bytes accessed | tf_op | source)
XLA Modules:
  0.0 304.3 jit_solution(13202225972643768455)
XLA Ops:
  9.7 2.0 collective-permute-start.1
  12.7 2.9 collective-permute-start.6
  17.6 2.4 collective-permute-done.6
  20.1 4.7 %collective-permute-start.7 = (bf16[560,256]{1,0:T(8,128)(2,1)S(1)}, bf16[560,256]{1,0:T(8,128)(2,1)S(1)}, u32[]{:S(2)}, u32[]{:S(2)}) collective-permute-start(bf16[560,256]{1,0:T(8,128)(2,1)S(1)} %constant_dynamic-update-slice_fusion), channel_id=1, source_target_pairs={{0,64},{64,0},{1,65},{65,1},{2,66},{66,2},{3,67},{67,3},{4,68},{68... | collective-permute-start | bytes 860168 | tf_op jit(solution)/shard_map/ppermute | solution.py:21
  24.7 4.6 %collective-permute-done.7 = bf16[560,256]{1,0:T(8,128)(2,1)S(1)} collective-permute-done((bf16[560,256]{1,0:T(8,128)(2,1)S(1)}, bf16[560,256]{1,0:T(8,128)(2,1)S(1)}, u32[]{:S(2)}, u32[]{:S(2)}) %collective-permute-start.7) | collective-permute-done | bytes 286752 | tf_op jit(solution)/shard_map/ppermute | solution.py:21
  32.9 1.6 collective-permute-start.9
  34.7 1.6 broadcast_in_dim.27
  36.3 7.2 %all-to-all-start = ((bf16[16,2,128,256]{3,2,1,0:T(8,128)(2,1)}), bf16[16,2,128,256]{3,2,1,0:T(8,128)(2,1)}, u32[]{:S(2)}, u32[]{:S(2)}) async-start(bf16[16,2,128,256]{3,2,1,0:T(8,128)(2,1)} %broadcast_in_dim.27), calls=%async_computation | async-start | bytes 4194304 | tf_op jit(solution)/shard_map/all_to_all | solution.py:274
  45.0 11.4 %collective-permute-done.4 = bf16[256,1024]{1,0:T(8,128)(2,1)S(1)} collective-permute-done((bf16[256,1024]{1,0:T(8,128)(2,1)S(1)}, bf16[256,1024]{1,0:T(8,128)(2,1)S(1)}, u32[]{:S(2)}, u32[]{:S(2)}) %collective-permute-start.4) | collective-permute-done | bytes 524320 | tf_op jit(solution)/shard_map/ppermute | solution.py:21
  56.4 18.2 %all-to-all-done = bf16[16,2,128,256]{3,2,1,0:T(8,128)(2,1)} async-done(((bf16[16,2,128,256]{3,2,1,0:T(8,128)(2,1)}), bf16[16,2,128,256]{3,2,1,0:T(8,128)(2,1)}, u32[]{:S(2)}, u32[]{:S(2)}) %all-to-all-start) | async-done | bytes 2097184 | tf_op jit(solution)/shard_map/all_to_all | solution.py:274
  74.6 1.5 fusion.36
  76.3 1.8 fusion.30
  78.3 8.0 %collective-permute-start.11 = (bf16[4,2,256]{2,1,0:T(2,128)(2,1)S(1)}, bf16[4,2,256]{2,1,0:T(2,128)(2,1)S(1)}, u32[]{:S(2)}, u32[]{:S(2)}) collective-permute-start(bf16[4,2,256]{2,1,0:T(2,128)(2,1)S(1)} %slice.374), channel_id=1, source_target_pairs={{0,4},{4,8},{8,12},{12,16},{16,20},{20,24},{24,28},{28,32},{32,36}... | collective-permute-start | bytes 12296 | tf_op jit(solution)/shard_map/ppermute | solution.py:291
  87.7 1.5 fusion.18
  90.4 2.4 collective-permute-done.12
  93.3 1.7 collective-permute-start.13
  95.0 12.3 %collective-permute-done.13 = bf16[256,1024]{1,0:T(8,128)(2,1)S(1)} collective-permute-done((bf16[256,1024]{1,0:T(8,128)(2,1)S(1)}, bf16[256,1024]{1,0:T(8,128)(2,1)S(1)}, u32[]{:S(2)}, u32[]{:S(2)}) %collective-permute-start.13) | collective-permute-done | bytes 524320 | tf_op jit(solution)/shard_map/ppermute | solution.py:21
  107.9 1.7 collective-permute-start.15
  109.6 11.6 %collective-permute-done.15.refs_2_ = bf16[256,1024]{1,0:T(8,128)(2,1)S(1)} collective-permute-done((bf16[256,1024]{1,0:T(8,128)(2,1)S(1)}, bf16[256,1024]{1,0:T(8,128)(2,1)S(1)}, u32[]{:S(2)}, u32[]{:S(2)}) %collective-permute-start.15) | collective-permute-done | bytes 524320 | tf_op jit(solution)/shard_map/ppermute | solution.py:21
  121.2 2.0 collective-permute-done.16.refs_3_
  123.3 35.1 %shard_map.170 = (f32[2,256,1024]{2,1,0:T(8,128)}, bf16[2,256,1024]{2,1,0:T(8,128)(2,1)}, f32[2,256,1024]{2,1,0:T(8,128)}, bf16[2,256,1024]{2,1,0:T(8,128)(2,1)}, bf16[16,2,432,256]{3,2,1,0:T(8,128)(2,1)}) custom-call(bf16[256,1024]{1,0:T(8,128)(2,1)} %copy-done.33, bf16[256,1024]{1,0:T(8,128)(2,1)} %copy-done.43, bf16[256,1024]{1,0:T(8,128)(2,1)} %copy-done.42, ...), custom_call_target="tpu_custom_call" | custom-call | flops 22000001024 | bytes 30000000 | tf_op jit(solution)/shard_map/pallas_call | solution.py:155
  159.7 2.5 collective-permute-done.18
  162.7 1.7 collective-permute-start.19
  164.4 12.3 %collective-permute-done.19 = bf16[256,1024]{1,0:T(8,128)(2,1)S(1)} collective-permute-done((bf16[256,1024]{1,0:T(8,128)(2,1)S(1)}, bf16[256,1024]{1,0:T(8,128)(2,1)S(1)}, u32[]{:S(2)}, u32[]{:S(2)}) %collective-permute-start.19) | collective-permute-done | bytes 524320 | tf_op jit(solution)/shard_map/ppermute | solution.py:21
  177.2 1.5 fusion.31
  178.7 1.6 collective-permute-start.21
  181.8 10.3 %collective-permute-done.21 = bf16[256,1024]{1,0:T(8,128)(2,1)S(1)} collective-permute-done((bf16[256,1024]{1,0:T(8,128)(2,1)}, bf16[256,1024]{1,0:T(8,128)(2,1)S(1)}, u32[]{:S(2)}, u32[]{:S(2)}) %collective-permute-start.21) | collective-permute-done | bytes 524320 | tf_op jit(solution)/shard_map/ppermute | solution.py:21
  192.2 1.7 pad_maximum_fusion.h_ref
  194.0 1.7 convert_element_type.192
  197.8 1.7 collective-permute-start.23
  201.3 2.1 collective-permute-start.24
  204.2 8.0 %collective-permute-done.23 = bf16[256,1024]{1,0:T(8,128)(2,1)S(1)} collective-permute-done((bf16[256,1024]{1,0:T(8,128)(2,1)S(1)}, bf16[256,1024]{1,0:T(8,128)(2,1)S(1)}, u32[]{:S(2)}, u32[]{:S(2)}) %collective-permute-start.23) | collective-permute-done | bytes 524320 | tf_op jit(solution)/shard_map/ppermute | solution.py:21
  212.2 1.4 collective-permute-done.24.later_ref
  213.6 6.2 %shard_map.171 = (bf16[32,144,256]{2,1,0:T(8,128)(2,1)S(1)}, f32[2,256,1024]{2,1,0:T(8,128)S(1)}, bf16[2,256,1024]{2,1,0:T(8,128)(2,1)S(1)}) custom-call(f32[4,256,256]{2,1,0:T(8,128)S(1)} %bitcast.183, bf16[256,1024]{1,0:T(8,128)(2,1)S(1)} %convolution_convert_fusion.gmix_ref, f32[4,256,768]{2,1,0:T(8,128)} %bitcast.189, f32[4,256,256]{2,1,0:T(8,128)S(1)} %copy-done.1, ...), custom_call_target="tpu_custom_call" | custom-call | flops 4000000000 | bytes 10000000 | tf_op jit(solution)/shard_map/pallas_call | solution.py:220
  220.0 2.6 collective-permute-done.25
  225.5 11.0 %all-to-all-start.1 = ((bf16[32,144,256]{2,1,0:T(8,128)(2,1)}), bf16[32,144,256]{2,1,0:T(8,128)(2,1)}, u32[]{:S(2)}, u32[]{:S(2)}) async-start(bf16[32,144,256]{2,1,0:T(8,128)(2,1)} %copy-done), calls=%async_computation.1 | async-start | bytes 4718592 | tf_op jit(solution)/shard_map/all_to_all | solution.py:336
  236.5 3.2 %fusion.10 = f32[1,256,1024]{2,1,0:T(8,128)} fusion(f32[2,256,1024]{2,1,0:T(8,128)} %copy-done.13, f32[256,1024]{1,0:T(8,128)S(1)} %copy-done.6, bf16[256,1024]{1,0:T(8,128)(2,1)} %copy-done.32, f32[2,256,1024]{2,1,0:T(8,128)} %get-tuple-element.22), kind=kLoop, calls=%fused_computation.21 | loop fusion | flops 1048576 | bytes 4718592 | tf_op jit(solution)/shard_map/broadcast_in_dim | solution.py:358
  239.7 4.5 %collective-permute-done.26 = bf16[256,1024]{1,0:T(8,128)(2,1)} collective-permute-done((bf16[256,1024]{1,0:T(8,128)(2,1)}, bf16[256,1024]{1,0:T(8,128)(2,1)}, u32[]{:S(2)}, u32[]{:S(2)}) %collective-permute-start.26) | collective-permute-done | bytes 524320 | tf_op jit(solution)/shard_map/ppermute | solution.py:21
  244.2 1.4 multiply_reduce_fusion
  245.6 13.6 %reduce-scatter.2.cloned.1.call-done = bf16[864,256]{1,0:T(8,128)(2,1)} async-done(((bf16[13824,256]{1,0:T(8,128)(2,1)}), bf16[864,256]{1,0:T(8,128)(2,1)}) %reduce-scatter.2.cloned.1.call-update) | async-done | bytes 442384 | tf_op jit(solution)/shard_map/reduce_scatter | solution.py:302
  260.6 9.2 %collective-permute-start.27 = (bf16[432,256]{1,0:T(8,128)(2,1)S(1)}, bf16[432,256]{1,0:T(8,128)(2,1)S(1)}, u32[]{:S(2)}, u32[]{:S(2)}) collective-permute-start(bf16[432,256]{1,0:T(8,128)(2,1)S(1)} %slice_bitcast_fusion.1), channel_id=1, source_target_pairs={{0,64},{64,0},{1,65},{65,1},{2,66},{66,2},{3,67},{67,3},{4,68},{68... | collective-permute-start | bytes 663560 | tf_op jit(solution)/shard_map/ppermute | solution.py:21
  269.8 2.7 add_bitcast_fusion
  273.8 2.0 collective-permute-start.28
  276.0 5.0 %collective-permute-done.28 = bf16[144,256]{1,0:T(8,128)(2,1)S(1)} collective-permute-done((bf16[144,256]{1,0:T(8,128)(2,1)S(1)}, bf16[144,256]{1,0:T(8,128)(2,1)S(1)}, u32[]{:S(2)}, u32[]{:S(2)}) %collective-permute-start.28) | collective-permute-done | bytes 73760 | tf_op jit(solution)/shard_map/ppermute | solution.py:305
  281.7 2.0 convert_reduce_fusion
  283.8 5.0 %collective-permute-start.30 = (bf16[1,144,256]{2,1,0:T(8,128)(2,1)S(1)}, bf16[1,144,256]{2,1,0:T(8,128)(2,1)S(1)}, u32[]{:S(2)}, u32[]{:S(2)}) collective-permute-start(bf16[1,144,256]{2,1,0:T(8,128)(2,1)S(1)} %convert_bitcast_fusion), channel_id=1, source_target_pairs={{0,2},{2,0},{1,3},{3,1},{4,6},{6,4},{5,7},{7,5},{8,10},{10,8},{9,1... | collective-permute-start | bytes 221192 | tf_op jit(solution)/shard_map/ppermute | solution.py:21
  288.9 1.9 collective-permute-start.32
  291.5 4.0 %collective-permute-done.32 = bf16[32,256]{1,0:T(8,128)(2,1)S(1)} collective-permute-done((bf16[32,256]{1,0:T(8,128)(2,1)S(1)}, bf16[32,256]{1,0:T(8,128)(2,1)S(1)}, u32[]{:S(2)}, u32[]{:S(2)}) %collective-permute-start.32) | collective-permute-done | bytes 16416 | tf_op jit(solution)/shard_map/ppermute | solution.py:348
  (223 shorter events, 31.8 us)
Async XLA Ops:
  7.2 116.1 %all-gather.2.cloned.1.call-start = ((), (), s32[]{:S(2)}) async-start(), calls=%async_computation.3 | async-start | bytes 7520256 | tf_op jit(solution)/shard_map/all_gather | solution.py:275
  9.6 7.9 %collective-permute-start = (bf16[1,48,768]{2,1,0:T(8,128)(2,1)S(1)}, bf16[1,48,768]{2,1,0:T(8,128)(2,1)S(1)}, u32[]{:S(2)}, u32[]{:S(2)}) collective-permute-start(bf16[1,48,768]{2,1,0:T(8,128)(2,1)S(1)} %maximum_bitcast_fusion), channel_id=1, source_target_pairs={{0,1},{1,0},{2,3},{3,2},{4,5},{5,4},{6,7},{7,6},{8,9},{9,8},{10,11... | collective-permute-start | bytes 221192 | tf_op jit(solution)/shard_map/ppermute | solution.py:21
  9.7 7.8 %collective-permute-start.1 = (bf16[1,48,768]{2,1,0:T(8,128)(2,1)S(1)}, bf16[1,48,768]{2,1,0:T(8,128)(2,1)S(1)}, u32[]{:S(2)}, u32[]{:S(2)}) collective-permute-start(bf16[1,48,768]{2,1,0:T(8,128)(2,1)S(1)} %maximum_bitcast_fusion), channel_id=1, source_target_pairs={{0,2},{2,0},{1,3},{3,1},{4,6},{6,4},{5,7},{7,5},{8,10},{10,8},{9,1... | collective-permute-start | bytes 221192 | tf_op jit(solution)/shard_map/ppermute | solution.py:21
  11.7 5.8 %collective-permute-start.2 = (bf16[1,48,768]{2,1,0:T(8,128)(2,1)S(1)}, bf16[1,48,768]{2,1,0:T(8,128)(2,1)S(1)}, u32[]{:S(2)}, u32[]{:S(2)}) collective-permute-start(bf16[1,48,768]{2,1,0:T(8,128)(2,1)S(1)} %maximum_bitcast_fusion), channel_id=1, source_target_pairs={{0,3},{1,2},{2,1},{3,0},{4,7},{5,6},{6,5},{7,4},{8,11},{9,10},{10,... | collective-permute-start | bytes 221192 | tf_op jit(solution)/shard_map/ppermute | solution.py:31
  12.7 7.3 %collective-permute-start.6 = (bf16[176,256]{1,0:T(8,128)(2,1)S(1)}, bf16[176,256]{1,0:T(8,128)(2,1)S(1)}, u32[]{:S(2)}, u32[]{:S(2)}) collective-permute-start(bf16[176,256]{1,0:T(8,128)(2,1)S(1)} %pad_maximum_fusion.6), channel_id=1, source_target_pairs={{0,0},{1,32},{2,64},{3,96},{4,4},{5,36},{6,68},{7,100},{8,8},{9,40... | collective-permute-start | bytes 270344 | tf_op jit(solution)/shard_map/ppermute | solution.py:270
  17.4 14.6 %copy-start.16 = (f32[1,256,1024]{2,1,0:T(8,128)S(1)}, f32[1,256,1024]{2,1,0:T(8,128)}, u32[]{:S(2)}) copy-start(f32[1,256,1024]{2,1,0:T(8,128)} %param.19) | copy-start | bytes 3145732
  20.0 14.5 %copy-start.7 = (f32[1,256,1024]{2,1,0:T(8,128)S(1)}, f32[1,256,1024]{2,1,0:T(8,128)}, u32[]{:S(2)}) copy-start(f32[1,256,1024]{2,1,0:T(8,128)} %param.10) | copy-start | bytes 3145732
  20.1 9.3 %collective-permute-start.7 = (bf16[560,256]{1,0:T(8,128)(2,1)S(1)}, bf16[560,256]{1,0:T(8,128)(2,1)S(1)}, u32[]{:S(2)}, u32[]{:S(2)}) collective-permute-start(bf16[560,256]{1,0:T(8,128)(2,1)S(1)} %constant_dynamic-update-slice_fusion), channel_id=1, source_target_pairs={{0,64},{64,0},{1,65},{65,1},{2,66},{66,2},{3,67},{67,3},{4,68},{68... | collective-permute-start | bytes 860168 | tf_op jit(solution)/shard_map/ppermute | solution.py:21
  32.9 11.5 %collective-permute-start.9 = (bf16[256,1024]{1,0:T(8,128)(2,1)}, bf16[256,1024]{1,0:T(8,128)(2,1)}, u32[]{:S(2)}, u32[]{:S(2)}) collective-permute-start(bf16[256,1024]{1,0:T(8,128)(2,1)} %bitcast_convert_fusion.refs_4_), channel_id=1, source_target_pairs={{0,2},{2,0},{1,3},{3,1},{4,6},{6,4},{5,7},{7,5},{8,10},{10,8},{9,1... | collective-permute-start | bytes 1572872 | tf_op jit(solution)/shard_map/ppermute | solution.py:21
  36.3 38.3 %all-to-all-start = ((bf16[16,2,128,256]{3,2,1,0:T(8,128)(2,1)}), bf16[16,2,128,256]{3,2,1,0:T(8,128)(2,1)}, u32[]{:S(2)}, u32[]{:S(2)}) async-start(bf16[16,2,128,256]{3,2,1,0:T(8,128)(2,1)} %broadcast_in_dim.27), calls=%async_computation | async-start | bytes 4194304 | tf_op jit(solution)/shard_map/all_to_all | solution.py:274
  43.5 215.7 %reduce-scatter.2.cloned.1.call-start = ((), (), s32[]{:S(2)}) async-start(), calls=%async_computation.4 | async-start | bytes 7520256 | tf_op jit(solution)/shard_map/reduce_scatter | solution.py:302
  43.8 32.4 %copy-start.27 = (bf16[256,1024]{1,0:T(8,128)(2,1)}, bf16[256,1024]{1,0:T(8,128)(2,1)S(1)}, u32[]{:S(2)}) copy-start(bf16[256,1024]{1,0:T(8,128)(2,1)S(1)} %multiply_convert_fusion.1) | copy-start | bytes 1572868
  43.8 12.5 %collective-permute-start.4 = (bf16[256,1024]{1,0:T(8,128)(2,1)S(1)}, bf16[256,1024]{1,0:T(8,128)(2,1)S(1)}, u32[]{:S(2)}, u32[]{:S(2)}) collective-permute-start(bf16[256,1024]{1,0:T(8,128)(2,1)S(1)} %multiply_convert_fusion.1), channel_id=1, source_target_pairs={{0,2},{2,0},{1,3},{3,1},{4,6},{6,4},{5,7},{7,5},{8,10},{10,8},{9,1... | collective-permute-start | bytes 1572872 | tf_op jit(solution)/shard_map/ppermute | solution.py:21
  44.4 12.0 %collective-permute-start.8 = (bf16[256,1024]{1,0:T(8,128)(2,1)}, bf16[256,1024]{1,0:T(8,128)(2,1)}, u32[]{:S(2)}, u32[]{:S(2)}) collective-permute-start(bf16[256,1024]{1,0:T(8,128)(2,1)} %bitcast_convert_fusion.refs_4_), channel_id=1, source_target_pairs={{0,1},{1,0},{2,3},{3,2},{4,5},{5,4},{6,7},{7,6},{8,9},{9,8},{10,11... | collective-permute-start | bytes 1572872 | tf_op jit(solution)/shard_map/ppermute | solution.py:21
  44.4 12.0 %collective-permute-start.10 = (bf16[256,1024]{1,0:T(8,128)(2,1)}, bf16[256,1024]{1,0:T(8,128)(2,1)}, u32[]{:S(2)}, u32[]{:S(2)}) collective-permute-start(bf16[256,1024]{1,0:T(8,128)(2,1)} %collective-permute-done.9.refs_6_), channel_id=1, source_target_pairs={{0,1},{1,0},{2,3},{3,2},{4,5},{5,4},{6,7},{7,6},{8,9},{9,8},{10,11... | collective-permute-start | bytes 1572872 | tf_op jit(solution)/shard_map/ppermute | solution.py:21
  44.9 31.3 %collective-permute-start.3 = (bf16[256,1024]{1,0:T(8,128)(2,1)S(1)}, bf16[256,1024]{1,0:T(8,128)(2,1)S(1)}, u32[]{:S(2)}, u32[]{:S(2)}) collective-permute-start(bf16[256,1024]{1,0:T(8,128)(2,1)S(1)} %multiply_convert_fusion.1), channel_id=1, source_target_pairs={{0,1},{1,0},{2,3},{3,2},{4,5},{5,4},{6,7},{7,6},{8,9},{9,8},{10,11... | collective-permute-start | bytes 1572872 | tf_op jit(solution)/shard_map/ppermute | solution.py:21
  56.4 19.9 %copy-start.34 = (bf16[256,1024]{1,0:T(8,128)(2,1)}, bf16[256,1024]{1,0:T(8,128)(2,1)S(1)}, u32[]{:S(2)}) copy-start(bf16[256,1024]{1,0:T(8,128)(2,1)S(1)} %collective-permute-done.4) | copy-start | bytes 1572868
  56.4 19.9 %collective-permute-start.5 = (bf16[256,1024]{1,0:T(8,128)(2,1)S(1)}, bf16[256,1024]{1,0:T(8,128)(2,1)S(1)}, u32[]{:S(2)}, u32[]{:S(2)}) collective-permute-start(bf16[256,1024]{1,0:T(8,128)(2,1)S(1)} %collective-permute-done.4), channel_id=1, source_target_pairs={{0,1},{1,0},{2,3},{3,2},{4,5},{5,4},{6,7},{7,6},{8,9},{9,8},{10,11... | collective-permute-start | bytes 1572872 | tf_op jit(solution)/shard_map/ppermute | solution.py:21
  78.3 9.3 %collective-permute-start.11 = (bf16[4,2,256]{2,1,0:T(2,128)(2,1)S(1)}, bf16[4,2,256]{2,1,0:T(2,128)(2,1)S(1)}, u32[]{:S(2)}, u32[]{:S(2)}) collective-permute-start(bf16[4,2,256]{2,1,0:T(2,128)(2,1)S(1)} %slice.374), channel_id=1, source_target_pairs={{0,4},{4,8},{8,12},{12,16},{16,20},{20,24},{24,28},{28,32},{32,36}... | collective-permute-start | bytes 12296 | tf_op jit(solution)/shard_map/ppermute | solution.py:291
  90.1 2.7 collective-permute-start.12
  93.3 14.0 %collective-permute-start.13 = (bf16[256,1024]{1,0:T(8,128)(2,1)S(1)}, bf16[256,1024]{1,0:T(8,128)(2,1)S(1)}, u32[]{:S(2)}, u32[]{:S(2)}) collective-permute-start(bf16[256,1024]{1,0:T(8,128)(2,1)S(1)} %fusion.20), channel_id=1, source_target_pairs={{0,2},{2,0},{1,3},{3,1},{4,6},{6,4},{5,7},{7,5},{8,10},{10,8},{9,1... | collective-permute-start | bytes 1572872 | tf_op jit(solution)/shard_map/ppermute | solution.py:21
  107.7 69.5 %copy-start.5 = (f32[256,1024]{1,0:T(8,128)}, f32[256,1024]{1,0:T(8,128)S(1)}, u32[]{:S(2)}) copy-start(f32[256,1024]{1,0:T(8,128)S(1)} %get-tuple-element.41) | copy-start | bytes 3145732
  107.9 15.4 %copy-start.33 = (bf16[256,1024]{1,0:T(8,128)(2,1)}, bf16[256,1024]{1,0:T(8,128)(2,1)S(1)}, u32[]{:S(2)}) copy-start(bf16[256,1024]{1,0:T(8,128)(2,1)S(1)} %multiply_convert_fusion.refs_0_) | copy-start | bytes 1572868
  107.9 13.3 %collective-permute-start.15 = (bf16[256,1024]{1,0:T(8,128)(2,1)S(1)}, bf16[256,1024]{1,0:T(8,128)(2,1)S(1)}, u32[]{:S(2)}, u32[]{:S(2)}) collective-permute-start(bf16[256,1024]{1,0:T(8,128)(2,1)S(1)} %multiply_convert_fusion.refs_0_), channel_id=1, source_target_pairs={{0,2},{2,0},{1,3},{3,1},{4,6},{6,4},{5,7},{7,5},{8,10},{10,8},{9,1... | collective-permute-start | bytes 1572872 | tf_op jit(solution)/shard_map/ppermute | solution.py:21
  109.6 11.6 %collective-permute-start.14 = (bf16[256,1024]{1,0:T(8,128)(2,1)S(1)}, bf16[256,1024]{1,0:T(8,128)(2,1)S(1)}, u32[]{:S(2)}, u32[]{:S(2)}) collective-permute-start(bf16[256,1024]{1,0:T(8,128)(2,1)S(1)} %multiply_convert_fusion.refs_0_), channel_id=1, source_target_pairs={{0,1},{1,0},{2,3},{3,2},{4,5},{5,4},{6,7},{7,6},{8,9},{9,8},{10,11... | collective-permute-start | bytes 1572872 | tf_op jit(solution)/shard_map/ppermute | solution.py:21
  121.2 2.0 collective-permute-start.16
  159.6 2.7 collective-permute-start.18
  162.7 14.0 %collective-permute-start.19 = (bf16[256,1024]{1,0:T(8,128)(2,1)S(1)}, bf16[256,1024]{1,0:T(8,128)(2,1)S(1)}, u32[]{:S(2)}, u32[]{:S(2)}) collective-permute-start(bf16[256,1024]{1,0:T(8,128)(2,1)S(1)} %fusion.22), channel_id=1, source_target_pairs={{0,2},{2,0},{1,3},{3,1},{4,6},{6,4},{5,7},{7,5},{8,10},{10,8},{9,1... | collective-permute-start | bytes 1572872 | tf_op jit(solution)/shard_map/ppermute | solution.py:21
  164.3 12.9 %copy-start.17 = (f32[1,256,1024]{2,1,0:T(8,128)S(1)}, f32[1,256,1024]{2,1,0:T(8,128)}, u32[]{:S(2)}) copy-start(f32[1,256,1024]{2,1,0:T(8,128)} %param.19) | copy-start | bytes 3145732
  164.3 29.7 %collective-permute-start.17 = (bf16[2,256,1024]{2,1,0:T(8,128)(2,1)}, bf16[2,256,1024]{2,1,0:T(8,128)(2,1)}, u32[]{:S(2)}, u32[]{:S(2)}) collective-permute-start(bf16[2,256,1024]{2,1,0:T(8,128)(2,1)} %get-tuple-element.23), channel_id=1, source_target_pairs={{0,1},{1,0},{2,3},{3,2},{4,5},{5,4},{6,7},{7,6},{8,9},{9,8},{10,11... | collective-permute-start | bytes 3145736 | tf_op jit(solution)/shard_map/ppermute | solution.py:21
  178.7 13.5 %collective-permute-start.21 = (bf16[256,1024]{1,0:T(8,128)(2,1)}, bf16[256,1024]{1,0:T(8,128)(2,1)S(1)}, u32[]{:S(2)}, u32[]{:S(2)}) collective-permute-start(bf16[256,1024]{1,0:T(8,128)(2,1)} %get-tuple-element.37), channel_id=1, source_target_pairs={{0,2},{2,0},{1,3},{3,1},{4,6},{6,4},{5,7},{7,5},{8,10},{10,8},{9,1... | collective-permute-start | bytes 1572872 | tf_op jit(solution)/shard_map/ppermute | solution.py:21
  181.7 14.6 %collective-permute-start.20 = (bf16[256,1024]{1,0:T(8,128)(2,1)}, bf16[256,1024]{1,0:T(8,128)(2,1)S(1)}, u32[]{:S(2)}, u32[]{:S(2)}) collective-permute-start(bf16[256,1024]{1,0:T(8,128)(2,1)} %get-tuple-element.37), channel_id=1, source_target_pairs={{0,1},{1,0},{2,3},{3,2},{4,5},{5,4},{6,7},{7,6},{8,9},{9,8},{10,11... | collective-permute-start | bytes 1572872 | tf_op jit(solution)/shard_map/ppermute | solution.py:21
  192.2 4.2 %collective-permute-start.22 = (bf16[256,1024]{1,0:T(8,128)(2,1)S(1)}, bf16[256,1024]{1,0:T(8,128)(2,1)S(1)}, u32[]{:S(2)}, u32[]{:S(2)}) collective-permute-start(bf16[256,1024]{1,0:T(8,128)(2,1)S(1)} %collective-permute-done.21), channel_id=1, source_target_pairs={{0,1},{1,0},{2,3},{3,2},{4,5},{5,4},{6,7},{7,6},{8,9},{9,8},{10,11... | collective-permute-start | bytes 1572872 | tf_op jit(solution)/shard_map/ppermute | solution.py:21
  197.8 14.4 %collective-permute-start.23 = (bf16[256,1024]{1,0:T(8,128)(2,1)S(1)}, bf16[256,1024]{1,0:T(8,128)(2,1)S(1)}, u32[]{:S(2)}, u32[]{:S(2)}) collective-permute-start(bf16[256,1024]{1,0:T(8,128)(2,1)S(1)} %fusion.21), channel_id=1, source_target_pairs={{0,2},{2,0},{1,3},{3,1},{4,6},{6,4},{5,7},{7,5},{8,10},{10,8},{9,1... | collective-permute-start | bytes 1572872 | tf_op jit(solution)/shard_map/ppermute | solution.py:21
  200.3 13.4 %copy-start.1 = (f32[4,256,256]{2,1,0:T(8,128)S(1)}, f32[4,256,256]{2,1,0:T(8,128)}, u32[]{:S(2)}) copy-start(f32[4,256,256]{2,1,0:T(8,128)} %get-tuple-element.43.cv_ref) | copy-start | bytes 3145732
  200.3 13.3 %copy-start.2 = (f32[4,256,1]{2,1,0:T(8,128)S(1)}, f32[4,256,1]{2,1,0:T(8,128)}, u32[]{:S(2)}) copy-start(f32[4,256,1]{2,1,0:T(8,128)} %copy.67.two_ref) | copy-start | bytes 12292
  201.3 12.3 %collective-permute-start.24 = (f32[4,3,256]{2,1,0:T(4,128)S(1)}, f32[4,3,256]{2,1,0:T(4,128)S(1)}, u32[]{:S(2)}, u32[]{:S(2)}) collective-permute-start(f32[4,3,256]{2,1,0:T(4,128)S(1)} %pad_maximum_fusion.9), channel_id=1, source_target_pairs={{4,0},{8,4},{12,8},{16,12},{20,16},{24,20},{28,24},{32,28},{36,32}... | collective-permute-start | bytes 36872 | tf_op jit(solution)/shard_map/ppermute | solution.py:319
  219.8 2.7 collective-permute-start.25
  225.1 19.1 %collective-permute-start.26 = (bf16[256,1024]{1,0:T(8,128)(2,1)}, bf16[256,1024]{1,0:T(8,128)(2,1)}, u32[]{:S(2)}, u32[]{:S(2)}) collective-permute-start(bf16[256,1024]{1,0:T(8,128)(2,1)} %fusion.23), channel_id=1, source_target_pairs={{0,2},{2,0},{1,3},{3,1},{4,6},{6,4},{5,7},{7,5},{8,10},{10,8},{9,1... | collective-permute-start | bytes 1572872 | tf_op jit(solution)/shard_map/ppermute | solution.py:21
  225.5 56.2 %all-to-all-start.1 = ((bf16[32,144,256]{2,1,0:T(8,128)(2,1)}), bf16[32,144,256]{2,1,0:T(8,128)(2,1)}, u32[]{:S(2)}, u32[]{:S(2)}) async-start(bf16[32,144,256]{2,1,0:T(8,128)(2,1)} %copy-done), calls=%async_computation.1 | async-start | bytes 4718592 | tf_op jit(solution)/shard_map/all_to_all | solution.py:336
  239.7 30.1 %copy-start.9 = (f32[1,256,1024]{2,1,0:T(8,128)S(1)}, f32[1,256,1024]{2,1,0:T(8,128)}, u32[]{:S(2)}) copy-start(f32[1,256,1024]{2,1,0:T(8,128)} %param.10) | copy-start | bytes 3145732
  260.6 13.2 %collective-permute-start.27 = (bf16[432,256]{1,0:T(8,128)(2,1)S(1)}, bf16[432,256]{1,0:T(8,128)(2,1)S(1)}, u32[]{:S(2)}, u32[]{:S(2)}) collective-permute-start(bf16[432,256]{1,0:T(8,128)(2,1)S(1)} %slice_bitcast_fusion.1), channel_id=1, source_target_pairs={{0,64},{64,0},{1,65},{65,1},{2,66},{66,2},{3,67},{67,3},{4,68},{68... | collective-permute-start | bytes 663560 | tf_op jit(solution)/shard_map/ppermute | solution.py:21
  273.8 7.2 %collective-permute-start.28 = (bf16[144,256]{1,0:T(8,128)(2,1)S(1)}, bf16[144,256]{1,0:T(8,128)(2,1)S(1)}, u32[]{:S(2)}, u32[]{:S(2)}) collective-permute-start(bf16[144,256]{1,0:T(8,128)(2,1)S(1)} %slice.561), channel_id=1, source_target_pairs={{0,0},{32,1},{64,2},{96,3},{4,4},{36,5},{68,6},{100,7},{8,8},{40,9... | collective-permute-start | bytes 221192 | tf_op jit(solution)/shard_map/ppermute | solution.py:305
  276.0 21.5 %copy-start.40 = (f32[32,1152]{1,0:T(8,128)}, f32[32,1152]{1,0:T(8,128)S(1)}, u32[]{:S(2)}) copy-start(f32[32,1152]{1,0:T(8,128)S(1)} %get-tuple-element.51) | copy-start | bytes 442372
  283.7 12.4 %collective-permute-start.29 = (bf16[1,144,256]{2,1,0:T(8,128)(2,1)S(1)}, bf16[1,144,256]{2,1,0:T(8,128)(2,1)S(1)}, u32[]{:S(2)}, u32[]{:S(2)}) collective-permute-start(bf16[1,144,256]{2,1,0:T(8,128)(2,1)S(1)} %convert_bitcast_fusion), channel_id=1, source_target_pairs={{0,1},{1,0},{2,3},{3,2},{4,5},{5,4},{6,7},{7,6},{8,9},{9,8},{10,11... | collective-permute-start | bytes 221192 | tf_op jit(solution)/shard_map/ppermute | solution.py:21
  283.8 12.3 %collective-permute-start.30 = (bf16[1,144,256]{2,1,0:T(8,128)(2,1)S(1)}, bf16[1,144,256]{2,1,0:T(8,128)(2,1)S(1)}, u32[]{:S(2)}, u32[]{:S(2)}) collective-permute-start(bf16[1,144,256]{2,1,0:T(8,128)(2,1)S(1)} %convert_bitcast_fusion), channel_id=1, source_target_pairs={{0,2},{2,0},{1,3},{3,1},{4,6},{6,4},{5,7},{7,5},{8,10},{10,8},{9,1... | collective-permute-start | bytes 221192 | tf_op jit(solution)/shard_map/ppermute | solution.py:21
  288.8 7.3 %collective-permute-start.31 = (bf16[1,144,256]{2,1,0:T(8,128)(2,1)S(1)}, bf16[1,144,256]{2,1,0:T(8,128)(2,1)S(1)}, u32[]{:S(2)}, u32[]{:S(2)}) collective-permute-start(bf16[1,144,256]{2,1,0:T(8,128)(2,1)S(1)} %convert_bitcast_fusion), channel_id=1, source_target_pairs={{0,3},{1,2},{2,1},{3,0},{4,7},{5,6},{6,5},{7,4},{8,11},{9,10},{10,... | collective-permute-start | bytes 221192 | tf_op jit(solution)/shard_map/ppermute | solution.py:31
  288.9 6.6 %collective-permute-start.32 = (bf16[32,256]{1,0:T(8,128)(2,1)S(1)}, bf16[32,256]{1,0:T(8,128)(2,1)S(1)}, u32[]{:S(2)}, u32[]{:S(2)}) collective-permute-start(bf16[32,256]{1,0:T(8,128)(2,1)S(1)} %slice.407), channel_id=1, source_target_pairs={{0,0},{32,1},{64,2},{96,3},{4,4},{36,5},{68,6},{100,7},{8,8},{40,9... | collective-permute-start | bytes 49160 | tf_op jit(solution)/shard_map/ppermute | solution.py:348
  (33 other events, 156.2 us)
Sparse Core Ops, SparseCore 0:
  32.1 82.3 all-gather.1
  158.5 100.7 reduce-scatter.1

commit v3 on v2

--- a/solution.py
+++ b/solution.py
@@ -168,11 +168,13 @@
 
 
 def mix_back_kernel(gm_ref, gmix_ref, mixed_ref, cv_ref, bx_ref, arrived_ref, later_ref, one_ref, two_ref, taps_ref,
-                    h_ref, w_ref, gains_ref, gain_two_ref, back_ref, keep_ref, send_ref, grads, small):
+                    h0_ref, h1_ref, h2_ref, h3_ref, w_ref, gains_ref, gain_two_ref, back_ref, keep_ref, send_ref, h_ref, grads, small):
     rows = lax.broadcasted_iota(jnp.int32, (256, 256), 0)
     taps = taps_ref[...]
     tap_grads = [jnp.zeros((1, 256), F32) for _ in range(3)]
     gain_one = jnp.zeros((1, 1024), F32)
+    for i, block in enumerate((h0_ref, h1_ref, h2_ref, h3_ref)):
+        h_ref[256 * i : 256 * (i + 1), :] = block[...]
     for s in range(4):
         grad_mixer = gm_ref[s]
         b_part, c_part, x_part = (mixed_ref[s, :, 256 * i : 256 * (i + 1)] for i in range(3))
@@ -222,7 +224,7 @@
         in_specs=[vmem] * len(args),
         out_specs=[vmem] * 3,
         out_shape=[jax.ShapeDtypeStruct((32, 144, 256), BF16), jax.ShapeDtypeStruct(half, F32), jax.ShapeDtypeStruct(half, BF16)],
-        scratch_shapes=[pltpu.VMEM((1024, 768), BF16), pltpu.VMEM((16, 256), F32)],
+        scratch_shapes=[pltpu.VMEM((1024, 1024), BF16), pltpu.VMEM((1024, 768), BF16), pltpu.VMEM((16, 256), F32)],
         compiler_params=pltpu.CompilerParams(vmem_limit_bytes=40 * 1024 * 1024),
         cost_estimate=pl.CostEstimate(flops=4 * 10**9, bytes_accessed=10**7, transcendentals=0),
     )(*args)
@@ -307,9 +309,10 @@
     grad_hidden2 = finish_scatter(grad_keep, grad_send)
     grad_norm_two, gain_two = norm_backward(grad_hidden2, normed2, inv_two, gain_rows[1])
     grad_middle = grad_result + grad_norm_two
-    grad_branch_all = jnp.concatenate(group_blocks(grad_middle.astype(BF16)), axis=0)
+    grad_branch_blocks = group_blocks(grad_middle.astype(BF16))
+    grad_branch_all = jnp.concatenate(grad_branch_blocks, axis=0)
     out_got = swap(out_send, "c").astype(F32)
-    out_far, _ = lax.optimization_barrier(((out_keep[1] + out_got[1]).astype(BF16), grad_branch_all))
+    out_far = after((out_keep[1] + out_got[1]).astype(BF16), grad_branch_blocks[1])
     out_far = swap(out_far, "zl")
     result = middle + out_keep[0] + out_got[0] + out_far.astype(F32)
     grad_mix = dot(mixer, grad_branch_all, ((0,), (0,))).astype(BF16)
@@ -328,7 +331,7 @@
         mask_one,
         mask_two,
         conv_taps,
-        hidden1_all,
+        *hidden1_blocks,
         w_in_f,
         gain_rows,
         gain_two[None],

time: 307 us -> 306 us (level)
  starting transfers between devices: 68.5 us -> 60.5 us
    ppermute x26, waiting for transfers between devices: 85.8 us -> 101 us  [swap(): return lax.ppermute(x, axis, [(0, 1), (1, 0)])]
    reduce_scatter x1, waiting for transfers between devices: 13.6 us -> 1.49 us  [local(): lax.psum_scatter(back_pack.reshape(16 * 864, 256), YX, scatter_dimension=...]
    ppermute x26, starting transfers between devices: 33.1 us -> 24.5 us  [swap(): return lax.ppermute(x, axis, [(0, 1), (1, 0)])]
    concatenate x2 -> x0, other arithmetic: 3.1 us -> none  [the longest x1 1.69 us: local(): hidden1_all = jnp.concatenate(hidden1_blocks, axis=0)]
  transfers between devices with their start and end apart: 37 -> 37, of which waited for: 20 -> 20; matrix products, arithmetic and copies ran while one was open for 12% -> 13% of each run, Pallas kernels for 2% -> 2%
where the time goes in v3:
time: 306 us; the launch traced here: 300 us
  waiting for transfers between devices  133 us (43%)
  starting transfers between devices  60.5 us (20%)
  Pallas kernels  41.3 us (13%)
  other arithmetic  30.1 us (10%)
  between operations  15.2 us (5%)
  local copies, waits for them, and re-layouts  14 us (5%)
  matrix products  6.25 us (2%)
    ppermute x26, waiting for transfers between devices, swap(): return lax.ppermute(x, axis, [(0, 1), (1, 0)])  101 us
    pallas_call x1, Pallas kernels, ffn(): pl.pallas_call(functools.partial(ffn_kernel, rows_t), grid=(3,), in_specs...  35.1 us
    ppermute x26, starting transfers between devices, swap(): return lax.ppermute(x, axis, [(0, 1), (1, 0)])  24.5 us
    all_to_all x1, waiting for transfers between devices, local(): first_all = lax.all_to_all(first_copies, YX, 0, 0, tiled=True)  18.1 us
    all_to_all x1, starting transfers between devices, local(): lax.all_to_all(first_back, SEQ, 0, 0, tiled=True).reshape(32, 144, 256)  10.1 us
    ppermute x1, starting transfers between devices, local(): lax.ppermute(product_bx[:, -2:], SEQ, [(i, i + 1) for i in range(31)])  8.01 us
    all_to_all x1, starting transfers between devices, local(): first_all = lax.all_to_all(first_copies, YX, 0, 0, tiled=True)  7.22 us
    dot_general x4, matrix products, dot(): return lax.dot_general(a, b, (dims, ((), ())), preferred_element_type=F32)  6.25 us
  transfers between devices with their start and end apart: 37, of which 20 were waited for; matrix products, arithmetic and copies ran while one was open for 13% of the time, Pallas kernels for 2%

profile of v3, /device:TPU:30, one launch (start us, length us, event | category | flops | bytes accessed | tf_op | source)
XLA Modules:
  0.0 300.3 jit_solution(7352647305347098796)
XLA Ops:
  9.7 2.0 collective-permute-start.1
  12.7 2.9 collective-permute-start.6
  17.6 2.4 collective-permute-done.6
  20.1 4.7 %collective-permute-start.7 = (bf16[560,256]{1,0:T(8,128)(2,1)S(1)}, bf16[560,256]{1,0:T(8,128)(2,1)S(1)}, u32[]{:S(2)}, u32[]{:S(2)}) collective-permute-start(bf16[560,256]{1,0:T(8,128)(2,1)S(1)} %constant_dynamic-update-slice_fusion), channel_id=1, source_target_pairs={{0,64},{64,0},{1,65},{65,1},{2,66},{66,2},{3,67},{67,3},{4,68},{68... | collective-permute-start | bytes 860168 | tf_op jit(solution)/shard_map/ppermute | solution.py:21
  24.7 4.6 %collective-permute-done.7 = bf16[560,256]{1,0:T(8,128)(2,1)S(1)} collective-permute-done((bf16[560,256]{1,0:T(8,128)(2,1)S(1)}, bf16[560,256]{1,0:T(8,128)(2,1)S(1)}, u32[]{:S(2)}, u32[]{:S(2)}) %collective-permute-start.7) | collective-permute-done | bytes 286752 | tf_op jit(solution)/shard_map/ppermute | solution.py:21
  32.9 1.6 collective-permute-start.9
  34.7 1.6 broadcast_in_dim.27
  36.3 7.2 %all-to-all-start = ((bf16[16,2,128,256]{3,2,1,0:T(8,128)(2,1)}), bf16[16,2,128,256]{3,2,1,0:T(8,128)(2,1)}, u32[]{:S(2)}, u32[]{:S(2)}) async-start(bf16[16,2,128,256]{3,2,1,0:T(8,128)(2,1)} %broadcast_in_dim.27), calls=%async_computation | async-start | bytes 4194304 | tf_op jit(solution)/shard_map/all_to_all | solution.py:276
  45.0 11.4 %collective-permute-done.4.h2_ref = bf16[256,1024]{1,0:T(8,128)(2,1)S(1)} collective-permute-done((bf16[256,1024]{1,0:T(8,128)(2,1)S(1)}, bf16[256,1024]{1,0:T(8,128)(2,1)S(1)}, u32[]{:S(2)}, u32[]{:S(2)}) %collective-permute-start.4) | collective-permute-done | bytes 524320 | tf_op jit(solution)/shard_map/ppermute | solution.py:21
  56.4 18.1 %all-to-all-done = bf16[16,2,128,256]{3,2,1,0:T(8,128)(2,1)} async-done(((bf16[16,2,128,256]{3,2,1,0:T(8,128)(2,1)}), bf16[16,2,128,256]{3,2,1,0:T(8,128)(2,1)}, u32[]{:S(2)}, u32[]{:S(2)}) %all-to-all-start) | async-done | bytes 2097184 | tf_op jit(solution)/shard_map/all_to_all | solution.py:276
  76.3 1.8 fusion
  78.3 8.0 %collective-permute-start.11 = (bf16[4,2,256]{2,1,0:T(2,128)(2,1)S(1)}, bf16[4,2,256]{2,1,0:T(2,128)(2,1)S(1)}, u32[]{:S(2)}, u32[]{:S(2)}) collective-permute-start(bf16[4,2,256]{2,1,0:T(2,128)(2,1)S(1)} %slice.374), channel_id=1, source_target_pairs={{0,4},{4,8},{8,12},{12,16},{16,20},{20,24},{24,28},{28,32},{32,36}... | collective-permute-start | bytes 12296 | tf_op jit(solution)/shard_map/ppermute | solution.py:293
  90.4 2.4 collective-permute-done.12
  93.3 1.7 collective-permute-start.13
  95.0 12.3 %collective-permute-done.13 = bf16[256,1024]{1,0:T(8,128)(2,1)S(1)} collective-permute-done((bf16[256,1024]{1,0:T(8,128)(2,1)S(1)}, bf16[256,1024]{1,0:T(8,128)(2,1)S(1)}, u32[]{:S(2)}, u32[]{:S(2)}) %collective-permute-start.13) | collective-permute-done | bytes 524320 | tf_op jit(solution)/shard_map/ppermute | solution.py:21
  107.9 1.7 collective-permute-start.15
  109.6 11.6 %collective-permute-done.15.refs_2_ = bf16[256,1024]{1,0:T(8,128)(2,1)S(1)} collective-permute-done((bf16[256,1024]{1,0:T(8,128)(2,1)S(1)}, bf16[256,1024]{1,0:T(8,128)(2,1)S(1)}, u32[]{:S(2)}, u32[]{:S(2)}) %collective-permute-start.15) | collective-permute-done | bytes 524320 | tf_op jit(solution)/shard_map/ppermute | solution.py:21
  121.2 2.0 collective-permute-done.16.refs_3_
  123.3 35.1 %shard_map.170 = (f32[2,256,1024]{2,1,0:T(8,128)}, bf16[2,256,1024]{2,1,0:T(8,128)(2,1)}, f32[2,256,1024]{2,1,0:T(8,128)}, bf16[2,256,1024]{2,1,0:T(8,128)(2,1)}, bf16[16,2,432,256]{3,2,1,0:T(8,128)(2,1)}) custom-call(bf16[256,1024]{1,0:T(8,128)(2,1)} %copy-done.35, bf16[256,1024]{1,0:T(8,128)(2,1)} %copy-done.43, bf16[256,1024]{1,0:T(8,128)(2,1)} %copy-done.42, ...), custom_call_target="tpu_custom_call" | custom-call | flops 22000001024 | bytes 30000000 | tf_op jit(solution)/shard_map/pallas_call | solution.py:155
  159.7 2.5 collective-permute-done.18
  162.7 1.7 collective-permute-start.19
  164.4 12.3 %collective-permute-done.19 = bf16[256,1024]{1,0:T(8,128)(2,1)S(1)} collective-permute-done((bf16[256,1024]{1,0:T(8,128)(2,1)S(1)}, bf16[256,1024]{1,0:T(8,128)(2,1)S(1)}, u32[]{:S(2)}, u32[]{:S(2)}) %collective-permute-start.19) | collective-permute-done | bytes 524320 | tf_op jit(solution)/shard_map/ppermute | solution.py:21
  178.7 1.6 collective-permute-start.22
  181.6 10.6 %collective-permute-done.22 = bf16[256,1024]{1,0:T(8,128)(2,1)S(1)} collective-permute-done((bf16[256,1024]{1,0:T(8,128)(2,1)}, bf16[256,1024]{1,0:T(8,128)(2,1)S(1)}, u32[]{:S(2)}, u32[]{:S(2)}) %collective-permute-start.22) | collective-permute-done | bytes 524320 | tf_op jit(solution)/shard_map/ppermute | solution.py:21
  193.8 1.7 convert_element_type.192
  196.1 1.7 collective-permute-start.21
  197.8 1.8 fusion.34
  200.5 2.1 collective-permute-start.24
  202.8 1.9 convolution_convert_fusion.gmix_ref
  204.7 5.6 %collective-permute-done.21 = bf16[256,1024]{1,0:T(8,128)(2,1)S(1)} collective-permute-done((bf16[256,1024]{1,0:T(8,128)(2,1)S(1)}, bf16[256,1024]{1,0:T(8,128)(2,1)S(1)}, u32[]{:S(2)}, u32[]{:S(2)}) %collective-permute-start.21) | collective-permute-done | bytes 524320 | tf_op jit(solution)/shard_map/ppermute | solution.py:21
  210.3 2.4 collective-permute-done.24.later_ref
  212.8 6.2 %shard_map.171 = (bf16[32,144,256]{2,1,0:T(8,128)(2,1)S(1)}, f32[2,256,1024]{2,1,0:T(8,128)S(1)}, bf16[2,256,1024]{2,1,0:T(8,128)(2,1)S(1)}) custom-call(f32[4,256,256]{2,1,0:T(8,128)S(1)} %bitcast.181, bf16[256,1024]{1,0:T(8,128)(2,1)S(1)} %convolution_convert_fusion.gmix_ref, f32[4,256,768]{2,1,0:T(8,128)} %bitcast.186, f32[4,256,256]{2,1,0:T(8,128)S(1)} %copy-done.1, ...), custom_call_target="tpu_custom_call" | custom-call | flops 4000000000 | bytes 10000000 | tf_op jit(solution)/shard_map/pallas_call | solution.py:222
  219.1 2.6 collective-permute-done.25
  221.7 1.6 convert_element_type.206
  223.3 2.2 fusion.31
  225.8 3.0 %fusion.18 = f32[1,256,1024]{2,1,0:T(8,128)} fusion(f32[2,256,1024]{2,1,0:T(8,128)} %copy-done.18, f32[256,1024]{1,0:T(8,128)S(1)} %copy-done.14, bf16[256,1024]{1,0:T(8,128)(2,1)} %copy-done.34, f32[2,256,1024]{2,1,0:T(8,128)} %get-tuple-element.22), kind=kLoop, calls=%fused_computation.28 | loop fusion | flops 1048576 | bytes 4718592 | tf_op jit(solution)/shard_map/broadcast_in_dim | solution.py:361
  228.8 10.1 %all-to-all-start.1 = ((bf16[32,144,256]{2,1,0:T(8,128)(2,1)}), bf16[32,144,256]{2,1,0:T(8,128)(2,1)}, u32[]{:S(2)}, u32[]{:S(2)}) async-start(bf16[32,144,256]{2,1,0:T(8,128)(2,1)} %copy-done), calls=%async_computation.1 | async-start | bytes 4718592 | tf_op jit(solution)/shard_map/all_to_all | solution.py:339
  238.9 2.2 collective-permute-done.26
  241.1 1.7 multiply_reduce_fusion
  245.6 3.4 %collective-permute-start.27 = (bf16[432,256]{1,0:T(8,128)(2,1)S(1)}, bf16[432,256]{1,0:T(8,128)(2,1)S(1)}, u32[]{:S(2)}, u32[]{:S(2)}) collective-permute-start(bf16[432,256]{1,0:T(8,128)(2,1)S(1)} %slice_bitcast_fusion.1), channel_id=1, source_target_pairs={{0,64},{64,0},{1,65},{65,1},{2,66},{66,2},{3,67},{67,3},{4,68},{68... | collective-permute-start | bytes 663560 | tf_op jit(solution)/shard_map/ppermute | solution.py:21
  249.1 2.7 add_bitcast_fusion
  251.8 20.5 %collective-permute-done.27 = bf16[432,256]{1,0:T(8,128)(2,1)S(1)} collective-permute-done((bf16[432,256]{1,0:T(8,128)(2,1)S(1)}, bf16[432,256]{1,0:T(8,128)(2,1)S(1)}, u32[]{:S(2)}, u32[]{:S(2)}) %collective-permute-start.27) | collective-permute-done | bytes 221216 | tf_op jit(solution)/shard_map/ppermute | solution.py:21
  272.4 2.8 collective-permute-start.28
  275.3 4.3 %collective-permute-done.28 = bf16[144,256]{1,0:T(8,128)(2,1)S(1)} collective-permute-done((bf16[144,256]{1,0:T(8,128)(2,1)S(1)}, bf16[144,256]{1,0:T(8,128)(2,1)S(1)}, u32[]{:S(2)}, u32[]{:S(2)}) %collective-permute-start.28) | collective-permute-done | bytes 73760 | tf_op jit(solution)/shard_map/ppermute | solution.py:307
  280.3 2.0 convert_reduce_fusion
  282.4 2.5 collective-permute-start.30
  285.0 2.7 collective-permute-start.32
  288.3 3.2 %collective-permute-done.32 = bf16[32,256]{1,0:T(8,128)(2,1)S(1)} collective-permute-done((bf16[32,256]{1,0:T(8,128)(2,1)S(1)}, bf16[32,256]{1,0:T(8,128)(2,1)S(1)}, u32[]{:S(2)}, u32[]{:S(2)}) %collective-permute-start.32) | collective-permute-done | bytes 16416 | tf_op jit(solution)/shard_map/ppermute | solution.py:351
  (221 shorter events, 32.1 us)
Async XLA Ops:
  7.2 116.1 %all-gather.2.cloned.1.call-start = ((), (), s32[]{:S(2)}) async-start(), calls=%async_computation.3 | async-start | bytes 7520256 | tf_op jit(solution)/shard_map/all_gather | solution.py:277
  9.6 7.9 %collective-permute-start = (bf16[1,48,768]{2,1,0:T(8,128)(2,1)S(1)}, bf16[1,48,768]{2,1,0:T(8,128)(2,1)S(1)}, u32[]{:S(2)}, u32[]{:S(2)}) collective-permute-start(bf16[1,48,768]{2,1,0:T(8,128)(2,1)S(1)} %maximum_bitcast_fusion), channel_id=1, source_target_pairs={{0,1},{1,0},{2,3},{3,2},{4,5},{5,4},{6,7},{7,6},{8,9},{9,8},{10,11... | collective-permute-start | bytes 221192 | tf_op jit(solution)/shard_map/ppermute | solution.py:21
  9.7 7.8 %collective-permute-start.1 = (bf16[1,48,768]{2,1,0:T(8,128)(2,1)S(1)}, bf16[1,48,768]{2,1,0:T(8,128)(2,1)S(1)}, u32[]{:S(2)}, u32[]{:S(2)}) collective-permute-start(bf16[1,48,768]{2,1,0:T(8,128)(2,1)S(1)} %maximum_bitcast_fusion), channel_id=1, source_target_pairs={{0,2},{2,0},{1,3},{3,1},{4,6},{6,4},{5,7},{7,5},{8,10},{10,8},{9,1... | collective-permute-start | bytes 221192 | tf_op jit(solution)/shard_map/ppermute | solution.py:21
  11.7 5.8 %collective-permute-start.2 = (bf16[1,48,768]{2,1,0:T(8,128)(2,1)S(1)}, bf16[1,48,768]{2,1,0:T(8,128)(2,1)S(1)}, u32[]{:S(2)}, u32[]{:S(2)}) collective-permute-start(bf16[1,48,768]{2,1,0:T(8,128)(2,1)S(1)} %maximum_bitcast_fusion), channel_id=1, source_target_pairs={{0,3},{1,2},{2,1},{3,0},{4,7},{5,6},{6,5},{7,4},{8,11},{9,10},{10,... | collective-permute-start | bytes 221192 | tf_op jit(solution)/shard_map/ppermute | solution.py:31
  12.7 7.3 %collective-permute-start.6 = (bf16[176,256]{1,0:T(8,128)(2,1)S(1)}, bf16[176,256]{1,0:T(8,128)(2,1)S(1)}, u32[]{:S(2)}, u32[]{:S(2)}) collective-permute-start(bf16[176,256]{1,0:T(8,128)(2,1)S(1)} %pad_maximum_fusion.7), channel_id=1, source_target_pairs={{0,0},{1,32},{2,64},{3,96},{4,4},{5,36},{6,68},{7,100},{8,8},{9,40... | collective-permute-start | bytes 270344 | tf_op jit(solution)/shard_map/ppermute | solution.py:272
  17.4 14.6 %copy-start.19 = (f32[1,256,1024]{2,1,0:T(8,128)S(1)}, f32[1,256,1024]{2,1,0:T(8,128)}, u32[]{:S(2)}) copy-start(f32[1,256,1024]{2,1,0:T(8,128)} %param.19) | copy-start | bytes 3145732
  20.0 14.5 %copy-start.15 = (f32[1,256,1024]{2,1,0:T(8,128)S(1)}, f32[1,256,1024]{2,1,0:T(8,128)}, u32[]{:S(2)}) copy-start(f32[1,256,1024]{2,1,0:T(8,128)} %param.10) | copy-start | bytes 3145732
  20.1 9.3 %collective-permute-start.7 = (bf16[560,256]{1,0:T(8,128)(2,1)S(1)}, bf16[560,256]{1,0:T(8,128)(2,1)S(1)}, u32[]{:S(2)}, u32[]{:S(2)}) collective-permute-start(bf16[560,256]{1,0:T(8,128)(2,1)S(1)} %constant_dynamic-update-slice_fusion), channel_id=1, source_target_pairs={{0,64},{64,0},{1,65},{65,1},{2,66},{66,2},{3,67},{67,3},{4,68},{68... | collective-permute-start | bytes 860168 | tf_op jit(solution)/shard_map/ppermute | solution.py:21
  32.9 11.5 %collective-permute-start.9 = (bf16[256,1024]{1,0:T(8,128)(2,1)}, bf16[256,1024]{1,0:T(8,128)(2,1)}, u32[]{:S(2)}, u32[]{:S(2)}) collective-permute-start(bf16[256,1024]{1,0:T(8,128)(2,1)} %bitcast_convert_fusion.refs_4_), channel_id=1, source_target_pairs={{0,2},{2,0},{1,3},{3,1},{4,6},{6,4},{5,7},{7,5},{8,10},{10,8},{9,1... | collective-permute-start | bytes 1572872 | tf_op jit(solution)/shard_map/ppermute | solution.py:21
  36.3 38.3 %all-to-all-start = ((bf16[16,2,128,256]{3,2,1,0:T(8,128)(2,1)}), bf16[16,2,128,256]{3,2,1,0:T(8,128)(2,1)}, u32[]{:S(2)}, u32[]{:S(2)}) async-start(bf16[16,2,128,256]{3,2,1,0:T(8,128)(2,1)} %broadcast_in_dim.27), calls=%async_computation | async-start | bytes 4194304 | tf_op jit(solution)/shard_map/all_to_all | solution.py:276
  43.5 200.8 %reduce-scatter.2.cloned.1.call-start = ((), (), s32[]{:S(2)}) async-start(), calls=%async_computation.4 | async-start | bytes 7520256 | tf_op jit(solution)/shard_map/reduce_scatter | solution.py:304
  43.8 32.4 %copy-start.3 = (bf16[256,1024]{1,0:T(8,128)(2,1)}, bf16[256,1024]{1,0:T(8,128)(2,1)S(1)}, u32[]{:S(2)}) copy-start(bf16[256,1024]{1,0:T(8,128)(2,1)S(1)} %multiply_convert_fusion.1.h0_ref) | copy-start | bytes 1572868
  43.8 12.5 %collective-permute-start.4 = (bf16[256,1024]{1,0:T(8,128)(2,1)S(1)}, bf16[256,1024]{1,0:T(8,128)(2,1)S(1)}, u32[]{:S(2)}, u32[]{:S(2)}) collective-permute-start(bf16[256,1024]{1,0:T(8,128)(2,1)S(1)} %multiply_convert_fusion.1.h0_ref), channel_id=1, source_target_pairs={{0,2},{2,0},{1,3},{3,1},{4,6},{6,4},{5,7},{7,5},{8,10},{10,8},{9,1... | collective-permute-start | bytes 1572872 | tf_op jit(solution)/shard_map/ppermute | solution.py:21
  44.4 12.0 %collective-permute-start.8 = (bf16[256,1024]{1,0:T(8,128)(2,1)}, bf16[256,1024]{1,0:T(8,128)(2,1)S(1)}, u32[]{:S(2)}, u32[]{:S(2)}) collective-permute-start(bf16[256,1024]{1,0:T(8,128)(2,1)} %bitcast_convert_fusion.refs_4_), channel_id=1, source_target_pairs={{0,1},{1,0},{2,3},{3,2},{4,5},{5,4},{6,7},{7,6},{8,9},{9,8},{10,11... | collective-permute-start | bytes 1572872 | tf_op jit(solution)/shard_map/ppermute | solution.py:21
  44.4 12.0 %collective-permute-start.10 = (bf16[256,1024]{1,0:T(8,128)(2,1)}, bf16[256,1024]{1,0:T(8,128)(2,1)}, u32[]{:S(2)}, u32[]{:S(2)}) collective-permute-start(bf16[256,1024]{1,0:T(8,128)(2,1)} %collective-permute-done.9.refs_6_), channel_id=1, source_target_pairs={{0,1},{1,0},{2,3},{3,2},{4,5},{5,4},{6,7},{7,6},{8,9},{9,8},{10,11... | collective-permute-start | bytes 1572872 | tf_op jit(solution)/shard_map/ppermute | solution.py:21
  44.9 31.3 %collective-permute-start.3 = (bf16[256,1024]{1,0:T(8,128)(2,1)S(1)}, bf16[256,1024]{1,0:T(8,128)(2,1)S(1)}, u32[]{:S(2)}, u32[]{:S(2)}) collective-permute-start(bf16[256,1024]{1,0:T(8,128)(2,1)S(1)} %multiply_convert_fusion.1.h0_ref), channel_id=1, source_target_pairs={{0,1},{1,0},{2,3},{3,2},{4,5},{5,4},{6,7},{7,6},{8,9},{9,8},{10,11... | collective-permute-start | bytes 1572872 | tf_op jit(solution)/shard_map/ppermute | solution.py:21
  56.4 19.9 %copy-start.7 = (bf16[256,1024]{1,0:T(8,128)(2,1)}, bf16[256,1024]{1,0:T(8,128)(2,1)S(1)}, u32[]{:S(2)}) copy-start(bf16[256,1024]{1,0:T(8,128)(2,1)S(1)} %collective-permute-done.4.h2_ref) | copy-start | bytes 1572868
  56.4 19.9 %collective-permute-start.5 = (bf16[256,1024]{1,0:T(8,128)(2,1)S(1)}, bf16[256,1024]{1,0:T(8,128)(2,1)S(1)}, u32[]{:S(2)}, u32[]{:S(2)}) collective-permute-start(bf16[256,1024]{1,0:T(8,128)(2,1)S(1)} %collective-permute-done.4.h2_ref), channel_id=1, source_target_pairs={{0,1},{1,0},{2,3},{3,2},{4,5},{5,4},{6,7},{7,6},{8,9},{9,8},{10,11... | collective-permute-start | bytes 1572872 | tf_op jit(solution)/shard_map/ppermute | solution.py:21
  56.4 19.7 %copy-start.41 = (bf16[256,1024]{1,0:T(8,128)(2,1)}, bf16[256,1024]{1,0:T(8,128)(2,1)S(1)}, u32[]{:S(2)}) copy-start(bf16[256,1024]{1,0:T(8,128)(2,1)S(1)} %collective-permute-done.8.refs_5_) | copy-start | bytes 1572868
  78.3 9.3 %collective-permute-start.11 = (bf16[4,2,256]{2,1,0:T(2,128)(2,1)S(1)}, bf16[4,2,256]{2,1,0:T(2,128)(2,1)S(1)}, u32[]{:S(2)}, u32[]{:S(2)}) collective-permute-start(bf16[4,2,256]{2,1,0:T(2,128)(2,1)S(1)} %slice.374), channel_id=1, source_target_pairs={{0,4},{4,8},{8,12},{12,16},{16,20},{20,24},{24,28},{28,32},{32,36}... | collective-permute-start | bytes 12296 | tf_op jit(solution)/shard_map/ppermute | solution.py:293
  90.1 2.7 collective-permute-start.12
  93.1 14.3 %copy-start.16 = (f32[1,256,1024]{2,1,0:T(8,128)S(1)}, f32[1,256,1024]{2,1,0:T(8,128)}, u32[]{:S(2)}) copy-start(f32[1,256,1024]{2,1,0:T(8,128)} %param.10) | copy-start | bytes 3145732
  93.3 14.0 %collective-permute-start.13 = (bf16[256,1024]{1,0:T(8,128)(2,1)S(1)}, bf16[256,1024]{1,0:T(8,128)(2,1)S(1)}, u32[]{:S(2)}, u32[]{:S(2)}) collective-permute-start(bf16[256,1024]{1,0:T(8,128)(2,1)S(1)} %fusion.28), channel_id=1, source_target_pairs={{0,2},{2,0},{1,3},{3,1},{4,6},{6,4},{5,7},{7,5},{8,10},{10,8},{9,1... | collective-permute-start | bytes 1572872 | tf_op jit(solution)/shard_map/ppermute | solution.py:21
  107.7 69.5 %copy-start.13 = (f32[256,1024]{1,0:T(8,128)}, f32[256,1024]{1,0:T(8,128)S(1)}, u32[]{:S(2)}) copy-start(f32[256,1024]{1,0:T(8,128)S(1)} %get-tuple-element.41) | copy-start | bytes 3145732
  107.9 15.4 %copy-start.35 = (bf16[256,1024]{1,0:T(8,128)(2,1)}, bf16[256,1024]{1,0:T(8,128)(2,1)S(1)}, u32[]{:S(2)}) copy-start(bf16[256,1024]{1,0:T(8,128)(2,1)S(1)} %multiply_convert_fusion.refs_0_) | copy-start | bytes 1572868
  107.9 13.3 %collective-permute-start.15 = (bf16[256,1024]{1,0:T(8,128)(2,1)S(1)}, bf16[256,1024]{1,0:T(8,128)(2,1)S(1)}, u32[]{:S(2)}, u32[]{:S(2)}) collective-permute-start(bf16[256,1024]{1,0:T(8,128)(2,1)S(1)} %multiply_convert_fusion.refs_0_), channel_id=1, source_target_pairs={{0,2},{2,0},{1,3},{3,1},{4,6},{6,4},{5,7},{7,5},{8,10},{10,8},{9,1... | collective-permute-start | bytes 1572872 | tf_op jit(solution)/shard_map/ppermute | solution.py:21
  109.6 11.6 %collective-permute-start.14 = (bf16[256,1024]{1,0:T(8,128)(2,1)S(1)}, bf16[256,1024]{1,0:T(8,128)(2,1)S(1)}, u32[]{:S(2)}, u32[]{:S(2)}) collective-permute-start(bf16[256,1024]{1,0:T(8,128)(2,1)S(1)} %multiply_convert_fusion.refs_0_), channel_id=1, source_target_pairs={{0,1},{1,0},{2,3},{3,2},{4,5},{5,4},{6,7},{7,6},{8,9},{9,8},{10,11... | collective-permute-start | bytes 1572872 | tf_op jit(solution)/shard_map/ppermute | solution.py:21
  121.2 2.0 collective-permute-start.16
  159.6 2.7 collective-permute-start.18
  162.7 14.0 %collective-permute-start.19 = (bf16[256,1024]{1,0:T(8,128)(2,1)S(1)}, bf16[256,1024]{1,0:T(8,128)(2,1)S(1)}, u32[]{:S(2)}, u32[]{:S(2)}) collective-permute-start(bf16[256,1024]{1,0:T(8,128)(2,1)S(1)} %fusion.30), channel_id=1, source_target_pairs={{0,2},{2,0},{1,3},{3,1},{4,6},{6,4},{5,7},{7,5},{8,10},{10,8},{9,1... | collective-permute-start | bytes 1572872 | tf_op jit(solution)/shard_map/ppermute | solution.py:21
  164.4 12.9 %copy-start.20 = (f32[1,256,1024]{2,1,0:T(8,128)S(1)}, f32[1,256,1024]{2,1,0:T(8,128)}, u32[]{:S(2)}) copy-start(f32[1,256,1024]{2,1,0:T(8,128)} %param.19) | copy-start | bytes 3145732
  164.4 29.4 %collective-permute-start.17 = (bf16[2,256,1024]{2,1,0:T(8,128)(2,1)}, bf16[2,256,1024]{2,1,0:T(8,128)(2,1)}, u32[]{:S(2)}, u32[]{:S(2)}) collective-permute-start(bf16[2,256,1024]{2,1,0:T(8,128)(2,1)} %get-tuple-element.23), channel_id=1, source_target_pairs={{0,1},{1,0},{2,3},{3,2},{4,5},{5,4},{6,7},{7,6},{8,9},{9,8},{10,11... | collective-permute-start | bytes 3145736 | tf_op jit(solution)/shard_map/ppermute | solution.py:21
  178.7 13.5 %collective-permute-start.22 = (bf16[256,1024]{1,0:T(8,128)(2,1)}, bf16[256,1024]{1,0:T(8,128)(2,1)S(1)}, u32[]{:S(2)}, u32[]{:S(2)}) collective-permute-start(bf16[256,1024]{1,0:T(8,128)(2,1)} %get-tuple-element.37), channel_id=1, source_target_pairs={{0,2},{2,0},{1,3},{3,1},{4,6},{6,4},{5,7},{7,5},{8,10},{10,8},{9,1... | collective-permute-start | bytes 1572872 | tf_op jit(solution)/shard_map/ppermute | solution.py:21
  181.6 14.5 %collective-permute-start.20 = (bf16[256,1024]{1,0:T(8,128)(2,1)}, bf16[256,1024]{1,0:T(8,128)(2,1)S(1)}, u32[]{:S(2)}, u32[]{:S(2)}) collective-permute-start(bf16[256,1024]{1,0:T(8,128)(2,1)} %get-tuple-element.37), channel_id=1, source_target_pairs={{0,1},{1,0},{2,3},{3,2},{4,5},{5,4},{6,7},{7,6},{8,9},{9,8},{10,11... | collective-permute-start | bytes 1572872 | tf_op jit(solution)/shard_map/ppermute | solution.py:21
  192.2 5.6 %collective-permute-start.23 = (bf16[256,1024]{1,0:T(8,128)(2,1)S(1)}, bf16[256,1024]{1,0:T(8,128)(2,1)S(1)}, u32[]{:S(2)}, u32[]{:S(2)}) collective-permute-start(bf16[256,1024]{1,0:T(8,128)(2,1)S(1)} %collective-permute-done.22), channel_id=1, source_target_pairs={{0,1},{1,0},{2,3},{3,2},{4,5},{5,4},{6,7},{7,6},{8,9},{9,8},{10,11... | collective-permute-start | bytes 1572872 | tf_op jit(solution)/shard_map/ppermute | solution.py:21
  196.1 14.3 %collective-permute-start.21 = (bf16[256,1024]{1,0:T(8,128)(2,1)S(1)}, bf16[256,1024]{1,0:T(8,128)(2,1)S(1)}, u32[]{:S(2)}, u32[]{:S(2)}) collective-permute-start(bf16[256,1024]{1,0:T(8,128)(2,1)S(1)} %fusion.29), channel_id=1, source_target_pairs={{0,2},{2,0},{1,3},{3,1},{4,6},{6,4},{5,7},{7,5},{8,10},{10,8},{9,1... | collective-permute-start | bytes 1572872 | tf_op jit(solution)/shard_map/ppermute | solution.py:21
  200.5 12.2 %collective-permute-start.24 = (f32[4,3,256]{2,1,0:T(4,128)S(1)}, f32[4,3,256]{2,1,0:T(4,128)S(1)}, u32[]{:S(2)}, u32[]{:S(2)}) collective-permute-start(f32[4,3,256]{2,1,0:T(4,128)S(1)} %pad_maximum_fusion.10), channel_id=1, source_target_pairs={{4,0},{8,4},{12,8},{16,12},{20,16},{24,20},{28,24},{32,28},{36,32}... | collective-permute-start | bytes 36872 | tf_op jit(solution)/shard_map/ppermute | solution.py:322
  219.0 2.7 collective-permute-start.25
  225.5 15.6 %collective-permute-start.26 = (bf16[256,1024]{1,0:T(8,128)(2,1)}, bf16[256,1024]{1,0:T(8,128)(2,1)}, u32[]{:S(2)}, u32[]{:S(2)}) collective-permute-start(bf16[256,1024]{1,0:T(8,128)(2,1)} %fusion.31), channel_id=1, source_target_pairs={{0,2},{2,0},{1,3},{3,1},{4,6},{6,4},{5,7},{7,5},{8,10},{10,8},{9,1... | collective-permute-start | bytes 1572872 | tf_op jit(solution)/shard_map/ppermute | solution.py:21
  228.8 12.3 %copy-start.17 = (f32[1,256,1024]{2,1,0:T(8,128)S(1)}, f32[1,256,1024]{2,1,0:T(8,128)}, u32[]{:S(2)}) copy-start(f32[1,256,1024]{2,1,0:T(8,128)} %param.10) | copy-start | bytes 3145732
  228.8 51.5 %all-to-all-start.1 = ((bf16[32,144,256]{2,1,0:T(8,128)(2,1)}), bf16[32,144,256]{2,1,0:T(8,128)(2,1)}, u32[]{:S(2)}, u32[]{:S(2)}) async-start(bf16[32,144,256]{2,1,0:T(8,128)(2,1)} %copy-done), calls=%async_computation.1 | async-start | bytes 4718592 | tf_op jit(solution)/shard_map/all_to_all | solution.py:339
  245.6 26.7 %collective-permute-start.27 = (bf16[432,256]{1,0:T(8,128)(2,1)S(1)}, bf16[432,256]{1,0:T(8,128)(2,1)S(1)}, u32[]{:S(2)}, u32[]{:S(2)}) collective-permute-start(bf16[432,256]{1,0:T(8,128)(2,1)S(1)} %slice_bitcast_fusion.1), channel_id=1, source_target_pairs={{0,64},{64,0},{1,65},{65,1},{2,66},{66,2},{3,67},{67,3},{4,68},{68... | collective-permute-start | bytes 663560 | tf_op jit(solution)/shard_map/ppermute | solution.py:21
  272.4 7.2 %collective-permute-start.28 = (bf16[144,256]{1,0:T(8,128)(2,1)S(1)}, bf16[144,256]{1,0:T(8,128)(2,1)S(1)}, u32[]{:S(2)}, u32[]{:S(2)}) collective-permute-start(bf16[144,256]{1,0:T(8,128)(2,1)S(1)} %slice.561), channel_id=1, source_target_pairs={{0,0},{32,1},{64,2},{96,3},{4,4},{36,5},{68,6},{100,7},{8,8},{40,9... | collective-permute-start | bytes 221192 | tf_op jit(solution)/shard_map/ppermute | solution.py:307
  275.3 18.2 %copy-start.39 = (f32[32,1152]{1,0:T(8,128)}, f32[32,1152]{1,0:T(8,128)S(1)}, u32[]{:S(2)}) copy-start(f32[32,1152]{1,0:T(8,128)S(1)} %get-tuple-element.51) | copy-start | bytes 442372
  282.3 9.8 %collective-permute-start.29 = (bf16[1,144,256]{2,1,0:T(8,128)(2,1)S(1)}, bf16[1,144,256]{2,1,0:T(8,128)(2,1)S(1)}, u32[]{:S(2)}, u32[]{:S(2)}) collective-permute-start(bf16[1,144,256]{2,1,0:T(8,128)(2,1)S(1)} %convert_bitcast_fusion), channel_id=1, source_target_pairs={{0,1},{1,0},{2,3},{3,2},{4,5},{5,4},{6,7},{7,6},{8,9},{9,8},{10,11... | collective-permute-start | bytes 221192 | tf_op jit(solution)/shard_map/ppermute | solution.py:21
  282.4 9.8 %collective-permute-start.30 = (bf16[1,144,256]{2,1,0:T(8,128)(2,1)S(1)}, bf16[1,144,256]{2,1,0:T(8,128)(2,1)S(1)}, u32[]{:S(2)}, u32[]{:S(2)}) collective-permute-start(bf16[1,144,256]{2,1,0:T(8,128)(2,1)S(1)} %convert_bitcast_fusion), channel_id=1, source_target_pairs={{0,2},{2,0},{1,3},{3,1},{4,6},{6,4},{5,7},{7,5},{8,10},{10,8},{9,1... | collective-permute-start | bytes 221192 | tf_op jit(solution)/shard_map/ppermute | solution.py:21
  284.9 7.3 %collective-permute-start.31 = (bf16[1,144,256]{2,1,0:T(8,128)(2,1)S(1)}, bf16[1,144,256]{2,1,0:T(8,128)(2,1)S(1)}, u32[]{:S(2)}, u32[]{:S(2)}) collective-permute-start(bf16[1,144,256]{2,1,0:T(8,128)(2,1)S(1)} %convert_bitcast_fusion), channel_id=1, source_target_pairs={{0,3},{1,2},{2,1},{3,0},{4,7},{5,6},{6,5},{7,4},{8,11},{9,10},{10,... | collective-permute-start | bytes 221192 | tf_op jit(solution)/shard_map/ppermute | solution.py:31
  285.0 6.6 %collective-permute-start.32 = (bf16[32,256]{1,0:T(8,128)(2,1)S(1)}, bf16[32,256]{1,0:T(8,128)(2,1)S(1)}, u32[]{:S(2)}, u32[]{:S(2)}) collective-permute-start(bf16[32,256]{1,0:T(8,128)(2,1)S(1)} %slice.407), channel_id=1, source_target_pairs={{0,0},{32,1},{64,2},{96,3},{4,4},{36,5},{68,6},{100,7},{8,8},{40,9... | collective-permute-start | bytes 49160 | tf_op jit(solution)/shard_map/ppermute | solution.py:351
  (33 other events, 150.0 us)
Sparse Core Ops, SparseCore 0:
  32.1 82.3 all-gather.1
  158.5 85.8 reduce-scatter.1

commit v4 on v3

--- a/solution.py
+++ b/solution.py
@@ -41,9 +41,9 @@
 
 
 def finish_scatter(keep, send):
-    got = swap(send, "c").astype(F32)
-    far = swap((keep[1] + got[1]).astype(BF16), "zl")
-    return keep[0] + got[0] + far.astype(F32)
+    got = swap(send, "c")
+    far = swap((keep[1] + got[1].astype(F32)).astype(BF16), "zl")
+    return keep[0] + got[0].astype(F32) + far.astype(F32)
 
 
 def norm_forward(values, norm_gain):
@@ -311,10 +311,9 @@
     grad_middle = grad_result + grad_norm_two
     grad_branch_blocks = group_blocks(grad_middle.astype(BF16))
     grad_branch_all = jnp.concatenate(grad_branch_blocks, axis=0)
-    out_got = swap(out_send, "c").astype(F32)
-    out_far = after((out_keep[1] + out_got[1]).astype(BF16), grad_branch_blocks[1])
+    out_got = swap(out_send, "c")
+    out_far = after((out_keep[1] + out_got[1].astype(F32)).astype(BF16), grad_branch_blocks[1])
     out_far = swap(out_far, "zl")
-    result = middle + out_keep[0] + out_got[0] + out_far.astype(F32)
     grad_mix = dot(mixer, grad_branch_all, ((0,), (0,))).astype(BF16)
     grad_mixer = dot(grad_branch_all, w_mix_f, ((1,), (1,))).reshape(4, rows, 256)
     edge = grad_mixer[:, :2] * c_part[:, :2]
@@ -339,6 +338,7 @@
     first_got = lax.all_to_all(first_back, SEQ, 0, 0, tiled=True).reshape(32, 144, 256)
     first_got, _ = lax.optimization_barrier((first_got, grad_down))
     first_sums = jnp.sum(first_got.astype(F32), axis=0)
+    result = middle + out_keep[0] + out_got[0].astype(F32) + after(out_far, first_sums).astype(F32)
     conv_total = first_sums[136:139]
     group_sums = gather_group(first_sums[None].astype(BF16))
     in_own = []

time: 306 us -> 308 us (level)
  starting transfers between devices: 60.5 us -> 66.8 us
    ppermute x26, waiting for transfers between devices: 101 us -> 89.2 us  [swap(): return lax.ppermute(x, axis, [(0, 1), (1, 0)])]
    reduce_scatter x1, waiting for transfers between devices: 1.49 us -> 12 us  [local(): lax.psum_scatter(back_pack.reshape(16 * 864, 256), YX, scatter_dimension=...]
    ppermute x26, starting transfers between devices: 24.5 us -> 31.7 us  [swap(): return lax.ppermute(x, axis, [(0, 1), (1, 0)])]
    convert_element_type x8 -> x4, other arithmetic: 6.46 us -> 4.76 us  [the longest x3 3.54 us: finish_scatter(): far = swap((keep[1] + got[1].astype(F32)).astype(BF16), 'zl')]
  transfers between devices with their start and end apart: 37 -> 37, of which waited for: 20 -> 20; matrix products, arithmetic and copies ran while one was open for 13% -> 12% of each run, Pallas kernels for 2% -> 2%
where the time goes in v4:
time: 308 us; the launch traced here: 304 us
  waiting for transfers between devices  131 us (43%)
  starting transfers between devices  66.8 us (22%)
  Pallas kernels  41.2 us (13%)
  other arithmetic  27.7 us (9%)
  between operations  15.2 us (5%)
  local copies, waits for them, and re-layouts  15.1 us (5%)
  matrix products  6.57 us (2%)
    ppermute x26, waiting for transfers between devices, swap(): return lax.ppermute(x, axis, [(0, 1), (1, 0)])  89.2 us
    pallas_call x1, Pallas kernels, ffn(): pl.pallas_call(functools.partial(ffn_kernel, rows_t), grid=(3,), in_specs...  35 us
    ppermute x26, starting transfers between devices, swap(): return lax.ppermute(x, axis, [(0, 1), (1, 0)])  31.7 us
    all_to_all x1, waiting for transfers between devices, local(): first_all = lax.all_to_all(first_copies, YX, 0, 0, tiled=True)  18.2 us
    reduce_scatter x1, waiting for transfers between devices, local(): lax.psum_scatter(back_pack.reshape(16 * 864, 256), YX, scatter_dimension=...  12 us
    all_to_all x1, starting transfers between devices, local(): lax.all_to_all(first_back, SEQ, 0, 0, tiled=True).reshape(32, 144, 256)  10.5 us
    ppermute x1, starting transfers between devices, local(): lax.ppermute(product_bx[:, -2:], SEQ, [(i, i + 1) for i in range(31)])  7.99 us
    all_to_all x1, starting transfers between devices, local(): first_all = lax.all_to_all(first_copies, YX, 0, 0, tiled=True)  7.22 us
  transfers between devices with their start and end apart: 37, of which 20 were waited for; matrix products, arithmetic and copies ran while one was open for 12% of the time, Pallas kernels for 2%

profile of v4, /device:TPU:30, one launch (start us, length us, event | category | flops | bytes accessed | tf_op | source)
XLA Modules:
  0.0 304.1 jit_solution(10386992829791098034)
XLA Ops:
  9.7 2.0 collective-permute-start.1
  12.7 2.9 collective-permute-start.6
  17.6 2.4 collective-permute-done.6
  20.1 4.7 %collective-permute-start.7 = (bf16[560,256]{1,0:T(8,128)(2,1)S(1)}, bf16[560,256]{1,0:T(8,128)(2,1)S(1)}, u32[]{:S(2)}, u32[]{:S(2)}) collective-permute-start(bf16[560,256]{1,0:T(8,128)(2,1)S(1)} %constant_dynamic-update-slice_fusion), channel_id=1, source_target_pairs={{0,64},{64,0},{1,65},{65,1},{2,66},{66,2},{3,67},{67,3},{4,68},{68... | collective-permute-start | bytes 860168 | tf_op jit(solution)/shard_map/ppermute | solution.py:21
  24.7 4.6 %collective-permute-done.7 = bf16[560,256]{1,0:T(8,128)(2,1)S(1)} collective-permute-done((bf16[560,256]{1,0:T(8,128)(2,1)S(1)}, bf16[560,256]{1,0:T(8,128)(2,1)S(1)}, u32[]{:S(2)}, u32[]{:S(2)}) %collective-permute-start.7) | collective-permute-done | bytes 286752 | tf_op jit(solution)/shard_map/ppermute | solution.py:21
  33.0 1.6 collective-permute-start.9
  34.8 1.6 broadcast_in_dim.27
  36.4 7.2 %all-to-all-start = ((bf16[16,2,128,256]{3,2,1,0:T(8,128)(2,1)}), bf16[16,2,128,256]{3,2,1,0:T(8,128)(2,1)}, u32[]{:S(2)}, u32[]{:S(2)}) async-start(bf16[16,2,128,256]{3,2,1,0:T(8,128)(2,1)} %broadcast_in_dim.27), calls=%async_computation | async-start | bytes 4194304 | tf_op jit(solution)/shard_map/all_to_all | solution.py:276
  45.1 11.4 %collective-permute-done.4.h2_ref = bf16[256,1024]{1,0:T(8,128)(2,1)S(1)} collective-permute-done((bf16[256,1024]{1,0:T(8,128)(2,1)S(1)}, bf16[256,1024]{1,0:T(8,128)(2,1)S(1)}, u32[]{:S(2)}, u32[]{:S(2)}) %collective-permute-start.4) | collective-permute-done | bytes 524320 | tf_op jit(solution)/shard_map/ppermute | solution.py:21
  56.5 18.2 %all-to-all-done = bf16[16,2,128,256]{3,2,1,0:T(8,128)(2,1)} async-done(((bf16[16,2,128,256]{3,2,1,0:T(8,128)(2,1)}), bf16[16,2,128,256]{3,2,1,0:T(8,128)(2,1)}, u32[]{:S(2)}, u32[]{:S(2)}) %all-to-all-start) | async-done | bytes 2097184 | tf_op jit(solution)/shard_map/all_to_all | solution.py:276
  76.4 1.8 fusion
  78.4 8.0 %collective-permute-start.11 = (bf16[4,2,256]{2,1,0:T(2,128)(2,1)S(1)}, bf16[4,2,256]{2,1,0:T(2,128)(2,1)S(1)}, u32[]{:S(2)}, u32[]{:S(2)}) collective-permute-start(bf16[4,2,256]{2,1,0:T(2,128)(2,1)S(1)} %slice.374), channel_id=1, source_target_pairs={{0,4},{4,8},{8,12},{12,16},{16,20},{20,24},{24,28},{28,32},{32,36}... | collective-permute-start | bytes 12296 | tf_op jit(solution)/shard_map/ppermute | solution.py:293
  90.5 2.4 collective-permute-done.12
  93.1 1.7 collective-permute-start.13
  94.8 12.3 %collective-permute-done.13 = bf16[256,1024]{1,0:T(8,128)(2,1)S(1)} collective-permute-done((bf16[256,1024]{1,0:T(8,128)(2,1)S(1)}, bf16[256,1024]{1,0:T(8,128)(2,1)S(1)}, u32[]{:S(2)}, u32[]{:S(2)}) %collective-permute-start.13) | collective-permute-done | bytes 524320 | tf_op jit(solution)/shard_map/ppermute | solution.py:21
  107.7 1.7 collective-permute-start.15
  109.4 11.6 %collective-permute-done.15.refs_2_ = bf16[256,1024]{1,0:T(8,128)(2,1)S(1)} collective-permute-done((bf16[256,1024]{1,0:T(8,128)(2,1)S(1)}, bf16[256,1024]{1,0:T(8,128)(2,1)S(1)}, u32[]{:S(2)}, u32[]{:S(2)}) %collective-permute-start.15) | collective-permute-done | bytes 524320 | tf_op jit(solution)/shard_map/ppermute | solution.py:21
  121.0 2.0 collective-permute-done.16.refs_3_
  123.0 35.0 %shard_map.170 = (f32[2,256,1024]{2,1,0:T(8,128)}, bf16[2,256,1024]{2,1,0:T(8,128)(2,1)}, f32[2,256,1024]{2,1,0:T(8,128)}, bf16[2,256,1024]{2,1,0:T(8,128)(2,1)}, bf16[16,2,432,256]{3,2,1,0:T(8,128)(2,1)}) custom-call(bf16[256,1024]{1,0:T(8,128)(2,1)} %copy-done.34, bf16[256,1024]{1,0:T(8,128)(2,1)} %copy-done.44, bf16[256,1024]{1,0:T(8,128)(2,1)} %copy-done.43, ...), custom_call_target="tpu_custom_call" | custom-call | flops 22000001024 | bytes 30000000 | tf_op jit(solution)/shard_map/pallas_call | solution.py:155
  159.4 2.5 collective-permute-done.18
  163.4 1.7 collective-permute-start.19
  165.1 12.3 %collective-permute-done.19 = bf16[256,1024]{1,0:T(8,128)(2,1)S(1)} collective-permute-done((bf16[256,1024]{1,0:T(8,128)(2,1)S(1)}, bf16[256,1024]{1,0:T(8,128)(2,1)S(1)}, u32[]{:S(2)}, u32[]{:S(2)}) %collective-permute-start.19) | collective-permute-done | bytes 524320 | tf_op jit(solution)/shard_map/ppermute | solution.py:21
  177.9 1.6 fusion.32
  179.5 1.6 collective-permute-start.22
  182.4 10.6 %collective-permute-done.22 = bf16[256,1024]{1,0:T(8,128)(2,1)} collective-permute-done((bf16[256,1024]{1,0:T(8,128)(2,1)}, bf16[256,1024]{1,0:T(8,128)(2,1)}, u32[]{:S(2)}, u32[]{:S(2)}) %collective-permute-start.22) | collective-permute-done | bytes 524320 | tf_op jit(solution)/shard_map/ppermute | solution.py:21
  193.2 1.6 pad_maximum_fusion.1.w_ref
  196.1 1.7 collective-permute-start.21
  197.8 2.0 fusion.26
  200.7 2.1 collective-permute-start.24
  202.9 2.1 convolution_convert_fusion.gmix_ref
  205.0 5.4 %collective-permute-done.21 = bf16[256,1024]{1,0:T(8,128)(2,1)S(1)} collective-permute-done((bf16[256,1024]{1,0:T(8,128)(2,1)S(1)}, bf16[256,1024]{1,0:T(8,128)(2,1)S(1)}, u32[]{:S(2)}, u32[]{:S(2)}) %collective-permute-start.21) | collective-permute-done | bytes 524320 | tf_op jit(solution)/shard_map/ppermute | solution.py:21
  210.4 2.7 collective-permute-done.24.later_ref
  213.2 6.2 %shard_map.171 = (bf16[32,144,256]{2,1,0:T(8,128)(2,1)S(1)}, f32[2,256,1024]{2,1,0:T(8,128)S(1)}, bf16[2,256,1024]{2,1,0:T(8,128)(2,1)S(1)}) custom-call(f32[4,256,256]{2,1,0:T(8,128)S(1)} %bitcast.180, bf16[256,1024]{1,0:T(8,128)(2,1)S(1)} %convolution_convert_fusion.gmix_ref, f32[4,256,768]{2,1,0:T(8,128)} %bitcast.185, f32[4,256,256]{2,1,0:T(8,128)S(1)} %copy-done.1, ...), custom_call_target="tpu_custom_call" | custom-call | flops 4000000000 | bytes 10000000 | tf_op jit(solution)/shard_map/pallas_call | solution.py:222
  220.9 2.8 collective-permute-done.27
  223.7 2.0 fusion.22
  225.7 10.5 %all-to-all-start.1 = ((bf16[32,144,256]{2,1,0:T(8,128)(2,1)}), bf16[32,144,256]{2,1,0:T(8,128)(2,1)}, u32[]{:S(2)}, u32[]{:S(2)}) async-start(bf16[32,144,256]{2,1,0:T(8,128)(2,1)} %copy-done), calls=%async_computation.1 | async-start | bytes 4718592 | tf_op jit(solution)/shard_map/all_to_all | solution.py:338
  236.2 9.7 %collective-permute-done.28 = bf16[256,1024]{1,0:T(8,128)(2,1)} collective-permute-done((bf16[256,1024]{1,0:T(8,128)(2,1)}, bf16[256,1024]{1,0:T(8,128)(2,1)}, u32[]{:S(2)}, u32[]{:S(2)}) %collective-permute-start.28) | collective-permute-done | bytes 524320 | tf_op jit(solution)/shard_map/ppermute | solution.py:21
  246.0 1.6 multiply_reduce_fusion
  247.5 12.0 %reduce-scatter.2.cloned.1.call-done = bf16[864,256]{1,0:T(8,128)(2,1)} async-done(((bf16[13824,256]{1,0:T(8,128)(2,1)}), bf16[864,256]{1,0:T(8,128)(2,1)}) %reduce-scatter.2.cloned.1.call-update) | async-done | bytes 442384 | tf_op jit(solution)/shard_map/reduce_scatter | solution.py:304
  260.8 8.4 %collective-permute-start.25 = (bf16[432,256]{1,0:T(8,128)(2,1)S(1)}, bf16[432,256]{1,0:T(8,128)(2,1)S(1)}, u32[]{:S(2)}, u32[]{:S(2)}) collective-permute-start(bf16[432,256]{1,0:T(8,128)(2,1)S(1)} %slice_bitcast_fusion.1), channel_id=1, source_target_pairs={{0,64},{64,0},{1,65},{65,1},{2,66},{66,2},{3,67},{67,3},{4,68},{68... | collective-permute-start | bytes 663560 | tf_op jit(solution)/shard_map/ppermute | solution.py:21
  269.2 2.6 add_bitcast_fusion
  273.3 2.2 collective-permute-start.26
  275.6 5.1 %collective-permute-done.26 = bf16[144,256]{1,0:T(8,128)(2,1)S(1)} collective-permute-done((bf16[144,256]{1,0:T(8,128)(2,1)S(1)}, bf16[144,256]{1,0:T(8,128)(2,1)S(1)}, u32[]{:S(2)}, u32[]{:S(2)}) %collective-permute-start.26) | collective-permute-done | bytes 73760 | tf_op jit(solution)/shard_map/ppermute | solution.py:307
  281.4 2.1 convert_reduce_fusion
  283.6 5.0 %collective-permute-start.30 = (bf16[1,144,256]{2,1,0:T(8,128)(2,1)S(1)}, bf16[1,144,256]{2,1,0:T(8,128)(2,1)S(1)}, u32[]{:S(2)}, u32[]{:S(2)}) collective-permute-start(bf16[1,144,256]{2,1,0:T(8,128)(2,1)S(1)} %convert_bitcast_fusion), channel_id=1, source_target_pairs={{0,2},{2,0},{1,3},{3,1},{4,6},{6,4},{5,7},{7,5},{8,10},{10,8},{9,1... | collective-permute-start | bytes 221192 | tf_op jit(solution)/shard_map/ppermute | solution.py:21
  288.7 1.9 collective-permute-start.32
  290.6 2.3 fusion.17
  293.6 1.7 collective-permute-done.32
  (219 shorter events, 31.6 us)
Async XLA Ops:
  7.2 115.9 %all-gather.2.cloned.1.call-start = ((), (), s32[]{:S(2)}) async-start(), calls=%async_computation.3 | async-start | bytes 7520256 | tf_op jit(solution)/shard_map/all_gather | solution.py:277
  9.6 7.9 %collective-permute-start = (bf16[1,48,768]{2,1,0:T(8,128)(2,1)S(1)}, bf16[1,48,768]{2,1,0:T(8,128)(2,1)S(1)}, u32[]{:S(2)}, u32[]{:S(2)}) collective-permute-start(bf16[1,48,768]{2,1,0:T(8,128)(2,1)S(1)} %maximum_bitcast_fusion), channel_id=1, source_target_pairs={{0,1},{1,0},{2,3},{3,2},{4,5},{5,4},{6,7},{7,6},{8,9},{9,8},{10,11... | collective-permute-start | bytes 221192 | tf_op jit(solution)/shard_map/ppermute | solution.py:21
  9.7 7.8 %collective-permute-start.1 = (bf16[1,48,768]{2,1,0:T(8,128)(2,1)S(1)}, bf16[1,48,768]{2,1,0:T(8,128)(2,1)S(1)}, u32[]{:S(2)}, u32[]{:S(2)}) collective-permute-start(bf16[1,48,768]{2,1,0:T(8,128)(2,1)S(1)} %maximum_bitcast_fusion), channel_id=1, source_target_pairs={{0,2},{2,0},{1,3},{3,1},{4,6},{6,4},{5,7},{7,5},{8,10},{10,8},{9,1... | collective-permute-start | bytes 221192 | tf_op jit(solution)/shard_map/ppermute | solution.py:21
  11.7 5.8 %collective-permute-start.2 = (bf16[1,48,768]{2,1,0:T(8,128)(2,1)S(1)}, bf16[1,48,768]{2,1,0:T(8,128)(2,1)S(1)}, u32[]{:S(2)}, u32[]{:S(2)}) collective-permute-start(bf16[1,48,768]{2,1,0:T(8,128)(2,1)S(1)} %maximum_bitcast_fusion), channel_id=1, source_target_pairs={{0,3},{1,2},{2,1},{3,0},{4,7},{5,6},{6,5},{7,4},{8,11},{9,10},{10,... | collective-permute-start | bytes 221192 | tf_op jit(solution)/shard_map/ppermute | solution.py:31
  12.7 7.3 %collective-permute-start.6 = (bf16[176,256]{1,0:T(8,128)(2,1)S(1)}, bf16[176,256]{1,0:T(8,128)(2,1)S(1)}, u32[]{:S(2)}, u32[]{:S(2)}) collective-permute-start(bf16[176,256]{1,0:T(8,128)(2,1)S(1)} %pad_maximum_fusion.7), channel_id=1, source_target_pairs={{0,0},{1,32},{2,64},{3,96},{4,4},{5,36},{6,68},{7,100},{8,8},{9,40... | collective-permute-start | bytes 270344 | tf_op jit(solution)/shard_map/ppermute | solution.py:272
  20.1 9.3 %collective-permute-start.7 = (bf16[560,256]{1,0:T(8,128)(2,1)S(1)}, bf16[560,256]{1,0:T(8,128)(2,1)S(1)}, u32[]{:S(2)}, u32[]{:S(2)}) collective-permute-start(bf16[560,256]{1,0:T(8,128)(2,1)S(1)} %constant_dynamic-update-slice_fusion), channel_id=1, source_target_pairs={{0,64},{64,0},{1,65},{65,1},{2,66},{66,2},{3,67},{67,3},{4,68},{68... | collective-permute-start | bytes 860168 | tf_op jit(solution)/shard_map/ppermute | solution.py:21
  33.0 11.5 %collective-permute-start.9 = (bf16[256,1024]{1,0:T(8,128)(2,1)}, bf16[256,1024]{1,0:T(8,128)(2,1)}, u32[]{:S(2)}, u32[]{:S(2)}) collective-permute-start(bf16[256,1024]{1,0:T(8,128)(2,1)} %bitcast_convert_fusion.refs_4_), channel_id=1, source_target_pairs={{0,2},{2,0},{1,3},{3,1},{4,6},{6,4},{5,7},{7,5},{8,10},{10,8},{9,1... | collective-permute-start | bytes 1572872 | tf_op jit(solution)/shard_map/ppermute | solution.py:21
  36.4 38.3 %all-to-all-start = ((bf16[16,2,128,256]{3,2,1,0:T(8,128)(2,1)}), bf16[16,2,128,256]{3,2,1,0:T(8,128)(2,1)}, u32[]{:S(2)}, u32[]{:S(2)}) async-start(bf16[16,2,128,256]{3,2,1,0:T(8,128)(2,1)} %broadcast_in_dim.27), calls=%async_computation | async-start | bytes 4194304 | tf_op jit(solution)/shard_map/all_to_all | solution.py:276
  43.6 215.9 %reduce-scatter.2.cloned.1.call-start = ((), (), s32[]{:S(2)}) async-start(), calls=%async_computation.4 | async-start | bytes 7520256 | tf_op jit(solution)/shard_map/reduce_scatter | solution.py:304
  43.9 32.5 %copy-start.3 = (bf16[256,1024]{1,0:T(8,128)(2,1)}, bf16[256,1024]{1,0:T(8,128)(2,1)S(1)}, u32[]{:S(2)}) copy-start(bf16[256,1024]{1,0:T(8,128)(2,1)S(1)} %multiply_convert_fusion.1.h0_ref) | copy-start | bytes 1572868
  43.9 12.5 %collective-permute-start.4 = (bf16[256,1024]{1,0:T(8,128)(2,1)S(1)}, bf16[256,1024]{1,0:T(8,128)(2,1)S(1)}, u32[]{:S(2)}, u32[]{:S(2)}) collective-permute-start(bf16[256,1024]{1,0:T(8,128)(2,1)S(1)} %multiply_convert_fusion.1.h0_ref), channel_id=1, source_target_pairs={{0,2},{2,0},{1,3},{3,1},{4,6},{6,4},{5,7},{7,5},{8,10},{10,8},{9,1... | collective-permute-start | bytes 1572872 | tf_op jit(solution)/shard_map/ppermute | solution.py:21
  44.5 12.0 %collective-permute-start.8 = (bf16[256,1024]{1,0:T(8,128)(2,1)}, bf16[256,1024]{1,0:T(8,128)(2,1)S(1)}, u32[]{:S(2)}, u32[]{:S(2)}) collective-permute-start(bf16[256,1024]{1,0:T(8,128)(2,1)} %bitcast_convert_fusion.refs_4_), channel_id=1, source_target_pairs={{0,1},{1,0},{2,3},{3,2},{4,5},{5,4},{6,7},{7,6},{8,9},{9,8},{10,11... | collective-permute-start | bytes 1572872 | tf_op jit(solution)/shard_map/ppermute | solution.py:21
  44.5 12.0 %collective-permute-start.10 = (bf16[256,1024]{1,0:T(8,128)(2,1)}, bf16[256,1024]{1,0:T(8,128)(2,1)}, u32[]{:S(2)}, u32[]{:S(2)}) collective-permute-start(bf16[256,1024]{1,0:T(8,128)(2,1)} %collective-permute-done.9.refs_6_), channel_id=1, source_target_pairs={{0,1},{1,0},{2,3},{3,2},{4,5},{5,4},{6,7},{7,6},{8,9},{9,8},{10,11... | collective-permute-start | bytes 1572872 | tf_op jit(solution)/shard_map/ppermute | solution.py:21
  45.0 31.4 %collective-permute-start.3 = (bf16[256,1024]{1,0:T(8,128)(2,1)S(1)}, bf16[256,1024]{1,0:T(8,128)(2,1)S(1)}, u32[]{:S(2)}, u32[]{:S(2)}) collective-permute-start(bf16[256,1024]{1,0:T(8,128)(2,1)S(1)} %multiply_convert_fusion.1.h0_ref), channel_id=1, source_target_pairs={{0,1},{1,0},{2,3},{3,2},{4,5},{5,4},{6,7},{7,6},{8,9},{9,8},{10,11... | collective-permute-start | bytes 1572872 | tf_op jit(solution)/shard_map/ppermute | solution.py:21
  56.4 19.9 %copy-start.7 = (bf16[256,1024]{1,0:T(8,128)(2,1)}, bf16[256,1024]{1,0:T(8,128)(2,1)S(1)}, u32[]{:S(2)}) copy-start(bf16[256,1024]{1,0:T(8,128)(2,1)S(1)} %collective-permute-done.4.h2_ref) | copy-start | bytes 1572868
  56.4 19.9 %collective-permute-start.5 = (bf16[256,1024]{1,0:T(8,128)(2,1)S(1)}, bf16[256,1024]{1,0:T(8,128)(2,1)S(1)}, u32[]{:S(2)}, u32[]{:S(2)}) collective-permute-start(bf16[256,1024]{1,0:T(8,128)(2,1)S(1)} %collective-permute-done.4.h2_ref), channel_id=1, source_target_pairs={{0,1},{1,0},{2,3},{3,2},{4,5},{5,4},{6,7},{7,6},{8,9},{9,8},{10,11... | collective-permute-start | bytes 1572872 | tf_op jit(solution)/shard_map/ppermute | solution.py:21
  56.5 19.7 %copy-start.42 = (bf16[256,1024]{1,0:T(8,128)(2,1)}, bf16[256,1024]{1,0:T(8,128)(2,1)S(1)}, u32[]{:S(2)}) copy-start(bf16[256,1024]{1,0:T(8,128)(2,1)S(1)} %collective-permute-done.8.refs_5_) | copy-start | bytes 1572868
  78.4 9.3 %collective-permute-start.11 = (bf16[4,2,256]{2,1,0:T(2,128)(2,1)S(1)}, bf16[4,2,256]{2,1,0:T(2,128)(2,1)S(1)}, u32[]{:S(2)}, u32[]{:S(2)}) collective-permute-start(bf16[4,2,256]{2,1,0:T(2,128)(2,1)S(1)} %slice.374), channel_id=1, source_target_pairs={{0,4},{4,8},{8,12},{12,16},{16,20},{20,24},{24,28},{28,32},{32,36}... | collective-permute-start | bytes 12296 | tf_op jit(solution)/shard_map/ppermute | solution.py:293
  90.2 2.7 collective-permute-start.12
  90.5 16.6 %copy-start.14 = (f32[1,256,1024]{2,1,0:T(8,128)S(1)}, f32[1,256,1024]{2,1,0:T(8,128)}, u32[]{:S(2)}) copy-start(f32[1,256,1024]{2,1,0:T(8,128)} %param.10) | copy-start | bytes 3145732
  93.1 14.0 %collective-permute-start.13 = (bf16[256,1024]{1,0:T(8,128)(2,1)S(1)}, bf16[256,1024]{1,0:T(8,128)(2,1)S(1)}, u32[]{:S(2)}, u32[]{:S(2)}) collective-permute-start(bf16[256,1024]{1,0:T(8,128)(2,1)S(1)} %fusion.23), channel_id=1, source_target_pairs={{0,2},{2,0},{1,3},{3,1},{4,6},{6,4},{5,7},{7,5},{8,10},{10,8},{9,1... | collective-permute-start | bytes 1572872 | tf_op jit(solution)/shard_map/ppermute | solution.py:21
  107.5 70.4 %copy-start.16 = (f32[256,1024]{1,0:T(8,128)}, f32[256,1024]{1,0:T(8,128)S(1)}, u32[]{:S(2)}) copy-start(f32[256,1024]{1,0:T(8,128)S(1)} %get-tuple-element.42) | copy-start | bytes 3145732
  107.7 13.3 %collective-permute-start.15 = (bf16[256,1024]{1,0:T(8,128)(2,1)S(1)}, bf16[256,1024]{1,0:T(8,128)(2,1)S(1)}, u32[]{:S(2)}, u32[]{:S(2)}) collective-permute-start(bf16[256,1024]{1,0:T(8,128)(2,1)S(1)} %multiply_convert_fusion.refs_0_), channel_id=1, source_target_pairs={{0,2},{2,0},{1,3},{3,1},{4,6},{6,4},{5,7},{7,5},{8,10},{10,8},{9,1... | collective-permute-start | bytes 1572872 | tf_op jit(solution)/shard_map/ppermute | solution.py:21
  109.4 11.6 %collective-permute-start.14 = (bf16[256,1024]{1,0:T(8,128)(2,1)S(1)}, bf16[256,1024]{1,0:T(8,128)(2,1)S(1)}, u32[]{:S(2)}, u32[]{:S(2)}) collective-permute-start(bf16[256,1024]{1,0:T(8,128)(2,1)S(1)} %multiply_convert_fusion.refs_0_), channel_id=1, source_target_pairs={{0,1},{1,0},{2,3},{3,2},{4,5},{5,4},{6,7},{7,6},{8,9},{9,8},{10,11... | collective-permute-start | bytes 1572872 | tf_op jit(solution)/shard_map/ppermute | solution.py:21
  121.0 2.0 collective-permute-start.16
  158.1 19.3 %copy-start.18 = (f32[2,256,1024]{2,1,0:T(8,128)S(1)}, f32[2,256,1024]{2,1,0:T(8,128)}, u32[]{:S(2)}) copy-start(f32[2,256,1024]{2,1,0:T(8,128)} %get-tuple-element.25) | copy-start | bytes 6291460
  159.3 2.7 collective-permute-start.18
  163.4 14.0 %collective-permute-start.19 = (bf16[256,1024]{1,0:T(8,128)(2,1)S(1)}, bf16[256,1024]{1,0:T(8,128)(2,1)S(1)}, u32[]{:S(2)}, u32[]{:S(2)}) collective-permute-start(bf16[256,1024]{1,0:T(8,128)(2,1)S(1)} %fusion.21), channel_id=1, source_target_pairs={{0,2},{2,0},{1,3},{3,1},{4,6},{6,4},{5,7},{7,5},{8,10},{10,8},{9,1... | collective-permute-start | bytes 1572872 | tf_op jit(solution)/shard_map/ppermute | solution.py:21
  165.1 29.7 %collective-permute-start.17 = (bf16[2,256,1024]{2,1,0:T(8,128)(2,1)}, bf16[2,256,1024]{2,1,0:T(8,128)(2,1)}, u32[]{:S(2)}, u32[]{:S(2)}) collective-permute-start(bf16[2,256,1024]{2,1,0:T(8,128)(2,1)} %get-tuple-element.24), channel_id=1, source_target_pairs={{0,1},{1,0},{2,3},{3,2},{4,5},{5,4},{6,7},{7,6},{8,9},{9,8},{10,11... | collective-permute-start | bytes 3145736 | tf_op jit(solution)/shard_map/ppermute | solution.py:21
  179.5 13.6 %collective-permute-start.22 = (bf16[256,1024]{1,0:T(8,128)(2,1)}, bf16[256,1024]{1,0:T(8,128)(2,1)}, u32[]{:S(2)}, u32[]{:S(2)}) collective-permute-start(bf16[256,1024]{1,0:T(8,128)(2,1)} %get-tuple-element.39), channel_id=1, source_target_pairs={{0,2},{2,0},{1,3},{3,1},{4,6},{6,4},{5,7},{7,5},{8,10},{10,8},{9,1... | collective-permute-start | bytes 1572872 | tf_op jit(solution)/shard_map/ppermute | solution.py:21
  182.4 13.6 %collective-permute-start.20 = (bf16[256,1024]{1,0:T(8,128)(2,1)}, bf16[256,1024]{1,0:T(8,128)(2,1)S(1)}, u32[]{:S(2)}, u32[]{:S(2)}) collective-permute-start(bf16[256,1024]{1,0:T(8,128)(2,1)} %get-tuple-element.39), channel_id=1, source_target_pairs={{0,1},{1,0},{2,3},{3,2},{4,5},{5,4},{6,7},{7,6},{8,9},{9,8},{10,11... | collective-permute-start | bytes 1572872 | tf_op jit(solution)/shard_map/ppermute | solution.py:21
  193.1 4.7 %collective-permute-start.23 = (bf16[256,1024]{1,0:T(8,128)(2,1)}, bf16[256,1024]{1,0:T(8,128)(2,1)S(1)}, u32[]{:S(2)}, u32[]{:S(2)}) collective-permute-start(bf16[256,1024]{1,0:T(8,128)(2,1)} %collective-permute-done.22), channel_id=1, source_target_pairs={{0,1},{1,0},{2,3},{3,2},{4,5},{5,4},{6,7},{7,6},{8,9},{9,8},{10,11... | collective-permute-start | bytes 1572872 | tf_op jit(solution)/shard_map/ppermute | solution.py:21
  196.1 14.3 %collective-permute-start.21 = (bf16[256,1024]{1,0:T(8,128)(2,1)S(1)}, bf16[256,1024]{1,0:T(8,128)(2,1)S(1)}, u32[]{:S(2)}, u32[]{:S(2)}) collective-permute-start(bf16[256,1024]{1,0:T(8,128)(2,1)S(1)} %fusion.20), channel_id=1, source_target_pairs={{0,2},{2,0},{1,3},{3,1},{4,6},{6,4},{5,7},{7,5},{8,10},{10,8},{9,1... | collective-permute-start | bytes 1572872 | tf_op jit(solution)/shard_map/ppermute | solution.py:21
  200.7 12.4 %collective-permute-start.24 = (f32[4,3,256]{2,1,0:T(4,128)S(1)}, f32[4,3,256]{2,1,0:T(4,128)S(1)}, u32[]{:S(2)}, u32[]{:S(2)}) collective-permute-start(f32[4,3,256]{2,1,0:T(4,128)S(1)} %pad_maximum_fusion.10), channel_id=1, source_target_pairs={{4,0},{8,4},{12,8},{16,12},{20,16},{24,20},{28,24},{32,28},{36,32}... | collective-permute-start | bytes 36872 | tf_op jit(solution)/shard_map/ppermute | solution.py:321
  220.9 2.8 collective-permute-start.27
  225.7 20.3 %collective-permute-start.28 = (bf16[256,1024]{1,0:T(8,128)(2,1)}, bf16[256,1024]{1,0:T(8,128)(2,1)}, u32[]{:S(2)}, u32[]{:S(2)}) collective-permute-start(bf16[256,1024]{1,0:T(8,128)(2,1)} %fusion.22), channel_id=1, source_target_pairs={{0,2},{2,0},{1,3},{3,1},{4,6},{6,4},{5,7},{7,5},{8,10},{10,8},{9,1... | collective-permute-start | bytes 1572872 | tf_op jit(solution)/shard_map/ppermute | solution.py:21
  225.7 20.3 %copy-start.15 = (f32[1,256,1024]{2,1,0:T(8,128)S(1)}, f32[1,256,1024]{2,1,0:T(8,128)}, u32[]{:S(2)}) copy-start(f32[1,256,1024]{2,1,0:T(8,128)} %param.10) | copy-start | bytes 3145732
  225.7 55.7 %all-to-all-start.1 = ((bf16[32,144,256]{2,1,0:T(8,128)(2,1)}), bf16[32,144,256]{2,1,0:T(8,128)(2,1)}, u32[]{:S(2)}, u32[]{:S(2)}) async-start(bf16[32,144,256]{2,1,0:T(8,128)(2,1)} %copy-done), calls=%async_computation.1 | async-start | bytes 4718592 | tf_op jit(solution)/shard_map/all_to_all | solution.py:338
  260.8 12.4 %collective-permute-start.25 = (bf16[432,256]{1,0:T(8,128)(2,1)S(1)}, bf16[432,256]{1,0:T(8,128)(2,1)S(1)}, u32[]{:S(2)}, u32[]{:S(2)}) collective-permute-start(bf16[432,256]{1,0:T(8,128)(2,1)S(1)} %slice_bitcast_fusion.1), channel_id=1, source_target_pairs={{0,64},{64,0},{1,65},{65,1},{2,66},{66,2},{3,67},{67,3},{4,68},{68... | collective-permute-start | bytes 663560 | tf_op jit(solution)/shard_map/ppermute | solution.py:21
  273.2 17.4 %copy-start.17 = (f32[256,1024]{1,0:T(8,128)S(1)}, f32[256,1024]{1,0:T(8,128)}, u32[]{:S(2)}) copy-start(f32[256,1024]{1,0:T(8,128)} %copy-done.16) | copy-start | bytes 3145732
  273.2 17.4 %copy-start.26 = (f32[2,256,1024]{2,1,0:T(8,128)S(1)}, f32[2,256,1024]{2,1,0:T(8,128)}, u32[]{:S(2)}) copy-start(f32[2,256,1024]{2,1,0:T(8,128)} %get-tuple-element.23) | copy-start | bytes 6291460
  273.3 7.4 %collective-permute-start.26 = (bf16[144,256]{1,0:T(8,128)(2,1)S(1)}, bf16[144,256]{1,0:T(8,128)(2,1)S(1)}, u32[]{:S(2)}, u32[]{:S(2)}) collective-permute-start(bf16[144,256]{1,0:T(8,128)(2,1)S(1)} %slice.545), channel_id=1, source_target_pairs={{0,0},{32,1},{64,2},{96,3},{4,4},{36,5},{68,6},{100,7},{8,8},{40,9... | collective-permute-start | bytes 221192 | tf_op jit(solution)/shard_map/ppermute | solution.py:307
  275.5 17.4 %copy-start.40 = (f32[32,1152]{1,0:T(8,128)}, f32[32,1152]{1,0:T(8,128)S(1)}, u32[]{:S(2)}) copy-start(f32[32,1152]{1,0:T(8,128)S(1)} %get-tuple-element.52) | copy-start | bytes 442372
  275.6 17.4 %copy-start.39 = (f32[32,1152]{1,0:T(8,128)}, f32[32,1152]{1,0:T(8,128)S(1)}, u32[]{:S(2)}) copy-start(f32[32,1152]{1,0:T(8,128)S(1)} %constant_dynamic-update-slice_fusion.5) | copy-start | bytes 442372
  283.5 12.4 %collective-permute-start.29 = (bf16[1,144,256]{2,1,0:T(8,128)(2,1)S(1)}, bf16[1,144,256]{2,1,0:T(8,128)(2,1)S(1)}, u32[]{:S(2)}, u32[]{:S(2)}) collective-permute-start(bf16[1,144,256]{2,1,0:T(8,128)(2,1)S(1)} %convert_bitcast_fusion), channel_id=1, source_target_pairs={{0,1},{1,0},{2,3},{3,2},{4,5},{5,4},{6,7},{7,6},{8,9},{9,8},{10,11... | collective-permute-start | bytes 221192 | tf_op jit(solution)/shard_map/ppermute | solution.py:21
  283.6 12.3 %collective-permute-start.30 = (bf16[1,144,256]{2,1,0:T(8,128)(2,1)S(1)}, bf16[1,144,256]{2,1,0:T(8,128)(2,1)S(1)}, u32[]{:S(2)}, u32[]{:S(2)}) collective-permute-start(bf16[1,144,256]{2,1,0:T(8,128)(2,1)S(1)} %convert_bitcast_fusion), channel_id=1, source_target_pairs={{0,2},{2,0},{1,3},{3,1},{4,6},{6,4},{5,7},{7,5},{8,10},{10,8},{9,1... | collective-permute-start | bytes 221192 | tf_op jit(solution)/shard_map/ppermute | solution.py:21
  288.6 7.3 %collective-permute-start.31 = (bf16[1,144,256]{2,1,0:T(8,128)(2,1)S(1)}, bf16[1,144,256]{2,1,0:T(8,128)(2,1)S(1)}, u32[]{:S(2)}, u32[]{:S(2)}) collective-permute-start(bf16[1,144,256]{2,1,0:T(8,128)(2,1)S(1)} %convert_bitcast_fusion), channel_id=1, source_target_pairs={{0,3},{1,2},{2,1},{3,0},{4,7},{5,6},{6,5},{7,4},{8,11},{9,10},{10,... | collective-permute-start | bytes 221192 | tf_op jit(solution)/shard_map/ppermute | solution.py:31
  288.7 6.6 %collective-permute-start.32 = (bf16[32,256]{1,0:T(8,128)(2,1)S(1)}, bf16[32,256]{1,0:T(8,128)(2,1)S(1)}, u32[]{:S(2)}, u32[]{:S(2)}) collective-permute-start(bf16[32,256]{1,0:T(8,128)(2,1)S(1)} %slice.407), channel_id=1, source_target_pairs={{0,0},{32,1},{64,2},{96,3},{4,4},{36,5},{68,6},{100,7},{8,8},{40,9... | collective-permute-start | bytes 49160 | tf_op jit(solution)/shard_map/ppermute | solution.py:351
  (34 other events, 213.6 us)
Sparse Core Ops, SparseCore 0:
  32.2 82.3 all-gather.1
  158.2 101.2 reduce-scatter.1
